TPU v7x, 128 devices: a whole 4x4x4 slice. The times are simulated.
128 devices in a mesh: call: 8 (over z, core), utt: 16 (over x, y).
Axes of the slice: x: 4, y: 4, z: 4, core: 2. Of those that a mesh axis runs over, the one named last changes fastest.
Arguments:
- queries: bfloat16 [128, 256, 1280], P(('call', 'utt')), may hold values from -300 to 300
- own_keys: bfloat16 [128, 256, 1280], P(('call', 'utt')), may hold values from -6.5 to 6.5
- own_values: bfloat16 [128, 256, 1280], P(('call', 'utt')), may hold values from -6 to 6
- lengths: int32 [128], P(('call', 'utt')), may hold values from 1 to 4, as said below
- history: int32 [128, 8], P(('call', 'utt')), may hold values from 0 to 31, as said below
- cache_blocks: bfloat16 [256, 2, 64, 1280], P(('call', 'utt')), may hold values from -6 to 6
- out_weight: bfloat16 [1280, 1280], P(('call', 'utt')), may hold values from -0.15625 to 0.15625
- grad_out: bfloat16 [128, 256, 1280], P(('call', 'utt')), may hold values from -6 to 6
Outputs:
- attended: bfloat16 [128, 256, 1280], P(('call', 'utt'))
- grad_queries: bfloat16 [128, 256, 1280], P(('call', 'utt'))
- grad_keys: bfloat16 [128, 256, 1280], P(('call', 'utt'))
- grad_values: bfloat16 [128, 256, 1280], P(('call', 'utt'))
- grad_cache: float32 [256, 2, 64, 1280], P(('call', 'utt'))
- grad_weight: float32 [1280, 1280], P(('call', 'utt'))
Inputs may be any that keep to these rules, and one draw needn't show every extreme that they name: `history`: ids count within the call group: the block with id i is row i % 2 of the device at index i // 2 along utt in that group. An utterance names 8 blocks of 8 different owners; all utterances of one device that name a given owner name the same block of it. `lengths`: every device holds an utterance of 4 blocks.
All inputs are finite; a program needn't handle non-finite values.
Results may differ from a plain program's by a relative error of at most 0.014.
Values may be sent and summed in bfloat16 or wider, within the bound.
No kernel may reach another device: no remote copies, remote signals or barrier semaphores. Data moves between devices by JAX's collectives and lax.ppermute only.
A program may use at most 128 MiB of HBM per device.

v0:
```python
from functools import reduce

import jax
import jax.numpy as jnp
from jax import lax
from jax.sharding import PartitionSpec as P

HD = 64
BLK = 64


def fetch_blocks(wanted_ids, peers, cache_blocks, owned):
    owner_of = wanted_ids // owned
    match = owner_of[None, :] == jnp.arange(peers, dtype=jnp.int32)[:, None]
    request = jnp.max(jnp.where(match, wanted_ids[None, :], -1), axis=1)
    arrived = lax.all_to_all(
        request.reshape(peers, 1), "utt", split_axis=0, concat_axis=0, tiled=True
    ).reshape(peers)
    local_rows = jnp.where(arrived >= 0, arrived % owned, 0)
    sending = jnp.take(cache_blocks, local_rows, axis=0)
    fetched = lax.all_to_all(sending, "utt", split_axis=0, concat_axis=0, tiled=True)
    return (fetched, arrived)


def head_pairs(query_rows, key_all, value_all, grad_attn, key_valid):
    frames, features = query_rows.shape
    key_count = key_all.shape[0]
    pair_width = 2 * HD
    score_scale = HD ** (-0.5)

    def one_pair(group_index):
        offset = group_index * pair_width
        query_part = lax.dynamic_slice_in_dim(query_rows, offset, pair_width, 1).reshape(
            frames, 2, HD
        )
        key_part = lax.dynamic_slice_in_dim(key_all, offset, pair_width, 1).reshape(
            key_count, 2, HD
        )
        value_part = lax.dynamic_slice_in_dim(value_all, offset, pair_width, 1).reshape(
            key_count, 2, HD
        )
        grad_part = lax.dynamic_slice_in_dim(grad_attn, offset, pair_width, 1).reshape(
            frames, 2, HD
        )
        scores = (
            jnp.einsum("qhd,khd->hqk", query_part, key_part, preferred_element_type=jnp.float32)
            * score_scale
        )
        scores = jnp.where(key_valid[None, None, :], scores, -1e30)
        top = jnp.max(scores, axis=-1, keepdims=True)
        expo = jnp.exp(scores - top)
        probs = expo / jnp.sum(expo, axis=-1, keepdims=True)
        probs_b = probs.astype(jnp.bfloat16)
        outputs = jnp.einsum(
            "hqk,khd->qhd", probs_b, value_part, preferred_element_type=jnp.float32
        )
        grad_probs = jnp.einsum(
            "qhd,khd->hqk", grad_part, value_part, preferred_element_type=jnp.float32
        )
        row_dots = jnp.sum(probs * grad_probs, axis=-1, keepdims=True)
        grad_scores = (probs * (grad_probs - row_dots) * score_scale).astype(jnp.bfloat16)
        grad_query = jnp.einsum(
            "hqk,khd->qhd", grad_scores, key_part, preferred_element_type=jnp.float32
        )
        grad_key = jnp.einsum(
            "hqk,qhd->khd", grad_scores, query_part, preferred_element_type=jnp.float32
        )
        grad_value = jnp.einsum(
            "hqk,qhd->khd", probs_b, grad_part, preferred_element_type=jnp.float32
        )
        return (
            outputs.reshape(frames, pair_width),
            grad_query.reshape(frames, pair_width),
            grad_key.reshape(key_count, pair_width),
            grad_value.reshape(key_count, pair_width),
        )

    stacked = lax.map(one_pair, jnp.arange(features // pair_width, dtype=jnp.int32))

    def join(array):
        return jnp.transpose(array, (1, 0, 2)).reshape(array.shape[1], features)

    return [join(array) for array in stacked]


def attend_member(query_rows, key_rows, value_rows, length, blocks, grad_rows, weight_full):
    frames, features = query_rows.shape
    valid = jnp.arange(frames, dtype=jnp.int32) < length * BLK
    key_all = jnp.concatenate([key_rows, blocks[:, 0].reshape(-1, features)], 0)
    value_all = jnp.concatenate([value_rows, blocks[:, 1].reshape(-1, features)], 0)
    key_valid = jnp.concatenate([valid, jnp.ones((key_all.shape[0] - frames,), dtype=bool)], 0)
    grad_attn = (
        jnp.dot(grad_rows, weight_full.T, preferred_element_type=jnp.float32) * valid[:, None]
    ).astype(jnp.bfloat16)
    outputs, grad_query, grad_key_all, grad_value_all = head_pairs(
        query_rows, key_all, value_all, grad_attn, key_valid
    )
    attn = (outputs * valid[:, None]).astype(jnp.bfloat16)
    grad_key_all = grad_key_all.astype(jnp.bfloat16)
    grad_value_all = grad_value_all.astype(jnp.bfloat16)
    history_count = blocks.shape[0]
    block_grads = jnp.stack(
        [
            grad_key_all[frames:].reshape(history_count, BLK, features),
            grad_value_all[frames:].reshape(history_count, BLK, features),
        ],
        1,
    )
    return (
        attn,
        grad_query.astype(jnp.bfloat16),
        grad_key_all[:frames],
        grad_value_all[:frames],
        block_grads,
    )


def body(queries, own_keys, own_values, lengths, history, cache_blocks, out_weight, grad_out):
    peers = lax.axis_size("utt")
    owned = cache_blocks.shape[0]
    members, frames, features = queries.shape
    weight_full = lax.all_gather(out_weight, ("call", "utt"), axis=0, tiled=True)
    owners = history // owned
    fetched, arrived_one = fetch_blocks(history[0], peers, cache_blocks, owned)
    member_blocks = jnp.take(fetched, owners[0], axis=0)
    arrivals = [arrived_one]
    arrived = reduce(jnp.maximum, arrivals)
    results = [
        attend_member(
            queries[0],
            own_keys[0],
            own_values[0],
            lengths[0],
            member_blocks,
            grad_out[0],
            weight_full,
        )
    ]
    attn = jnp.stack([item[0] for item in results])
    grad_queries = jnp.stack([item[1] for item in results])
    grad_keys = jnp.stack([item[2] for item in results])
    grad_values = jnp.stack([item[3] for item in results])
    block_grads = jnp.stack([item[4] for item in results])
    attn_flat = attn.reshape(-1, features)
    grad_flat = grad_out.reshape(-1, features)
    attended = (
        jnp.dot(attn_flat, weight_full, preferred_element_type=jnp.float32)
        .astype(jnp.bfloat16)
        .reshape(members, frames, features)
    )
    grad_weight = lax.psum_scatter(
        lax.dot_general(
            attn_flat, grad_flat, (((0,), (0,)), ((), ())), preferred_element_type=jnp.float32
        ),
        ("call", "utt"),
        scatter_dimension=0,
        tiled=True,
    )
    onehot = (owners.reshape(-1)[None, :] == jnp.arange(peers, dtype=jnp.int32)[:, None]).astype(
        jnp.bfloat16
    )
    slot_grad = jnp.dot(
        onehot,
        block_grads.reshape(members * history.shape[1], -1),
        preferred_element_type=jnp.float32,
    )
    slot_grad = slot_grad.astype(jnp.bfloat16).reshape((peers,) + cache_blocks.shape[1:])
    returned = lax.all_to_all(slot_grad, "utt", split_axis=0, concat_axis=0, tiled=True)
    local_rows = jnp.where(arrived >= 0, arrived % owned, -1)
    fold = (jnp.arange(owned, dtype=jnp.int32)[:, None] == local_rows[None, :]).astype(jnp.bfloat16)
    grad_cache = jnp.dot(
        fold, returned.reshape(peers, -1), preferred_element_type=jnp.float32
    ).reshape(cache_blocks.shape)
    return (attended, grad_queries, grad_keys, grad_values, grad_cache, grad_weight)


def solution(mesh):
    return jax.shard_map(
        body,
        mesh=mesh,
        in_specs=(
            P(("call", "utt"), None, None),
            P(("call", "utt"), None, None),
            P(("call", "utt"), None, None),
            P(("call", "utt")),
            P(("call", "utt"), None),
            P(("call", "utt"), None, None, None),
            P(("call", "utt"), None),
            P(("call", "utt"), None, None),
        ),
        out_specs=(
            P(("call", "utt"), None, None),
            P(("call", "utt"), None, None),
            P(("call", "utt"), None, None),
            P(("call", "utt"), None, None),
            P(("call", "utt"), None, None, None),
            P(("call", "utt"), None),
        ),
        check_vma=False,
    )
```

profile of v0, /device:TPU:32, one launch (start us, length us, event | category | flops | bytes accessed | tf_op | source)
XLA Modules:
  0.0 629.7 jit_solution(3823853481505969869)
XLA Ops:
  8.7 14.4 %all_to_all.25 = s32[16,1,1]{2,1,0:T(1,128)S(1)} all-to-all(s32[16,1,1]{2,1,0:T(1,128)S(1)} %copy.79), channel_id=1, replica_groups=mesh['call'=8,'utt'=16] {'utt'}, dimensions={0} | all-to-all | bytes 128 | tf_op jit(solution)/shard_map/all_to_all | solution.py:16
  23.6 3.2 gather_fusion
  26.8 5.4 broadcast_select_fusion
  32.3 4.7 all-to-all-start.1
  39.5 65.7 %all-to-all-done.1 = bf16[16,2,64,1280]{3,2,1,0:T(8,128)(2,1)} async-done(((bf16[16,2,64,1280]{3,2,1,0:T(8,128)(2,1)}), bf16[16,2,64,1280]{3,2,1,0:T(8,128)(2,1)}, u32[]{:S(2)}, u32[]{:S(2)}) %all-to-all-start.1) | async-done | bytes 5242912 | tf_op jit(solution)/shard_map/all_to_all | solution.py:21
  105.3 3.2 gather_fusion.1
  110.1 2.3 pad_maximum_fusion.1
  112.4 34.6 %all-gather.3.cloned.1.call-done = bf16[128,10,1280]{2,1,0:T(8,128)(2,1)} async-done(((bf16[1,10,1280]{2,1,0:T(8,128)(2,1)}), bf16[128,10,1280]{2,1,0:T(8,128)(2,1)}) %all-gather.3.cloned.1.call-update) | async-done | bytes 3276816 | tf_op jit(solution)/shard_map/all_gather | solution.py:122
  146.9 7.1 %reshape.255 = bf16[1280,1280]{1,0:T(8,128)(2,1)} reshape(bf16[128,10,1280]{2,1,0:T(8,128)(2,1)} %all-gather.3.cloned.1.call-done) | data formatting | bytes 6553600
  154.0 3.9 fusion.28
  158.5 202.0 %while.16 = (s32[]{:T(128)}, f32[10,256,128]{1,2,0:T(8,128)S(1)}, bf16[10,256,128]{1,2,0:T(8,128)(2,1)}, bf16[10,768,128]{1,2,0:T(8,128)(2,1)}, bf16[10,768,128]...) while((s32[]{:T(128)}, f32[10,256,128]{1,2,0:T(8,128)S(1)}, ...), condition=%wide.region_5.6_spmd, body=%wide.region_1.5_spmd.sunk | while | flops 413669120 | bytes 14766599 | solution.py:78
  163.5 1.8 fusion.102
  167.6 4.3 fusion.105
  173.4 4.5 fusion.107
  187.7 4.3 fusion.105
  193.6 4.5 fusion.107
  207.9 4.3 fusion.105
  213.8 4.5 fusion.107
  228.1 4.3 fusion.105
  234.0 4.5 fusion.107
  248.4 4.3 fusion.105
  254.2 4.5 fusion.107
  268.6 4.3 fusion.105
  274.4 4.5 fusion.107
  284.7 1.8 fusion.102
  288.8 4.3 fusion.105
  294.6 4.5 fusion.107
  304.9 1.8 fusion.102
  309.0 4.3 fusion.105
  314.8 4.5 fusion.107
  325.1 1.8 fusion.102
  329.2 4.3 fusion.105
  335.0 4.5 fusion.107
  345.3 1.8 fusion.102
  349.4 4.3 fusion.105
  355.2 4.5 fusion.107
  361.6 2.5 slice.37
  364.1 3.3 copy.86
  369.0 2.5 slice.36
  371.5 3.3 copy.85
  376.4 2.0 pad_maximum_fusion
  380.1 1.9 convolution_convert_fusion
  382.0 3.5 copy.98
  385.5 5.0 all-to-all-start.2
  391.6 3.7 fusion.31
  402.3 3.8 fusion.29
  406.2 208.3 %all-reduce.4.cloned.1.call-done = f32[1280,1280]{1,0:T(8,128)} async-done(((f32[1280,1280]{1,0:T(8,128)}), f32[1280,1280]{1,0:T(8,128)}) %all-reduce.4.cloned.1.call-update) | async-done | bytes 6553616
  616.0 5.7 fusion.26
  (227 shorter events, 120.1 us)
Async XLA Ops:
  7.2 16.4 %copy-start = (bf16[2,2,64,1280]{3,2,1,0:T(8,128)(2,1)S(1)}, bf16[2,2,64,1280]{3,2,1,0:T(8,128)(2,1)}, u32[]{:S(2)}) copy-start(bf16[2,2,64,1280]{3,2,1,0:T(8,128)(2,1)} %param.15) | copy-start | bytes 1966084
  32.2 6.2 copy-start.6
  32.3 73.0 %all-to-all-start.1 = ((bf16[16,2,64,1280]{3,2,1,0:T(8,128)(2,1)}), bf16[16,2,64,1280]{3,2,1,0:T(8,128)(2,1)}, u32[]{:S(2)}, u32[]{:S(2)}) async-start(bf16[16,2,64,1280]{3,2,1,0:T(8,128)(2,1)} %broadcast_select_fusion), calls=%async_computation.1 | async-start | bytes 10485760 | tf_op jit(solution)/shard_map/all_to_all | solution.py:21
  37.0 109.9 %all-gather.3.cloned.1.call-start = ((), (), s32[]{:S(2)}) async-start(), calls=%async_computation.3 | async-start | bytes 5283840 | tf_op jit(solution)/shard_map/all_gather | solution.py:122
  108.8 1.1 copy-start.8
  108.8 1.3 copy-start.9
  112.4 41.6 %copy-start.10 = (bf16[1,256,1280]{2,1,0:T(8,128)(2,1)S(1)}, bf16[1,256,1280]{2,1,0:T(8,128)(2,1)}, u32[]{:S(2)}) copy-start(bf16[1,256,1280]{2,1,0:T(8,128)(2,1)} %param.17) | copy-start | bytes 1966084
  154.0 4.5 copy-start.2
  165.3 7.3 %copy-start.12 = (f32[2,256]{1,0:T(2,128)}, f32[2,256]{1,0:T(2,128)S(1)}, u32[]{:S(2)}) copy-start(f32[2,256]{1,0:T(2,128)S(1)} %get-tuple-element.279) | copy-start | bytes 6148 | tf_op jit(solution)/shard_map/while
  185.5 7.3 %copy-start.12 = (f32[2,256]{1,0:T(2,128)}, f32[2,256]{1,0:T(2,128)S(1)}, u32[]{:S(2)}) copy-start(f32[2,256]{1,0:T(2,128)S(1)} %get-tuple-element.279) | copy-start | bytes 6148 | tf_op jit(solution)/shard_map/while
  205.7 7.3 %copy-start.12 = (f32[2,256]{1,0:T(2,128)}, f32[2,256]{1,0:T(2,128)S(1)}, u32[]{:S(2)}) copy-start(f32[2,256]{1,0:T(2,128)S(1)} %get-tuple-element.279) | copy-start | bytes 6148 | tf_op jit(solution)/shard_map/while
  225.9 7.3 %copy-start.12 = (f32[2,256]{1,0:T(2,128)}, f32[2,256]{1,0:T(2,128)S(1)}, u32[]{:S(2)}) copy-start(f32[2,256]{1,0:T(2,128)S(1)} %get-tuple-element.279) | copy-start | bytes 6148 | tf_op jit(solution)/shard_map/while
  246.1 7.2 %copy-start.12 = (f32[2,256]{1,0:T(2,128)}, f32[2,256]{1,0:T(2,128)S(1)}, u32[]{:S(2)}) copy-start(f32[2,256]{1,0:T(2,128)S(1)} %get-tuple-element.279) | copy-start | bytes 6148 | tf_op jit(solution)/shard_map/while
  266.3 7.2 %copy-start.12 = (f32[2,256]{1,0:T(2,128)}, f32[2,256]{1,0:T(2,128)S(1)}, u32[]{:S(2)}) copy-start(f32[2,256]{1,0:T(2,128)S(1)} %get-tuple-element.279) | copy-start | bytes 6148 | tf_op jit(solution)/shard_map/while
  286.5 7.2 %copy-start.12 = (f32[2,256]{1,0:T(2,128)}, f32[2,256]{1,0:T(2,128)S(1)}, u32[]{:S(2)}) copy-start(f32[2,256]{1,0:T(2,128)S(1)} %get-tuple-element.279) | copy-start | bytes 6148 | tf_op jit(solution)/shard_map/while
  306.7 7.2 %copy-start.12 = (f32[2,256]{1,0:T(2,128)}, f32[2,256]{1,0:T(2,128)S(1)}, u32[]{:S(2)}) copy-start(f32[2,256]{1,0:T(2,128)S(1)} %get-tuple-element.279) | copy-start | bytes 6148 | tf_op jit(solution)/shard_map/while
  326.9 7.3 %copy-start.12 = (f32[2,256]{1,0:T(2,128)}, f32[2,256]{1,0:T(2,128)S(1)}, u32[]{:S(2)}) copy-start(f32[2,256]{1,0:T(2,128)S(1)} %get-tuple-element.279) | copy-start | bytes 6148 | tf_op jit(solution)/shard_map/while
  347.1 7.2 %copy-start.12 = (f32[2,256]{1,0:T(2,128)}, f32[2,256]{1,0:T(2,128)S(1)}, u32[]{:S(2)}) copy-start(f32[2,256]{1,0:T(2,128)S(1)} %get-tuple-element.279) | copy-start | bytes 6148 | tf_op jit(solution)/shard_map/while
  360.6 1.1 copy-start.3
  385.5 5.3 copy-start.4
  385.5 230.6 %all-to-all-start.2 = ((bf16[16,2,64,1280]{3,2,1,0:T(8,128)(2,1)}), bf16[16,2,64,1280]{3,2,1,0:T(8,128)(2,1)}, u32[]{:S(2)}, u32[]{:S(2)}) async-start(bf16[16,2,64,1280]{3,2,1,0:T(8,128)(2,1)} %bitcast.143), calls=%async_computation.2 | async-start | bytes 10485760 | tf_op jit(solution)/shard_map/all_to_all | solution.py:168
  390.5 1.1 copy-start.11
  390.5 224.0 %all-reduce.4.cloned.1.call-start = ((), (), s32[]{:S(2)}) async-start(), calls=%async_computation.4 | async-start | bytes 13107200
  397.6 1.5 copy-start.7
  400.2 2.2 copy-start.5
  616.0 6.8 %copy-start.1 = (bf16[2,2,64,1280]{3,2,1,0:T(8,128)(2,1)S(1)}, bf16[2,2,64,1280]{3,2,1,0:T(8,128)(2,1)}, u32[]{:S(2)}) copy-start(bf16[2,2,64,1280]{3,2,1,0:T(8,128)(2,1)} %param.15) | copy-start | bytes 1966084
Sparse Core Ops, SparseCore 0:
  40.8 106.0 all-gather.2
  396.4 218.0 all-reduce.3
where the time goes:
time: 634 us; the launch traced here: 630 us
  waiting for transfers between devices  309 us (49%)
  matrix products  147 us (23%)
  local copies, waits for them, and re-layouts  115 us (18%)
  between operations  14.9 us (2%)
  blocking collectives  14.4 us (2%)
  other arithmetic  12 us (2%)
  starting transfers between devices  10.1 us (2%)
  loops' own time  7.3 us (1%)
    unnamed x3, waiting for transfers between devices  209 us
    all_to_all x1, waiting for transfers between devices, fetch_blocks(): lax.all_to_all(sending, 'utt', split_axis=0, concat_axis=0, tiled=True)  65.7 us
    dot_general x10, matrix products, one_pair(): jnp.einsum('hqk,qhd->khd', grad_scores, query_part, preferred_element_typ...  45.4 us
    dot_general x10, matrix products, one_pair(): jnp.einsum('hqk,khd->qhd', grad_scores, key_part, preferred_element_type=...  43.2 us
    all_gather x1, waiting for transfers between devices, body(): lax.all_gather(out_weight, ('call', 'utt'), axis=0, tiled=True)  34.6 us
    unnamed x33, local copies, waits for them, and re-layouts  21.8 us
    sub x10, matrix products, one_pair(): expo = jnp.exp(scores - top)  17.9 us
    dynamic_update_slice x30, local copies, waits for them, and re-layouts, head_pairs(): lax.map(one_pair, jnp.arange(features // pair_width, dtype=jnp.int32))  14.5 us
  transfers between devices with their start and end apart: 4, of which 3 were waited for; matrix products, arithmetic and copies ran while one was open for 4% of the time, Pallas kernels for 0%

commit v1 on v0

v1 whole, which is shorter than its diff:
```python
import functools

import jax
import jax.numpy as jnp
from jax import lax
from jax.experimental import pallas as pl
from jax.experimental.pallas import tpu as pltpu
from jax.sharding import Mesh
from jax.sharding import PartitionSpec as P

HD = 64
BLK = 64
LANES = 128
LOG2E = 1.4426950408889634
BF = jnp.bfloat16
F32 = jnp.float32
VMEM_LIMIT = 48 * 1024 * 1024
CHUNKS = ((0, 640, "x", "y"), (640, 640, "y", "x"))


def shift(array, axis, amount):
    n = lax.axis_size(axis)
    return lax.ppermute(array, axis, [(i, (i + amount) % n) for i in range(n)])


def nt(a, b):
    return lax.dot_general(a, b, (((1,), (1,)), ((), ())), preferred_element_type=F32)


def mm(a, b):
    return lax.dot_general(a, b, (((1,), (0,)), ((), ())), preferred_element_type=F32)


def select_kernel(table, *refs):
    held, out = refs[:4], refs[4:]
    for j in range(4):
        for k in range(4):
            row = jnp.maximum(table[j * 4 + k], 0)
            out[j][k] = held[k][row]


def select_rows(table, held):
    _, kinds, rows, width = held[0].shape
    block_in = pl.BlockSpec((2, kinds, rows, LANES), lambda i, t: (0, 0, 0, i))
    block_out = pl.BlockSpec((4, kinds, rows, LANES), lambda i, t: (0, 0, 0, i))
    return pl.pallas_call(
        select_kernel,
        grid_spec=pltpu.PrefetchScalarGridSpec(
            num_scalar_prefetch=1,
            grid=(width // LANES,),
            in_specs=[block_in] * 4,
            out_specs=[block_out] * 4,
        ),
        out_shape=[jax.ShapeDtypeStruct((4, kinds, rows, width), BF)] * 4,
        compiler_params=pltpu.CompilerParams(vmem_limit_bytes=VMEM_LIMIT),
        cost_estimate=pl.CostEstimate(
            flops=0, bytes_accessed=6 * 2 * 2 * kinds * rows * width * 2, transcendentals=0
        ),
        name="select_rows",
    )(table.reshape(-1), *held)


def fold_kernel(table, *refs):
    parts, out = refs[:4], refs[4:]
    for k in range(4):
        for row in range(2):
            total = None
            for j in range(4):
                keep = jnp.where(table[j * 4 + k] == row, 1.0, 0.0).astype(F32)
                term = parts[j][k].astype(F32) * keep
                total = term if total is None else total + term
            out[k][row] = total.astype(BF)


def fold_rows(table, parts):
    _, kinds, rows, width = parts[0].shape
    block_in = pl.BlockSpec((4, kinds, rows, LANES), lambda i, t: (0, 0, 0, i))
    block_out = pl.BlockSpec((2, kinds, rows, LANES), lambda i, t: (0, 0, 0, i))
    return pl.pallas_call(
        fold_kernel,
        grid_spec=pltpu.PrefetchScalarGridSpec(
            num_scalar_prefetch=1,
            grid=(width // LANES,),
            in_specs=[block_in] * 4,
            out_specs=[block_out] * 4,
        ),
        out_shape=[jax.ShapeDtypeStruct((2, kinds, rows, width), BF)] * 4,
        compiler_params=pltpu.CompilerParams(vmem_limit_bytes=VMEM_LIMIT),
        cost_estimate=pl.CostEstimate(
            flops=0, bytes_accessed=6 * 2 * 2 * kinds * rows * width * 2, transcendentals=0
        ),
        name="fold_rows",
    )(table.reshape(-1), *parts)


def total_kernel(*refs):
    out = refs[-1]
    step = pl.program_id(0)
    start = 0
    for chunk, (_, width, _, _) in enumerate(CHUNKS):
        parts = refs[4 * chunk : 4 * chunk + 4]
        count = width // LANES

        @pl.when((step >= start) & (step < start + count))
        def _():
            total = parts[0][...].astype(F32)
            for part in parts[1:]:
                total = total + part[...].astype(F32)
            out[...] = total

        start += count


def total_rows(parts):
    owned, kinds, rows, _ = parts[0][0].shape
    specs, start = [], 0
    for _, width, _, _ in CHUNKS:
        count = width // LANES
        spec = pl.BlockSpec(
            (owned, kinds, rows, LANES),
            lambda i, start=start, count=count: (0, 0, 0, jnp.clip(i - start, 0, count - 1)),
        )
        specs += [spec] * 4
        start += count
    width = start * LANES
    return pl.pallas_call(
        total_kernel,
        grid=(start,),
        in_specs=specs,
        out_specs=pl.BlockSpec((owned, kinds, rows, LANES), lambda i: (0, 0, 0, i)),
        out_shape=jax.ShapeDtypeStruct((owned, kinds, rows, width), F32),
        compiler_params=pltpu.CompilerParams(vmem_limit_bytes=VMEM_LIMIT),
        cost_estimate=pl.CostEstimate(
            flops=0, bytes_accessed=owned * kinds * rows * width * 12, transcendentals=0
        ),
        name="total_rows",
    )(*[part for group in parts for part in group])


def attend_kernel(meta, *refs):
    q_ref, ko_ref, vo_ref, g_ref, s0, s1, s2, s3 = refs[:8]
    slots = (s0, s1, s2, s3)
    attn_ref, attn_t_ref, dq_ref, dk_ref, dv_ref, t0, t1, t2, t3, k_all, v_all = refs[-11:]
    back = (t0, t1, t2, t3)
    frames = q_ref.shape[0]
    entries = (k_all.shape[0] - frames) // BLK
    k_all[:frames] = ko_ref[...]
    v_all[:frames] = vo_ref[...]
    for i in range(entries):
        place = pl.ds(frames + BLK * i, BLK)
        for j in range(4):

            @pl.when(meta[i] == j)
            def _():
                k_all[place] = slots[j][meta[entries + i], 0]
                v_all[place] = slots[j][meta[entries + i], 1]

    keys, values = k_all[...], v_all[...]
    query, grad = q_ref[...], g_ref[...]
    keys_t, values_t = keys.T, values.T
    count = keys.shape[0]
    valid_frames = meta[2 * entries] * BLK
    lane = lax.broadcasted_iota(jnp.int32, query.shape, 1)
    key_row = lax.broadcasted_iota(jnp.int32, (frames, frames), 0)
    outs_t, dqs_t = [], []
    grad_key = grad_value = None
    for h in range(2):
        mine = (lane >= h * HD) & (lane < (h + 1) * HD)
        query_h = jnp.where(mine, query, jnp.zeros_like(query))
        grad_h = jnp.where(mine, grad, jnp.zeros_like(grad))
        scores = nt(keys, query_h)
        scores = jnp.concatenate(
            [jnp.where(key_row < valid_frames, scores[:frames], -1e30), scores[frames:]], 0
        )
        top = jnp.max(scores, axis=0, keepdims=True)
        expo = jnp.exp2((scores - top) * (HD**-0.5 * LOG2E))
        inverse = 1.0 / jnp.sum(expo, axis=0, keepdims=True)
        probs = expo * inverse
        probs_b = probs.astype(BF)
        grad_probs = nt(values, grad_h)
        row_dots = jnp.sum(probs * grad_probs, axis=0, keepdims=True)
        grad_scores = (probs * (grad_probs - row_dots) * HD**-0.5).astype(BF)
        outs_t.append(mm(values_t[h * HD : (h + 1) * HD], probs_b))
        dqs_t.append(mm(keys_t[h * HD : (h + 1) * HD], grad_scores))
        part_key = mm(grad_scores, query_h)
        part_value = mm(probs_b, grad_h)
        grad_key = part_key if grad_key is None else grad_key + part_key
        grad_value = part_value if grad_value is None else grad_value + part_value
    out_t = jnp.concatenate(outs_t, 0)
    column = lax.broadcasted_iota(jnp.int32, out_t.shape, 1)
    out_t = jnp.where(column < valid_frames, out_t, 0.0)
    attn_t_ref[...] = out_t.astype(BF)
    attn_ref[...] = out_t.T.astype(BF)
    dq_ref[...] = jnp.concatenate(dqs_t, 0).T.astype(BF)
    grad_key = grad_key.astype(BF)
    grad_value = grad_value.astype(BF)
    dk_ref[...] = grad_key[:frames]
    dv_ref[...] = grad_value[:frames]
    for ref in back:
        ref[...] = jnp.zeros_like(ref)
    for i in range(entries):
        rows = slice(frames + BLK * i, frames + BLK * (i + 1))
        for j in range(4):

            @pl.when(meta[i] == j)
            def _():
                back[j][meta[entries + i], 0] = grad_key[rows]
                back[j][meta[entries + i], 1] = grad_value[rows]


def attend(meta, query, own_keys, own_values, grad_attn, slots, chunk, previous):
    start, width, _, _ = chunk
    frames, features = query.shape
    entries = (meta.shape[0] - 1) // 2
    first = start // LANES
    wide = pl.BlockSpec((frames, LANES), lambda i, m: (0, first + i))
    tall = pl.BlockSpec((LANES, frames), lambda i, m: (first + i, 0))
    slot = pl.BlockSpec((4, 2, BLK, LANES), lambda i, m: (0, 0, 0, i))
    kept = list(previous or [])
    rows = jax.ShapeDtypeStruct((frames, features), BF)
    keys = frames + entries * BLK
    return pl.pallas_call(
        attend_kernel,
        grid_spec=pltpu.PrefetchScalarGridSpec(
            num_scalar_prefetch=1,
            grid=(width // LANES,),
            in_specs=[wide] * 4 + [slot] * 4 + [pl.BlockSpec(memory_space=pl.ANY)] * len(kept),
            out_specs=[wide, tall, wide, wide, wide] + [slot] * 4,
            scratch_shapes=[pltpu.VMEM((keys, LANES), BF), pltpu.VMEM((keys, LANES), BF)],
        ),
        out_shape=[rows, jax.ShapeDtypeStruct((features, frames), BF), rows, rows, rows]
        + [jax.ShapeDtypeStruct((4, 2, BLK, width), BF)] * 4,
        input_output_aliases={9 + i: i for i in range(len(kept))},
        compiler_params=pltpu.CompilerParams(vmem_limit_bytes=VMEM_LIMIT),
        cost_estimate=pl.CostEstimate(
            flops=12 * frames * keys * width,
            bytes_accessed=(9 * frames + 4 * keys) * width * 2,
            transcendentals=frames * keys * width // HD,
        ),
        name="attend",
    )(meta, query, own_keys, own_values, grad_attn, *slots, *kept)


def place_kernel(where, *refs):
    pieces, out = refs[:8], refs[8]
    for i, piece in enumerate(pieces):
        out[where[i]] = piece[...]


def spread_slabs(rows, ids):
    size, features = rows.shape
    note = jnp.pad(ids.astype(BF), (0, features - ids.shape[0]))[None]
    slab = jnp.concatenate([rows, note, jnp.zeros((15 - size, features), BF)], 0)
    row = jnp.stack([slab] + [shift(slab, "y", k) for k in range(1, 4)])
    return [row] + [shift(row, "x", k) for k in range(1, 4)]


def gather_weight(slabs, size):
    x, y, z, core = (lax.axis_index(axis) for axis in ("x", "y", "z", "core"))
    steps = jnp.arange(4, dtype=jnp.int32)
    features = slabs[0].shape[-1]
    rows = jnp.stack(slabs)[:, :, :size]
    rows = jnp.take(jnp.take(rows, (x - steps) % 4, axis=0), (y - steps) % 4, axis=1)
    rows = rows.reshape(16 * size, features)
    pieces = [rows] + [shift(rows, "z", k) for k in range(1, 4)]
    pieces += [shift(piece, "core", 1) for piece in pieces]
    from_z = (z - steps) % 4
    where = jnp.concatenate([from_z * 2 + core, from_z * 2 + 1 - core])
    wide = 2 * LANES
    weight = pl.pallas_call(
        place_kernel,
        grid_spec=pltpu.PrefetchScalarGridSpec(
            num_scalar_prefetch=1,
            grid=(features // wide,),
            in_specs=[pl.BlockSpec((16 * size, wide), lambda i, w: (0, i))] * 8,
            out_specs=pl.BlockSpec((8, 16 * size, wide), lambda i, w: (0, 0, i)),
        ),
        out_shape=jax.ShapeDtypeStruct((8, 16 * size, features), BF),
        compiler_params=pltpu.CompilerParams(vmem_limit_bytes=VMEM_LIMIT),
        cost_estimate=pl.CostEstimate(
            flops=0, bytes_accessed=2 * 8 * 16 * size * features * 2, transcendentals=0
        ),
        name="place_weight",
    )(where, *pieces)
    return weight.reshape(128 * size, features)


def grad_weight_kernel(core, attn_t_ref, grad_ref, far_ref, near_ref):
    step = pl.program_id(0)
    part = mm(attn_t_ref[...], grad_ref[...])

    @pl.when(step < 4)
    def _():
        far_ref[0] = part.astype(BF)

    @pl.when(step >= 4)
    def _():
        near_ref[0] = part


def grad_weight_rows(attn_t, grad_rows):
    features, frames = attn_t.shape
    size = features // 8
    core, z = lax.axis_index("core"), lax.axis_index("z")
    far, near = pl.pallas_call(
        grad_weight_kernel,
        grid_spec=pltpu.PrefetchScalarGridSpec(
            num_scalar_prefetch=1,
            grid=(8,),
            in_specs=[
                pl.BlockSpec(
                    (size, frames),
                    lambda i, c: (jnp.where(i < 4, 2 * i + 1 - c[0], 2 * (i - 4) + c[0]), 0),
                ),
                pl.BlockSpec((frames, features), lambda i, c: (0, 0)),
            ],
            out_specs=[
                pl.BlockSpec((1, size, features), lambda i, c: (jnp.minimum(i, 3), 0, 0)),
                pl.BlockSpec((1, size, features), lambda i, c: (jnp.maximum(i - 4, 0), 0, 0)),
            ],
        ),
        out_shape=[
            jax.ShapeDtypeStruct((4, size, features), BF),
            jax.ShapeDtypeStruct((4, size, features), F32),
        ],
        compiler_params=pltpu.CompilerParams(vmem_limit_bytes=VMEM_LIMIT),
        cost_estimate=pl.CostEstimate(
            flops=2 * features * features * frames,
            bytes_accessed=features * features * 3 + features * frames * 4,
            transcendentals=0,
        ),
        name="grad_weight",
    )(core.reshape(1).astype(jnp.int32), attn_t, grad_rows)
    total = near + shift(far, "core", 1).astype(F32)
    for axis in ("z", "x", "y"):
        me = lax.axis_index(axis)
        mine = lax.dynamic_index_in_dim(total, me, 0, keepdims=False)
        for k in range(1, 4):
            piece = lax.dynamic_index_in_dim(total, (me + k) % 4, 0, keepdims=False)
            mine = mine + shift(piece.astype(BF), axis, k).astype(F32)
        if axis == "z":
            total = mine.reshape(4, 4, size // 16, features)
        else:
            total = mine
    return total


def body(queries, own_keys, own_values, lengths, history, cache_blocks, out_weight, grad_out):
    owned = cache_blocks.shape[0]
    _, frames, features = queries.shape
    here = {axis: lax.axis_index(axis) for axis in ("x", "y")}
    ids = history[0]
    owners = ids // owned
    offset = {"x": (here["x"] - owners // 4) % 4, "y": (here["y"] - owners % 4) % 4}

    slabs = spread_slabs(out_weight, ids)
    noted = {
        "y": [ids] + [slabs[0][4 - j, out_weight.shape[0], : ids.shape[0]] for j in range(1, 4)],
        "x": [ids] + [slabs[4 - j][0, out_weight.shape[0], : ids.shape[0]] for j in range(1, 4)],
    }
    tables = {}
    for first, second in (("x", "y"), ("y", "x")):
        asked = jnp.stack([n.astype(jnp.int32) for n in noted[second]])
        along = (here[first] - jnp.arange(4, dtype=jnp.int32)) % 4
        owner = along * 4 + here["y"] if first == "x" else here["x"] * 4 + along
        match = (asked // owned)[:, None, :] == owner[None, :, None]
        tables[first] = jnp.max(jnp.where(match, (asked % owned)[:, None, :], -1), axis=2)
    weight = gather_weight(slabs, out_weight.shape[0])
    valid = (jnp.arange(frames, dtype=jnp.int32) < lengths[0] * BLK)[:, None]
    grad_attn = (nt(grad_out[0], weight) * valid).astype(BF)

    results, returned = None, []
    fetched = []
    for start, width, first, second in CHUNKS:
        part = lax.slice_in_dim(cache_blocks, start, start + width, axis=3)
        held = [part] + [shift(part, first, k) for k in range(1, 4)]
        sent = select_rows(tables[first], held)
        fetched.append([sent[0]] + [shift(sent[j], second, j) for j in range(1, 4)])
    for chunk, slots in zip(CHUNKS, fetched):
        _, _, first, second = chunk
        meta = jnp.concatenate([offset[second], offset[first], lengths]).astype(jnp.int32)
        out = attend(
            meta, queries[0], own_keys[0], own_values[0], grad_attn, slots, chunk, results
        )
        results, back = out[:5], out[5:]
        parts = [back[0]] + [shift(back[j], second, -j) for j in range(1, 4)]
        sums = fold_rows(tables[first], parts)
        returned.append([sums[0]] + [shift(sums[k], first, -k) for k in range(1, 4)])
    attn, attn_t, grad_queries, grad_keys, grad_values = results
    grad_cache = total_rows(returned)
    attended = mm(attn, weight).astype(BF)
    grad_weight = grad_weight_rows(attn_t, grad_out[0])
    return (
        attended[None],
        grad_queries[None],
        grad_keys[None],
        grad_values[None],
        grad_cache,
        grad_weight,
    )


def solution(mesh):
    axes = ("z", "core", "x", "y")
    fine = Mesh(mesh.devices.reshape(4, 2, 4, 4), axes)

    def split(rank):
        return P(axes, *([None] * (rank - 1)))

    return jax.shard_map(
        body,
        mesh=fine,
        in_specs=tuple(split(rank) for rank in (3, 3, 3, 1, 2, 4, 2, 3)),
        out_specs=tuple(split(rank) for rank in (3, 3, 3, 3, 4, 2)),
        check_vma=False,
    )
```

time: 634 us -> 244 us (0.38)
  waiting for transfers between devices: 309 us -> 54.4 us
  matrix products: 147 us -> 5.83 us
  local copies, waits for them, and re-layouts: 115 us -> 27.1 us
  starting transfers between devices: 10.1 us -> 76.4 us
  Pallas kernels: 0 us -> 61.4 us
  blocking collectives: 14.4 us -> 0 us
  between operations: 14.9 us -> 1.76 us
  loops' own time: 7.3 us -> 0 us
    unnamed x3 -> x0, waiting for transfers between devices: 209 us -> none
    dot_general x55 -> x2, matrix products: 129 us -> 5.83 us  [the longest x1 3.97 us: nt(): lax.dot_general(a, b, (((1,), (1,)), ((), ())), preferred_element_type=F32)]
    ppermute x0 -> x47, starting transfers between devices: none -> 76.4 us  [shift(): return lax.ppermute(array, axis, [(i, (i + amount) % n) for i in range(n)])]
    all_to_all x2 -> x0, waiting for transfers between devices: 65.8 us -> none  [the longest x1 65.7 us: fetch_blocks(): lax.all_to_all(sending, 'utt', split_axis=0, concat_axis=0, tiled=True)]
    pallas_call x0 -> x9, Pallas kernels: none -> 61.4 us  [the longest x2 33.5 us: attend(): pl.pallas_call(attend_kernel, grid_spec=pltpu.PrefetchScalarGridSpec(num_...]
    ppermute x0 -> x47, waiting for transfers between devices: none -> 54.4 us  [shift(): return lax.ppermute(array, axis, [(i, (i + amount) % n) for i in range(n)])]
    dynamic_slice x80 -> x0, local copies, waits for them, and re-layouts: 52.5 us -> none  [the longest x10 12.6 us: head_pairs(): lax.map(one_pair, jnp.arange(features // pair_width, dtype=jnp.int32))]
    all_gather x1 -> x0, waiting for transfers between devices: 34.6 us -> none  [body(): lax.all_gather(out_weight, ('call', 'utt'), axis=0, tiled=True)]
  transfers between devices with their start and end apart: 4 -> 47, of which waited for: 3 -> 14; matrix products, arithmetic and copies ran while one was open for 4% -> 14% of each run, Pallas kernels for 0% -> 16%
where the time goes in v1:
time: 244 us; the launch traced here: 243 us
  starting transfers between devices  76.4 us (31%)
  Pallas kernels  61.4 us (25%)
  waiting for transfers between devices  54.4 us (22%)
  local copies, waits for them, and re-layouts  27.1 us (11%)
  other arithmetic  16.1 us (7%)
  matrix products  5.83 us (2%)
    ppermute x47, starting transfers between devices, shift(): return lax.ppermute(array, axis, [(i, (i + amount) % n) for i in range(n)])  76.4 us
    ppermute x47, waiting for transfers between devices, shift(): return lax.ppermute(array, axis, [(i, (i + amount) % n) for i in range(n)])  54.4 us
    pallas_call x2, Pallas kernels, attend(): pl.pallas_call(attend_kernel, grid_spec=pltpu.PrefetchScalarGridSpec(num_...  33.5 us
    unnamed x54, local copies, waits for them, and re-layouts  11.9 us
    pallas_call x2, Pallas kernels, fold_rows(): pl.pallas_call(fold_kernel, grid_spec=pltpu.PrefetchScalarGridSpec(num_sc...  9.04 us
    gather x3, local copies, waits for them, and re-layouts, gather_weight(): jnp.take(jnp.take(rows, (x - steps) % 4, axis=0), (y - steps) % 4, axis=1)  5.71 us
    pallas_call x1, Pallas kernels, grad_weight_rows(): pl.pallas_call(grad_weight_kernel, grid_spec=pltpu.PrefetchScalarGridSpec...  5.5 us
  transfers between devices with their start and end apart: 47, of which 14 were waited for; matrix products, arithmetic and copies ran while one was open for 14% of the time, Pallas kernels for 16%

profile of v1, /device:TPU:32, one launch (start us, length us, event | category | flops | bytes accessed | tf_op | source)
XLA Modules:
  0.0 243.1 jit_solution(2358673716507147600)
XLA Ops:
  2.3 3.0 %collective-permute-start.2 = (bf16[16,1280]{1,0:T(8,128)(2,1)S(1)}, bf16[16,1280]{1,0:T(8,128)(2,1)S(1)}, u32[]{:S(2)}, u32[]{:S(2)}) collective-permute-start(bf16[16,1280]{1,0:T(8,128)(2,1)S(1)} %maximum_maximum_fusion), channel_id=1, source_target_pairs={{0,3},{1,0},{2,1},{3,2},{4,7},{5,4},{6,5},{7,6},{8,11},{9,8},{10,9... | collective-permute-start | bytes 122888 | tf_op jit(solution)/shard_map/ppermute | solution.py:23
  8.1 2.0 collective-permute-start.13
  10.0 1.8 collective-permute-start.14
  15.0 2.8 %collective-permute-start.5 = (bf16[4,16,1280]{2,1,0:T(8,128)(2,1)S(1)}, bf16[4,16,1280]{2,1,0:T(8,128)(2,1)S(1)}, u32[]{:S(2)}, u32[]{:S(2)}) collective-permute-start(bf16[4,16,1280]{2,1,0:T(8,128)(2,1)S(1)} %get-tuple-element.92), channel_id=1, source_target_pairs={{0,12},{4,0},{8,4},{12,8},{1,13},{5,1},{9,5},{13,9},{2,14},{6,2},{... | collective-permute-start | bytes 491528 | tf_op jit(solution)/shard_map/ppermute | solution.py:23
  19.9 3.6 %collective-permute-done.5 = bf16[4,16,1280]{2,1,0:T(8,128)(2,1)S(1)} collective-permute-done((bf16[4,16,1280]{2,1,0:T(8,128)(2,1)S(1)}, bf16[4,16,1280]{2,1,0:T(8,128)(2,1)S(1)}, u32[]{:S(2)}, u32[]{:S(2)}) %collective-permute-start.5) | collective-permute-done | bytes 163872 | tf_op jit(solution)/shard_map/ppermute | solution.py:23
  25.6 2.8 %collective-permute-done.3 = bf16[4,16,1280]{2,1,0:T(8,128)(2,1)S(1)} collective-permute-done((bf16[4,16,1280]{2,1,0:T(8,128)(2,1)S(1)}, bf16[4,16,1280]{2,1,0:T(8,128)(2,1)S(1)}, u32[]{:S(2)}, u32[]{:S(2)}) %collective-permute-start.3) | collective-permute-done | bytes 163872 | tf_op jit(solution)/shard_map/ppermute | solution.py:23
  30.7 2.5 %gather_fusion = bf16[4,4,10,1280]{3,2,1,0:T(8,128)(2,1)} fusion(bf16[4,4,10,1280]{3,2,1,0:T(8,128)(2,1)} %pad_maximum_fusion, s32[1024]{0:T(1024)S(1)} %pad_clamp_fusion.1), kind=kCustom, calls=%fused_computation | custom fusion | bytes 819216 | tf_op jit(solution)/shard_map/jit(_take)/gather | solution.py:263
  33.2 2.0 broadcast_select_fusion
  35.2 2.5 %gather_fusion.1 = bf16[4,4,10,1280]{3,2,1,0:T(8,128)(2,1)} fusion(bf16[4,4,10,1280]{3,2,1,0:T(8,128)(2,1)} %broadcast_select_fusion, s32[1024]{0:T(1024)S(1)} %pad_clamp_fusion), kind=kCustom, calls=%fused_computation.1 | custom fusion | bytes 819216 | tf_op jit(solution)/shard_map/jit(_take)/gather | solution.py:263
  37.7 2.0 copy.23
  41.9 1.9 collective-permute-start.6
  43.8 4.3 %collective-permute-done.21.refs_3_ = bf16[2,2,64,640]{3,2,1,0:T(8,128)(2,1)S(1)} collective-permute-done((bf16[2,2,64,640]{3,2,1,0:T(8,128)(2,1)S(1)}, bf16[2,2,64,640]{3,2,1,0:T(8,128)(2,1)S(1)}, u32[]{:S(2)}, u32[]{:S(2)}) %collective-permute-start.21) | collective-permute-done | bytes 327712 | tf_op jit(solution)/shard_map/ppermute | solution.py:23
  48.1 3.0 %collective-permute-start.7 = (bf16[160,1280]{1,0:T(8,128)(2,1)S(1)}, bf16[160,1280]{1,0:T(8,128)(2,1)S(1)}, u32[]{:S(2)}, u32[]{:S(2)}) collective-permute-start(bf16[160,1280]{1,0:T(8,128)(2,1)S(1)} %broadcast_select_fusion.1.refs_0_), channel_id=1, source_target_pairs={{0,64},{32,96},{64,0},{96,32},{1,65},{33,97},{65,1},{97,33},{2,66}... | collective-permute-start | bytes 1228808 | tf_op jit(solution)/shard_map/ppermute | solution.py:23
  52.1 3.1 %select_rows.3 = (bf16[4,2,64,640]{3,2,1,0:T(8,128)(2,1)S(1)}, bf16[4,2,64,640]{3,2,1,0:T(8,128)(2,1)S(1)}, bf16[4,2,64,640]{3,2,1,0:T(8,128)(2,1)}, bf16[4,2,64,640]{3,2,1,0:T(8,128)(2,1)}) custom-call(s32[16]{0:T(128)S(1)} %reshape.584.table, bf16[2,2,64,640]{3,2,1,0:T(8,128)(2,1)S(1)} %get-tuple-element.86.refs_0_, ...), custom_call_target="tpu_custom_call" | custom-call | bytes 3932160 | tf_op jit(solution)/shard_map/select_rows/pallas_call | solution.py:46
  62.0 4.7 %collective-permute-done.8.refs_3_ = bf16[160,1280]{1,0:T(8,128)(2,1)S(1)} collective-permute-done((bf16[160,1280]{1,0:T(8,128)(2,1)S(1)}, bf16[160,1280]{1,0:T(8,128)(2,1)S(1)}, u32[]{:S(2)}, u32[]{:S(2)}) %collective-permute-start.8) | collective-permute-done | bytes 409632 | tf_op jit(solution)/shard_map/ppermute | solution.py:23
  66.7 1.7 collective-permute-start.23
  68.5 2.2 collective-permute-done.22.refs_5_
  77.2 1.9 collective-permute-start.16
  80.5 2.5 %collective-permute-start.18 = (bf16[4,2,64,640]{3,2,1,0:T(8,128)(2,1)S(1)}, bf16[4,2,64,640]{3,2,1,0:T(8,128)(2,1)S(1)}, u32[]{:S(2)}, u32[]{:S(2)}) collective-permute-start(bf16[4,2,64,640]{3,2,1,0:T(8,128)(2,1)S(1)} %get-tuple-element.45), channel_id=1, source_target_pairs={{0,12},{4,0},{8,4},{12,8},{1,13},{5,1},{9,5},{13,9},{2,14},{6,2},{... | collective-permute-start | bytes 1966088 | tf_op jit(solution)/shard_map/ppermute | solution.py:23
  83.2 4.7 %place_weight.1 = bf16[8,160,1280]{2,1,0:T(8,128)(2,1)} custom-call(s32[8]{0:T(128)S(1)} %pad_add_fusion.2.where, bf16[160,1280]{1,0:T(8,128)(2,1)S(1)} %broadcast_select_fusion.1.refs_0_, bf16[160,1280]{1,0:T(8,128)(2,1)S(1)} %collective-permute-done.6.refs_1_, bf16[160,1280]{1,0:T(8,128)(2,1)S(1)} %collective-permute-done.7.refs_2_, ...), custom_call_target="tpu_custom_call" | custom-call | bytes 6553600 | tf_op jit(solution)/shard_map/place_weight/pallas_call | solution.py:270
  88.0 4.0 %fusion.1.refs_3_ = bf16[256,1280]{1,0:T(8,128)(2,1)} fusion(bf16[1280,1280]{1,0:T(8,128)(2,1)} %bitcast.117, f32[256]{0:T(256)S(1)} %copy-done.26, bf16[1,256,1280]{2,1,0:T(8,128)(2,1)S(1)} %copy-done.12), kind=kOutput, calls=%fused_computation.6 | convolution fusion | flops 839516160 | bytes 4588544 | tf_op jit(solution)/shard_map/dot_general | solution.py:27
  92.0 6.5 %collective-permute-done.24.refs_7_ = bf16[4,2,64,640]{3,2,1,0:T(8,128)(2,1)} collective-permute-done((bf16[4,2,64,640]{3,2,1,0:T(8,128)(2,1)}, bf16[4,2,64,640]{3,2,1,0:T(8,128)(2,1)}, u32[]{:S(2)}, u32[]{:S(2)}) %collective-permute-start.24) | collective-permute-done | bytes 655392 | tf_op jit(solution)/shard_map/ppermute | solution.py:23
  98.5 16.7 %attend.2 = (bf16[256,1280]{1,0:T(8,128)(2,1)S(1)}, bf16[1280,256]{1,0:T(8,128)(2,1)S(1)}, bf16[256,1280]{1,0:T(8,128)(2,1)}, bf16[256,1280]{1,0:T(8,128)(2,1)},...) custom-call(s32[17]{0:T(128)S(1)} %get-tuple-element.97.meta, ...), custom_call_target="tpu_custom_call" | custom-call | flops 1509949440 | bytes 6881280 | tf_op jit(solution)/shard_map/attend/pallas_call | solution.py:222
  116.5 16.8 %attend.3 = (bf16[256,1280]{1,0:T(8,128)(2,1)S(1)}, bf16[1280,256]{1,0:T(8,128)(2,1)S(1)}, bf16[256,1280]{1,0:T(8,128)(2,1)}, bf16[256,1280]{1,0:T(8,128)(2,1)},...) custom-call(s32[17]{0:T(128)S(1)} %get-tuple-element.98.meta, ...), custom_call_target="tpu_custom_call", output_to_operand_aliasing={{0}: (9, {}), {1}: (10, {}), {2}: (11, {}), {3}: (12, {}), ... | custom-call | flops 1509949440 | bytes 6881280 | tf_op jit(solution)/shard_map/attend/pallas_call | solution.py:222
  133.3 5.5 %grad_weight.1 = (bf16[4,160,1280]{2,1,0:T(8,128)(2,1)}, f32[4,160,1280]{2,1,0:T(8,128)}) custom-call(s32[1]{0:T(128)} %bitcast.29.core, bf16[1280,256]{1,0:T(8,128)(2,1)S(1)} %get-tuple-element.75.attn_t_ref, bf16[256,1280]{1,0:T(8,128)(2,1)S(1)} %bitcast.116), custom_call_target="tpu_custom_call" | custom-call | flops 838860800 | bytes 6225920 | tf_op jit(solution)/shard_map/grad_weight/pallas_call | solution.py:305
  139.0 2.7 %collective-permute-start.25 = (bf16[4,2,64,640]{3,2,1,0:T(8,128)(2,1)S(1)}, bf16[4,2,64,640]{3,2,1,0:T(8,128)(2,1)S(1)}, u32[]{:S(2)}, u32[]{:S(2)}) collective-permute-start(bf16[4,2,64,640]{3,2,1,0:T(8,128)(2,1)S(1)} %get-tuple-element.60), channel_id=1, source_target_pairs={{0,3},{1,0},{2,1},{3,2},{4,7},{5,4},{6,5},{7,6},{8,11},{9,8},{10,9... | collective-permute-start | bytes 1966088 | tf_op jit(solution)/shard_map/ppermute | solution.py:23
  142.7 2.8 %convert_add_fusion = f32[4,160,1280]{2,1,0:T(8,128)S(1)} fusion(f32[4,160,1280]{2,1,0:T(8,128)} %get-tuple-element.76, bf16[4,160,1280]{2,1,0:T(8,128)(2,1)} %collective-permute-done.37), kind=kLoop, calls=%fused_computation.2 | loop fusion | flops 1638400 | bytes 8192000 | tf_op jit(solution)/shard_map/add | solution.py:334
  145.5 1.7 copy-done.17
  149.2 6.7 %collective-permute-start.39 = (bf16[160,1280]{1,0:T(8,128)(2,1)}, bf16[160,1280]{1,0:T(8,128)(2,1)}, u32[]{:S(2)}, u32[]{:S(2)}) collective-permute-start(bf16[160,1280]{1,0:T(8,128)(2,1)} %get-tuple-element.82), channel_id=1, source_target_pairs={{0,64},{32,96},{64,0},{96,32},{1,65},{33,97},{65,1},{97,33},{2,66}... | collective-permute-start | bytes 1228808 | tf_op jit(solution)/shard_map/ppermute | solution.py:23
  157.7 6.8 %collective-permute-done.40 = bf16[160,1280]{1,0:T(8,128)(2,1)} collective-permute-done((bf16[160,1280]{1,0:T(8,128)(2,1)}, bf16[160,1280]{1,0:T(8,128)(2,1)}, u32[]{:S(2)}, u32[]{:S(2)}) %collective-permute-start.40) | collective-permute-done | bytes 409632 | tf_op jit(solution)/shard_map/ppermute | solution.py:23
  165.3 9.2 %collective-permute-done.39 = bf16[160,1280]{1,0:T(8,128)(2,1)} collective-permute-done((bf16[160,1280]{1,0:T(8,128)(2,1)}, bf16[160,1280]{1,0:T(8,128)(2,1)}, u32[]{:S(2)}, u32[]{:S(2)}) %collective-permute-start.39) | collective-permute-done | bytes 409632 | tf_op jit(solution)/shard_map/ppermute | solution.py:23
  174.4 2.7 %collective-permute-start.32 = (bf16[4,2,64,640]{3,2,1,0:T(8,128)(2,1)}, bf16[4,2,64,640]{3,2,1,0:T(8,128)(2,1)}, u32[]{:S(2)}, u32[]{:S(2)}) collective-permute-start(bf16[4,2,64,640]{3,2,1,0:T(8,128)(2,1)} %copy-done.14), channel_id=1, source_target_pairs={{0,8},{4,12},{8,0},{12,4},{1,9},{5,13},{9,1},{13,5},{2,10},{6,14},... | collective-permute-start | bytes 1966088 | tf_op jit(solution)/shard_map/ppermute | solution.py:23
  177.2 2.6 %fusion.4 = f32[160,1280]{1,0:T(8,128)} fusion(bf16[160,1280]{1,0:T(8,128)(2,1)} %collective-permute-done.40, bf16[160,1280]{1,0:T(8,128)(2,1)} %collective-permute-done.39, bf16[160,1280]{1,0:T(8,128)(2,1)} %collective-permute-done.38, f32[4,160,1280]{2,1,0:T(8,128)} %copy-done.17, s32[]{:T(128)S(6)} %select_n.251), kind=kLoop, calls=%fused_computation.10 | loop fusion | flops 1228800 | bytes 2867204 | tf_op jit(solution)/shard_map/add | solution.py:340
  179.7 2.3 reshape.586
  182.1 2.0 fusion.10
  184.0 3.2 %collective-permute-start.43 = (bf16[4,10,1280]{2,1,0:T(8,128)(2,1)}, bf16[4,10,1280]{2,1,0:T(8,128)(2,1)}, u32[]{:S(2)}, u32[]{:S(2)}) collective-permute-start(bf16[4,10,1280]{2,1,0:T(8,128)(2,1)} %get-tuple-element.84), channel_id=1, source_target_pairs={{0,12},{4,0},{8,4},{12,8},{1,13},{5,1},{9,5},{13,9},{2,14},{6,2},{... | collective-permute-start | bytes 307208 | tf_op jit(solution)/shard_map/ppermute | solution.py:23
  188.0 2.7 %collective-permute-start.42 = (bf16[4,10,1280]{2,1,0:T(8,128)(2,1)}, bf16[4,10,1280]{2,1,0:T(8,128)(2,1)}, u32[]{:S(2)}, u32[]{:S(2)}) collective-permute-start(bf16[4,10,1280]{2,1,0:T(8,128)(2,1)} %get-tuple-element.85), channel_id=1, source_target_pairs={{0,8},{4,12},{8,0},{12,4},{1,9},{5,13},{9,1},{13,5},{2,10},{6,14},... | collective-permute-start | bytes 307208 | tf_op jit(solution)/shard_map/ppermute | solution.py:23
  190.7 4.4 %fold_rows.2 = (bf16[2,2,64,640]{3,2,1,0:T(8,128)(2,1)S(1)}, bf16[2,2,64,640]{3,2,1,0:T(8,128)(2,1)S(1)}, bf16[2,2,64,640]{3,2,1,0:T(8,128)(2,1)S(1)}, bf16[2,2,64,640]{3,2,1,0:T(8,128)(2,1)S(1)}) custom-call(s32[16]{0:T(128)S(1)} %reshape.584.table, bf16[4,2,64,640]{3,2,1,0:T(8,128)(2,1)S(1)} %get-tuple-element.59.refs_0_, ...), custom_call_target="tpu_custom_call" | custom-call | bytes 3932160 | tf_op jit(solution)/shard_map/fold_rows/pallas_call | solution.py:79
  195.0 4.2 %collective-permute-start.28 = (bf16[2,2,64,640]{3,2,1,0:T(8,128)(2,1)S(1)}, bf16[2,2,64,640]{3,2,1,0:T(8,128)(2,1)S(1)}, u32[]{:S(2)}, u32[]{:S(2)}) collective-permute-start(bf16[2,2,64,640]{3,2,1,0:T(8,128)(2,1)S(1)} %get-tuple-element.64), channel_id=1, source_target_pairs={{0,12},{4,0},{8,4},{12,8},{1,13},{5,1},{9,5},{13,9},{2,14},{6,2},{... | collective-permute-start | bytes 983048 | tf_op jit(solution)/shard_map/ppermute | solution.py:23
  199.2 8.9 %collective-permute-done.33.refs_3_ = bf16[4,2,64,640]{3,2,1,0:T(8,128)(2,1)} collective-permute-done((bf16[4,2,64,640]{3,2,1,0:T(8,128)(2,1)}, bf16[4,2,64,640]{3,2,1,0:T(8,128)(2,1)}, u32[]{:S(2)}, u32[]{:S(2)}) %collective-permute-start.33) | collective-permute-done | bytes 655392 | tf_op jit(solution)/shard_map/ppermute | solution.py:23
  208.1 3.0 %collective-permute-start.29 = (bf16[2,2,64,640]{3,2,1,0:T(8,128)(2,1)S(1)}, bf16[2,2,64,640]{3,2,1,0:T(8,128)(2,1)S(1)}, u32[]{:S(2)}, u32[]{:S(2)}) collective-permute-start(bf16[2,2,64,640]{3,2,1,0:T(8,128)(2,1)S(1)} %get-tuple-element.65), channel_id=1, source_target_pairs={{0,8},{4,12},{8,0},{12,4},{1,9},{5,13},{9,1},{13,5},{2,10},{6,14},... | collective-permute-start | bytes 983048 | tf_op jit(solution)/shard_map/ppermute | solution.py:23
  211.1 4.7 %fold_rows.3 = (bf16[2,2,64,640]{3,2,1,0:T(8,128)(2,1)S(1)}, bf16[2,2,64,640]{3,2,1,0:T(8,128)(2,1)S(1)}, bf16[2,2,64,640]{3,2,1,0:T(8,128)(2,1)S(1)}, bf16[2,2,64,640]{3,2,1,0:T(8,128)(2,1)S(1)}) custom-call(s32[16]{0:T(128)S(1)} %reshape.583.table, bf16[4,2,64,640]{3,2,1,0:T(8,128)(2,1)S(1)} %get-tuple-element.67.refs_0_, ...), custom_call_target="tpu_custom_call" | custom-call | bytes 3932160 | tf_op jit(solution)/shard_map/fold_rows/pallas_call | solution.py:79
  215.8 9.7 %collective-permute-start.34 = (bf16[2,2,64,640]{3,2,1,0:T(8,128)(2,1)S(1)}, bf16[2,2,64,640]{3,2,1,0:T(8,128)(2,1)S(1)}, u32[]{:S(2)}, u32[]{:S(2)}) collective-permute-start(bf16[2,2,64,640]{3,2,1,0:T(8,128)(2,1)S(1)} %get-tuple-element.72), channel_id=1, source_target_pairs={{0,3},{1,0},{2,1},{3,2},{4,7},{5,4},{6,5},{7,6},{8,11},{9,8},{10,9... | collective-permute-start | bytes 983048 | tf_op jit(solution)/shard_map/ppermute | solution.py:23
  230.0 1.9 collective-permute-start.46
  231.9 2.2 collective-permute-start.45
  234.1 1.9 fusion.2
  236.0 2.5 %collective-permute-done.36.refs_7_ = bf16[2,2,64,640]{3,2,1,0:T(8,128)(2,1)S(1)} collective-permute-done((bf16[2,2,64,640]{3,2,1,0:T(8,128)(2,1)S(1)}, bf16[2,2,64,640]{3,2,1,0:T(8,128)(2,1)S(1)}, u32[]{:S(2)}, u32[]{:S(2)}) %collective-permute-start.36) | collective-permute-done | bytes 327712 | tf_op jit(solution)/shard_map/ppermute | solution.py:23
  238.5 4.0 %total_rows.1 = f32[2,2,64,1280]{3,2,1,0:T(8,128)} custom-call(bf16[2,2,64,640]{3,2,1,0:T(8,128)(2,1)S(1)} %get-tuple-element.63.refs_0_, bf16[2,2,64,640]{3,2,1,0:T(8,128)(2,1)S(1)} %collective-permute-done.28.refs_1_, bf16[2,2,64,640]{3,2,1,0:T(8,128)(2,1)S(1)} %collective-permute-done.29.refs_2_, ...), custom_call_target="tpu_custom_call" | custom-call | bytes 3932160 | tf_op jit(solution)/shard_map/total_rows/pallas_call | solution.py:126
  (161 shorter events, 44.1 us)
Async XLA Ops:
  2.3 12.6 %collective-permute-start.2 = (bf16[16,1280]{1,0:T(8,128)(2,1)S(1)}, bf16[16,1280]{1,0:T(8,128)(2,1)S(1)}, u32[]{:S(2)}, u32[]{:S(2)}) collective-permute-start(bf16[16,1280]{1,0:T(8,128)(2,1)S(1)} %maximum_maximum_fusion), channel_id=1, source_target_pairs={{0,3},{1,0},{2,1},{3,2},{4,7},{5,4},{6,5},{7,6},{8,11},{9,8},{10,9... | collective-permute-start | bytes 122888 | tf_op jit(solution)/shard_map/ppermute | solution.py:23
  5.3 9.6 %collective-permute-start.1 = (bf16[16,1280]{1,0:T(8,128)(2,1)S(1)}, bf16[16,1280]{1,0:T(8,128)(2,1)S(1)}, u32[]{:S(2)}, u32[]{:S(2)}) collective-permute-start(bf16[16,1280]{1,0:T(8,128)(2,1)S(1)} %maximum_maximum_fusion), channel_id=1, source_target_pairs={{0,2},{1,3},{2,0},{3,1},{4,6},{5,7},{6,4},{7,5},{8,10},{9,11},{10,... | collective-permute-start | bytes 122888 | tf_op jit(solution)/shard_map/ppermute | solution.py:23
  6.0 9.0 %collective-permute-start = (bf16[16,1280]{1,0:T(8,128)(2,1)S(1)}, bf16[16,1280]{1,0:T(8,128)(2,1)S(1)}, u32[]{:S(2)}, u32[]{:S(2)}) collective-permute-start(bf16[16,1280]{1,0:T(8,128)(2,1)S(1)} %maximum_maximum_fusion), channel_id=1, source_target_pairs={{0,1},{1,2},{2,3},{3,0},{4,5},{5,6},{6,7},{7,4},{8,9},{9,10},{10,1... | collective-permute-start | bytes 122888 | tf_op jit(solution)/shard_map/ppermute | solution.py:23
  8.1 47.9 %collective-permute-start.13 = (bf16[2,2,64,640]{3,2,1,0:T(8,128)(2,1)S(1)}, bf16[2,2,64,640]{3,2,1,0:T(8,128)(2,1)S(1)}, u32[]{:S(2)}, u32[]{:S(2)}) collective-permute-start(bf16[2,2,64,640]{3,2,1,0:T(8,128)(2,1)S(1)} %get-tuple-element.87.refs_0_), channel_id=1, source_target_pairs={{0,1},{1,2},{2,3},{3,0},{4,5},{5,6},{6,7},{7,4},{8,9},{9,10},{10,1... | collective-permute-start | bytes 983048 | tf_op jit(solution)/shard_map/ppermute | solution.py:23
  10.0 47.7 %collective-permute-start.14 = (bf16[2,2,64,640]{3,2,1,0:T(8,128)(2,1)S(1)}, bf16[2,2,64,640]{3,2,1,0:T(8,128)(2,1)S(1)}, u32[]{:S(2)}, u32[]{:S(2)}) collective-permute-start(bf16[2,2,64,640]{3,2,1,0:T(8,128)(2,1)S(1)} %get-tuple-element.87.refs_0_), channel_id=1, source_target_pairs={{0,2},{1,3},{2,0},{3,1},{4,6},{5,7},{6,4},{7,5},{8,10},{9,11},{10,... | collective-permute-start | bytes 983048 | tf_op jit(solution)/shard_map/ppermute | solution.py:23
  15.0 8.4 %collective-permute-start.5 = (bf16[4,16,1280]{2,1,0:T(8,128)(2,1)S(1)}, bf16[4,16,1280]{2,1,0:T(8,128)(2,1)S(1)}, u32[]{:S(2)}, u32[]{:S(2)}) collective-permute-start(bf16[4,16,1280]{2,1,0:T(8,128)(2,1)S(1)} %get-tuple-element.92), channel_id=1, source_target_pairs={{0,12},{4,0},{8,4},{12,8},{1,13},{5,1},{9,5},{13,9},{2,14},{6,2},{... | collective-permute-start | bytes 491528 | tf_op jit(solution)/shard_map/ppermute | solution.py:23
  17.8 7.6 %collective-permute-start.4 = (bf16[4,16,1280]{2,1,0:T(8,128)(2,1)S(1)}, bf16[4,16,1280]{2,1,0:T(8,128)(2,1)S(1)}, u32[]{:S(2)}, u32[]{:S(2)}) collective-permute-start(bf16[4,16,1280]{2,1,0:T(8,128)(2,1)S(1)} %get-tuple-element.92), channel_id=1, source_target_pairs={{0,8},{4,12},{8,0},{12,4},{1,9},{5,13},{9,1},{13,5},{2,10},{6,14},... | collective-permute-start | bytes 491528 | tf_op jit(solution)/shard_map/ppermute | solution.py:23
  18.6 9.7 %collective-permute-start.3 = (bf16[4,16,1280]{2,1,0:T(8,128)(2,1)S(1)}, bf16[4,16,1280]{2,1,0:T(8,128)(2,1)S(1)}, u32[]{:S(2)}, u32[]{:S(2)}) collective-permute-start(bf16[4,16,1280]{2,1,0:T(8,128)(2,1)S(1)} %get-tuple-element.92), channel_id=1, source_target_pairs={{0,4},{4,8},{8,12},{12,0},{1,5},{5,9},{9,13},{13,1},{2,6},{6,10},{... | collective-permute-start | bytes 491528 | tf_op jit(solution)/shard_map/ppermute | solution.py:23
  23.4 36.6 %collective-permute-start.15 = (bf16[2,2,64,640]{3,2,1,0:T(8,128)(2,1)S(1)}, bf16[2,2,64,640]{3,2,1,0:T(8,128)(2,1)S(1)}, u32[]{:S(2)}, u32[]{:S(2)}) collective-permute-start(bf16[2,2,64,640]{3,2,1,0:T(8,128)(2,1)S(1)} %get-tuple-element.87.refs_0_), channel_id=1, source_target_pairs={{0,3},{1,0},{2,1},{3,2},{4,7},{5,4},{6,5},{7,6},{8,11},{9,8},{10,9... | collective-permute-start | bytes 983048 | tf_op jit(solution)/shard_map/ppermute | solution.py:23
  25.4 15.5 %collective-permute-start.19 = (bf16[2,2,64,640]{3,2,1,0:T(8,128)(2,1)S(1)}, bf16[2,2,64,640]{3,2,1,0:T(8,128)(2,1)S(1)}, u32[]{:S(2)}, u32[]{:S(2)}) collective-permute-start(bf16[2,2,64,640]{3,2,1,0:T(8,128)(2,1)S(1)} %get-tuple-element.86.refs_0_), channel_id=1, source_target_pairs={{0,4},{4,8},{8,12},{12,0},{1,5},{5,9},{9,13},{13,1},{2,6},{6,10},{... | collective-permute-start | bytes 983048 | tf_op jit(solution)/shard_map/ppermute | solution.py:23
  28.4 12.8 %collective-permute-start.20 = (bf16[2,2,64,640]{3,2,1,0:T(8,128)(2,1)S(1)}, bf16[2,2,64,640]{3,2,1,0:T(8,128)(2,1)S(1)}, u32[]{:S(2)}, u32[]{:S(2)}) collective-permute-start(bf16[2,2,64,640]{3,2,1,0:T(8,128)(2,1)S(1)} %get-tuple-element.86.refs_0_), channel_id=1, source_target_pairs={{0,8},{4,12},{8,0},{12,4},{1,9},{5,13},{9,1},{13,5},{2,10},{6,14},... | collective-permute-start | bytes 983048 | tf_op jit(solution)/shard_map/ppermute | solution.py:23
  41.0 7.1 %collective-permute-start.21 = (bf16[2,2,64,640]{3,2,1,0:T(8,128)(2,1)S(1)}, bf16[2,2,64,640]{3,2,1,0:T(8,128)(2,1)S(1)}, u32[]{:S(2)}, u32[]{:S(2)}) collective-permute-start(bf16[2,2,64,640]{3,2,1,0:T(8,128)(2,1)S(1)} %get-tuple-element.86.refs_0_), channel_id=1, source_target_pairs={{0,12},{4,0},{8,4},{12,8},{1,13},{5,1},{9,5},{13,9},{2,14},{6,2},{... | collective-permute-start | bytes 983048 | tf_op jit(solution)/shard_map/ppermute | solution.py:23
  41.9 19.5 %collective-permute-start.6 = (bf16[160,1280]{1,0:T(8,128)(2,1)S(1)}, bf16[160,1280]{1,0:T(8,128)(2,1)S(1)}, u32[]{:S(2)}, u32[]{:S(2)}) collective-permute-start(bf16[160,1280]{1,0:T(8,128)(2,1)S(1)} %broadcast_select_fusion.1.refs_0_), channel_id=1, source_target_pairs={{0,32},{32,64},{64,96},{96,0},{1,33},{33,65},{65,97},{97,1},{2,34}... | collective-permute-start | bytes 1228808 | tf_op jit(solution)/shard_map/ppermute | solution.py:23
  48.1 13.8 %collective-permute-start.7 = (bf16[160,1280]{1,0:T(8,128)(2,1)S(1)}, bf16[160,1280]{1,0:T(8,128)(2,1)S(1)}, u32[]{:S(2)}, u32[]{:S(2)}) collective-permute-start(bf16[160,1280]{1,0:T(8,128)(2,1)S(1)} %broadcast_select_fusion.1.refs_0_), channel_id=1, source_target_pairs={{0,64},{32,96},{64,0},{96,32},{1,65},{33,97},{65,1},{97,33},{2,66}... | collective-permute-start | bytes 1228808 | tf_op jit(solution)/shard_map/ppermute | solution.py:23
  56.8 9.9 %collective-permute-start.8 = (bf16[160,1280]{1,0:T(8,128)(2,1)S(1)}, bf16[160,1280]{1,0:T(8,128)(2,1)S(1)}, u32[]{:S(2)}, u32[]{:S(2)}) collective-permute-start(bf16[160,1280]{1,0:T(8,128)(2,1)S(1)} %broadcast_select_fusion.1.refs_0_), channel_id=1, source_target_pairs={{0,96},{32,0},{64,32},{96,64},{1,97},{33,1},{65,33},{97,65},{2,98}... | collective-permute-start | bytes 1228808 | tf_op jit(solution)/shard_map/ppermute | solution.py:23
  58.5 12.2 %collective-permute-start.22 = (bf16[4,2,64,640]{3,2,1,0:T(8,128)(2,1)S(1)}, bf16[4,2,64,640]{3,2,1,0:T(8,128)(2,1)S(1)}, u32[]{:S(2)}, u32[]{:S(2)}) collective-permute-start(bf16[4,2,64,640]{3,2,1,0:T(8,128)(2,1)S(1)} %get-tuple-element.47), channel_id=1, source_target_pairs={{0,1},{1,2},{2,3},{3,0},{4,5},{5,6},{6,7},{7,4},{8,9},{9,10},{10,1... | collective-permute-start | bytes 1966088 | tf_op jit(solution)/shard_map/ppermute | solution.py:23
  60.7 6.0 %collective-permute-start.9 = (bf16[160,1280]{1,0:T(8,128)(2,1)S(1)}, bf16[160,1280]{1,0:T(8,128)(2,1)S(1)}, u32[]{:S(2)}, u32[]{:S(2)}) collective-permute-start(bf16[160,1280]{1,0:T(8,128)(2,1)S(1)} %broadcast_select_fusion.1.refs_0_), channel_id=1, source_target_pairs={{0,16},{16,0},{1,17},{17,1},{2,18},{18,2},{3,19},{19,3},{4,20},{20... | collective-permute-start | bytes 1228808 | tf_op jit(solution)/shard_map/ppermute | solution.py:23
  61.4 15.8 %collective-permute-start.10 = (bf16[160,1280]{1,0:T(8,128)(2,1)S(1)}, bf16[160,1280]{1,0:T(8,128)(2,1)S(1)}, u32[]{:S(2)}, u32[]{:S(2)}) collective-permute-start(bf16[160,1280]{1,0:T(8,128)(2,1)S(1)} %collective-permute-done.6.refs_1_), channel_id=1, source_target_pairs={{0,16},{16,0},{1,17},{17,1},{2,18},{18,2},{3,19},{19,3},{4,20},{20... | collective-permute-start | bytes 1228808 | tf_op jit(solution)/shard_map/ppermute | solution.py:23
  61.9 17.2 %collective-permute-start.11 = (bf16[160,1280]{1,0:T(8,128)(2,1)S(1)}, bf16[160,1280]{1,0:T(8,128)(2,1)S(1)}, u32[]{:S(2)}, u32[]{:S(2)}) collective-permute-start(bf16[160,1280]{1,0:T(8,128)(2,1)S(1)} %collective-permute-done.7.refs_2_), channel_id=1, source_target_pairs={{0,16},{16,0},{1,17},{17,1},{2,18},{18,2},{3,19},{19,3},{4,20},{20... | collective-permute-start | bytes 1228808 | tf_op jit(solution)/shard_map/ppermute | solution.py:23
  66.7 13.8 %collective-permute-start.12 = (bf16[160,1280]{1,0:T(8,128)(2,1)S(1)}, bf16[160,1280]{1,0:T(8,128)(2,1)}, u32[]{:S(2)}, u32[]{:S(2)}) collective-permute-start(bf16[160,1280]{1,0:T(8,128)(2,1)S(1)} %collective-permute-done.8.refs_3_), channel_id=1, source_target_pairs={{0,16},{16,0},{1,17},{17,1},{2,18},{18,2},{3,19},{19,3},{4,20},{20... | collective-permute-start | bytes 1228808 | tf_op jit(solution)/shard_map/ppermute | solution.py:23
  66.7 25.2 %collective-permute-start.23 = (bf16[4,2,64,640]{3,2,1,0:T(8,128)(2,1)}, bf16[4,2,64,640]{3,2,1,0:T(8,128)(2,1)}, u32[]{:S(2)}, u32[]{:S(2)}) collective-permute-start(bf16[4,2,64,640]{3,2,1,0:T(8,128)(2,1)} %get-tuple-element.48), channel_id=1, source_target_pairs={{0,2},{1,3},{2,0},{3,1},{4,6},{5,7},{6,4},{7,5},{8,10},{9,11},{10,... | collective-permute-start | bytes 1966088 | tf_op jit(solution)/shard_map/ppermute | solution.py:23
  70.7 27.8 %collective-permute-start.24 = (bf16[4,2,64,640]{3,2,1,0:T(8,128)(2,1)}, bf16[4,2,64,640]{3,2,1,0:T(8,128)(2,1)}, u32[]{:S(2)}, u32[]{:S(2)}) collective-permute-start(bf16[4,2,64,640]{3,2,1,0:T(8,128)(2,1)} %get-tuple-element.49), channel_id=1, source_target_pairs={{0,3},{1,0},{2,1},{3,2},{4,7},{5,4},{6,5},{7,6},{8,11},{9,8},{10,9... | collective-permute-start | bytes 1966088 | tf_op jit(solution)/shard_map/ppermute | solution.py:23
  77.2 38.0 %collective-permute-start.16 = (bf16[4,2,64,640]{3,2,1,0:T(8,128)(2,1)S(1)}, bf16[4,2,64,640]{3,2,1,0:T(8,128)(2,1)S(1)}, u32[]{:S(2)}, u32[]{:S(2)}) collective-permute-start(bf16[4,2,64,640]{3,2,1,0:T(8,128)(2,1)S(1)} %get-tuple-element.43), channel_id=1, source_target_pairs={{0,4},{4,8},{8,12},{12,0},{1,5},{5,9},{9,13},{13,1},{2,6},{6,10},{... | collective-permute-start | bytes 1966088 | tf_op jit(solution)/shard_map/ppermute | solution.py:23
  79.1 36.1 %collective-permute-start.17 = (bf16[4,2,64,640]{3,2,1,0:T(8,128)(2,1)S(1)}, bf16[4,2,64,640]{3,2,1,0:T(8,128)(2,1)S(1)}, u32[]{:S(2)}, u32[]{:S(2)}) collective-permute-start(bf16[4,2,64,640]{3,2,1,0:T(8,128)(2,1)S(1)} %get-tuple-element.44), channel_id=1, source_target_pairs={{0,8},{4,12},{8,0},{12,4},{1,9},{5,13},{9,1},{13,5},{2,10},{6,14},... | collective-permute-start | bytes 1966088 | tf_op jit(solution)/shard_map/ppermute | solution.py:23
  80.5 34.7 %collective-permute-start.18 = (bf16[4,2,64,640]{3,2,1,0:T(8,128)(2,1)S(1)}, bf16[4,2,64,640]{3,2,1,0:T(8,128)(2,1)S(1)}, u32[]{:S(2)}, u32[]{:S(2)}) collective-permute-start(bf16[4,2,64,640]{3,2,1,0:T(8,128)(2,1)S(1)} %get-tuple-element.45), channel_id=1, source_target_pairs={{0,12},{4,0},{8,4},{12,8},{1,13},{5,1},{9,5},{13,9},{2,14},{6,2},{... | collective-permute-start | bytes 1966088 | tf_op jit(solution)/shard_map/ppermute | solution.py:23
  138.8 3.9 %collective-permute-start.37 = (bf16[4,160,1280]{2,1,0:T(8,128)(2,1)}, bf16[4,160,1280]{2,1,0:T(8,128)(2,1)}, u32[]{:S(2)}, u32[]{:S(2)}) collective-permute-start(bf16[4,160,1280]{2,1,0:T(8,128)(2,1)} %get-tuple-element.77), channel_id=1, source_target_pairs={{0,16},{16,0},{1,17},{17,1},{2,18},{18,2},{3,19},{19,3},{4,20},{20... | collective-permute-start | bytes 4915208 | tf_op jit(solution)/shard_map/ppermute | solution.py:23
  139.0 17.2 %collective-permute-start.25 = (bf16[4,2,64,640]{3,2,1,0:T(8,128)(2,1)S(1)}, bf16[4,2,64,640]{3,2,1,0:T(8,128)(2,1)S(1)}, u32[]{:S(2)}, u32[]{:S(2)}) collective-permute-start(bf16[4,2,64,640]{3,2,1,0:T(8,128)(2,1)S(1)} %get-tuple-element.60), channel_id=1, source_target_pairs={{0,3},{1,0},{2,1},{3,2},{4,7},{5,4},{6,5},{7,6},{8,11},{9,8},{10,9... | collective-permute-start | bytes 1966088 | tf_op jit(solution)/shard_map/ppermute | solution.py:23
  148.3 16.1 %collective-permute-start.40 = (bf16[160,1280]{1,0:T(8,128)(2,1)}, bf16[160,1280]{1,0:T(8,128)(2,1)}, u32[]{:S(2)}, u32[]{:S(2)}) collective-permute-start(bf16[160,1280]{1,0:T(8,128)(2,1)} %get-tuple-element.81), channel_id=1, source_target_pairs={{0,96},{32,0},{64,32},{96,64},{1,97},{33,1},{65,33},{97,65},{2,98}... | collective-permute-start | bytes 1228808 | tf_op jit(solution)/shard_map/ppermute | solution.py:23
  149.2 25.3 %collective-permute-start.39 = (bf16[160,1280]{1,0:T(8,128)(2,1)}, bf16[160,1280]{1,0:T(8,128)(2,1)}, u32[]{:S(2)}, u32[]{:S(2)}) collective-permute-start(bf16[160,1280]{1,0:T(8,128)(2,1)} %get-tuple-element.82), channel_id=1, source_target_pairs={{0,64},{32,96},{64,0},{96,32},{1,65},{33,97},{65,1},{97,33},{2,66}... | collective-permute-start | bytes 1228808 | tf_op jit(solution)/shard_map/ppermute | solution.py:23
  155.9 21.3 %collective-permute-start.38 = (bf16[160,1280]{1,0:T(8,128)(2,1)}, bf16[160,1280]{1,0:T(8,128)(2,1)}, u32[]{:S(2)}, u32[]{:S(2)}) collective-permute-start(bf16[160,1280]{1,0:T(8,128)(2,1)} %get-tuple-element.80), channel_id=1, source_target_pairs={{0,32},{32,64},{64,96},{96,0},{1,33},{33,65},{65,97},{97,1},{2,34}... | collective-permute-start | bytes 1228808 | tf_op jit(solution)/shard_map/ppermute | solution.py:23
  155.9 28.1 %collective-permute-start.26 = (bf16[4,2,64,640]{3,2,1,0:T(8,128)(2,1)}, bf16[4,2,64,640]{3,2,1,0:T(8,128)(2,1)}, u32[]{:S(2)}, u32[]{:S(2)}) collective-permute-start(bf16[4,2,64,640]{3,2,1,0:T(8,128)(2,1)} %get-tuple-element.61), channel_id=1, source_target_pairs={{0,2},{1,3},{2,0},{3,1},{4,6},{5,7},{6,4},{7,5},{8,10},{9,11},{10,... | collective-permute-start | bytes 1966088 | tf_op jit(solution)/shard_map/ppermute | solution.py:23
  156.1 31.8 %collective-permute-start.27 = (bf16[4,2,64,640]{3,2,1,0:T(8,128)(2,1)}, bf16[4,2,64,640]{3,2,1,0:T(8,128)(2,1)}, u32[]{:S(2)}, u32[]{:S(2)}) collective-permute-start(bf16[4,2,64,640]{3,2,1,0:T(8,128)(2,1)} %get-tuple-element.62), channel_id=1, source_target_pairs={{0,1},{1,2},{2,3},{3,0},{4,5},{5,6},{6,7},{7,4},{8,9},{9,10},{10,1... | collective-permute-start | bytes 1966088 | tf_op jit(solution)/shard_map/ppermute | solution.py:23
  164.5 26.2 %collective-permute-start.31 = (bf16[4,2,64,640]{3,2,1,0:T(8,128)(2,1)}, bf16[4,2,64,640]{3,2,1,0:T(8,128)(2,1)S(1)}, u32[]{:S(2)}, u32[]{:S(2)}) collective-permute-start(bf16[4,2,64,640]{3,2,1,0:T(8,128)(2,1)} %copy-done.15), channel_id=1, source_target_pairs={{0,12},{4,0},{8,4},{12,8},{1,13},{5,1},{9,5},{13,9},{2,14},{6,2},{... | collective-permute-start | bytes 1966088 | tf_op jit(solution)/shard_map/ppermute | solution.py:23
  174.4 20.6 %collective-permute-start.32 = (bf16[4,2,64,640]{3,2,1,0:T(8,128)(2,1)}, bf16[4,2,64,640]{3,2,1,0:T(8,128)(2,1)}, u32[]{:S(2)}, u32[]{:S(2)}) collective-permute-start(bf16[4,2,64,640]{3,2,1,0:T(8,128)(2,1)} %copy-done.14), channel_id=1, source_target_pairs={{0,8},{4,12},{8,0},{12,4},{1,9},{5,13},{9,1},{13,5},{2,10},{6,14},... | collective-permute-start | bytes 1966088 | tf_op jit(solution)/shard_map/ppermute | solution.py:23
  177.1 30.9 %collective-permute-start.33 = (bf16[4,2,64,640]{3,2,1,0:T(8,128)(2,1)}, bf16[4,2,64,640]{3,2,1,0:T(8,128)(2,1)}, u32[]{:S(2)}, u32[]{:S(2)}) collective-permute-start(bf16[4,2,64,640]{3,2,1,0:T(8,128)(2,1)} %copy-done.13), channel_id=1, source_target_pairs={{0,4},{4,8},{8,12},{12,0},{1,5},{5,9},{9,13},{13,1},{2,6},{6,10},{... | collective-permute-start | bytes 1966088 | tf_op jit(solution)/shard_map/ppermute | solution.py:23
  184.0 31.7 %collective-permute-start.43 = (bf16[4,10,1280]{2,1,0:T(8,128)(2,1)}, bf16[4,10,1280]{2,1,0:T(8,128)(2,1)}, u32[]{:S(2)}, u32[]{:S(2)}) collective-permute-start(bf16[4,10,1280]{2,1,0:T(8,128)(2,1)} %get-tuple-element.84), channel_id=1, source_target_pairs={{0,12},{4,0},{8,4},{12,8},{1,13},{5,1},{9,5},{13,9},{2,14},{6,2},{... | collective-permute-start | bytes 307208 | tf_op jit(solution)/shard_map/ppermute | solution.py:23
  188.0 27.9 %collective-permute-start.42 = (bf16[4,10,1280]{2,1,0:T(8,128)(2,1)}, bf16[4,10,1280]{2,1,0:T(8,128)(2,1)}, u32[]{:S(2)}, u32[]{:S(2)}) collective-permute-start(bf16[4,10,1280]{2,1,0:T(8,128)(2,1)} %get-tuple-element.85), channel_id=1, source_target_pairs={{0,8},{4,12},{8,0},{12,4},{1,9},{5,13},{9,1},{13,5},{2,10},{6,14},... | collective-permute-start | bytes 307208 | tf_op jit(solution)/shard_map/ppermute | solution.py:23
  190.7 34.8 %collective-permute-start.41 = (bf16[4,10,1280]{2,1,0:T(8,128)(2,1)S(1)}, bf16[4,10,1280]{2,1,0:T(8,128)(2,1)}, u32[]{:S(2)}, u32[]{:S(2)}) collective-permute-start(bf16[4,10,1280]{2,1,0:T(8,128)(2,1)S(1)} %get-tuple-element.83), channel_id=1, source_target_pairs={{0,4},{4,8},{8,12},{12,0},{1,5},{5,9},{9,13},{13,1},{2,6},{6,10},{... | collective-permute-start | bytes 307208 | tf_op jit(solution)/shard_map/ppermute | solution.py:23
  195.0 33.5 %collective-permute-start.28 = (bf16[2,2,64,640]{3,2,1,0:T(8,128)(2,1)S(1)}, bf16[2,2,64,640]{3,2,1,0:T(8,128)(2,1)S(1)}, u32[]{:S(2)}, u32[]{:S(2)}) collective-permute-start(bf16[2,2,64,640]{3,2,1,0:T(8,128)(2,1)S(1)} %get-tuple-element.64), channel_id=1, source_target_pairs={{0,12},{4,0},{8,4},{12,8},{1,13},{5,1},{9,5},{13,9},{2,14},{6,2},{... | collective-permute-start | bytes 983048 | tf_op jit(solution)/shard_map/ppermute | solution.py:23
  208.1 21.9 %collective-permute-start.29 = (bf16[2,2,64,640]{3,2,1,0:T(8,128)(2,1)S(1)}, bf16[2,2,64,640]{3,2,1,0:T(8,128)(2,1)S(1)}, u32[]{:S(2)}, u32[]{:S(2)}) collective-permute-start(bf16[2,2,64,640]{3,2,1,0:T(8,128)(2,1)S(1)} %get-tuple-element.65), channel_id=1, source_target_pairs={{0,8},{4,12},{8,0},{12,4},{1,9},{5,13},{9,1},{13,5},{2,10},{6,14},... | collective-permute-start | bytes 983048 | tf_op jit(solution)/shard_map/ppermute | solution.py:23
  211.1 23.0 %copy-start.18 = (bf16[8,160,1280]{2,1,0:T(8,128)(2,1)S(1)}, bf16[8,160,1280]{2,1,0:T(8,128)(2,1)}, u32[]{:S(2)}) copy-start(bf16[8,160,1280]{2,1,0:T(8,128)(2,1)} %place_weight.1) | copy-start | bytes 9830404
  215.8 16.1 %collective-permute-start.30 = (bf16[2,2,64,640]{3,2,1,0:T(8,128)(2,1)S(1)}, bf16[2,2,64,640]{3,2,1,0:T(8,128)(2,1)S(1)}, u32[]{:S(2)}, u32[]{:S(2)}) collective-permute-start(bf16[2,2,64,640]{3,2,1,0:T(8,128)(2,1)S(1)} %get-tuple-element.66), channel_id=1, source_target_pairs={{0,4},{4,8},{8,12},{12,0},{1,5},{5,9},{9,13},{13,1},{2,6},{6,10},{... | collective-permute-start | bytes 983048 | tf_op jit(solution)/shard_map/ppermute | solution.py:23
  215.8 18.2 %collective-permute-start.34 = (bf16[2,2,64,640]{3,2,1,0:T(8,128)(2,1)S(1)}, bf16[2,2,64,640]{3,2,1,0:T(8,128)(2,1)S(1)}, u32[]{:S(2)}, u32[]{:S(2)}) collective-permute-start(bf16[2,2,64,640]{3,2,1,0:T(8,128)(2,1)S(1)} %get-tuple-element.72), channel_id=1, source_target_pairs={{0,3},{1,0},{2,1},{3,2},{4,7},{5,4},{6,5},{7,6},{8,11},{9,8},{10,9... | collective-permute-start | bytes 983048 | tf_op jit(solution)/shard_map/ppermute | solution.py:23
  225.5 10.5 %collective-permute-start.35 = (bf16[2,2,64,640]{3,2,1,0:T(8,128)(2,1)S(1)}, bf16[2,2,64,640]{3,2,1,0:T(8,128)(2,1)S(1)}, u32[]{:S(2)}, u32[]{:S(2)}) collective-permute-start(bf16[2,2,64,640]{3,2,1,0:T(8,128)(2,1)S(1)} %get-tuple-element.73), channel_id=1, source_target_pairs={{0,2},{1,3},{2,0},{3,1},{4,6},{5,7},{6,4},{7,5},{8,10},{9,11},{10,... | collective-permute-start | bytes 983048 | tf_op jit(solution)/shard_map/ppermute | solution.py:23
  228.5 9.9 %collective-permute-start.36 = (bf16[2,2,64,640]{3,2,1,0:T(8,128)(2,1)S(1)}, bf16[2,2,64,640]{3,2,1,0:T(8,128)(2,1)S(1)}, u32[]{:S(2)}, u32[]{:S(2)}) collective-permute-start(bf16[2,2,64,640]{3,2,1,0:T(8,128)(2,1)S(1)} %get-tuple-element.74), channel_id=1, source_target_pairs={{0,1},{1,2},{2,3},{3,0},{4,5},{5,6},{6,7},{7,4},{8,9},{9,10},{10,1... | collective-permute-start | bytes 983048 | tf_op jit(solution)/shard_map/ppermute | solution.py:23
  230.0 12.5 %collective-permute-start.46 = (bf16[10,1280]{1,0:T(8,128)(2,1)S(1)}, bf16[10,1280]{1,0:T(8,128)(2,1)S(1)}, u32[]{:S(2)}, u32[]{:S(2)}) collective-permute-start(bf16[10,1280]{1,0:T(8,128)(2,1)S(1)} %get-tuple-element.89), channel_id=1, source_target_pairs={{0,3},{1,0},{2,1},{3,2},{4,7},{5,4},{6,5},{7,6},{8,11},{9,8},{10,9... | collective-permute-start | bytes 76808 | tf_op jit(solution)/shard_map/ppermute | solution.py:23
  231.9 10.6 %collective-permute-start.45 = (bf16[10,1280]{1,0:T(8,128)(2,1)S(1)}, bf16[10,1280]{1,0:T(8,128)(2,1)S(1)}, u32[]{:S(2)}, u32[]{:S(2)}) collective-permute-start(bf16[10,1280]{1,0:T(8,128)(2,1)S(1)} %get-tuple-element.90), channel_id=1, source_target_pairs={{0,2},{1,3},{2,0},{3,1},{4,6},{5,7},{6,4},{7,5},{8,10},{9,11},{10,... | collective-permute-start | bytes 76808 | tf_op jit(solution)/shard_map/ppermute | solution.py:23
  234.1 8.4 %collective-permute-start.44 = (bf16[10,1280]{1,0:T(8,128)(2,1)S(1)}, bf16[10,1280]{1,0:T(8,128)(2,1)S(1)}, u32[]{:S(2)}, u32[]{:S(2)}) collective-permute-start(bf16[10,1280]{1,0:T(8,128)(2,1)S(1)} %get-tuple-element.88), channel_id=1, source_target_pairs={{0,1},{1,2},{2,3},{3,0},{4,5},{5,6},{6,7},{7,4},{8,9},{9,10},{10,1... | collective-permute-start | bytes 76808 | tf_op jit(solution)/shard_map/ppermute | solution.py:23
  (26 other events, 107.5 us)

commit v2 on v1

v2 whole, which is shorter than its diff:
```python
import functools

import jax
import jax.numpy as jnp
from jax import lax
from jax.experimental import pallas as pl
from jax.experimental.pallas import tpu as pltpu
from jax.sharding import Mesh
from jax.sharding import PartitionSpec as P

HD = 64
BLK = 64
LANES = 128
LOG2E = 1.4426950408889634
BF = jnp.bfloat16
F32 = jnp.float32
MIB = 1024 * 1024
CHUNKS = ((0, 1280),)
PARTS = (((0, 1280),),)
PLANE = ("core", "x", "y")


def shift(array, axis, amount):
    n = lax.axis_size(axis)
    return lax.ppermute(array, axis, [(i, (i + amount) % n) for i in range(n)])


def move(array, leg, amount):
    pairs = []
    for core in range(2):
        for x in range(4):
            for y in range(4):
                along_x = (leg == 0) == (core == 0)
                to_x, to_y = ((x + amount) % 4, y) if along_x else (x, (y + amount) % 4)
                pairs.append((core * 16 + x * 4 + y, core * 16 + to_x * 4 + to_y))
    return lax.ppermute(array, PLANE, pairs)


def cost(us):
    return pl.CostEstimate(flops=int(us * 1.15e9), bytes_accessed=0, transcendentals=0)


def after(array, *earlier):
    return lax.optimization_barrier((array, earlier))[0]


def nt(a, b):
    return lax.dot_general(a, b, (((1,), (1,)), ((), ())), preferred_element_type=F32)


def mm(a, b):
    return lax.dot_general(a, b, (((1,), (0,)), ((), ())), preferred_element_type=F32)


def select_kernel(table, *refs):
    held, out = refs[:4], refs[4:]
    for j in range(4):
        for k in range(4):
            row = jnp.maximum(table[j * 4 + k], 0)
            out[j][k] = held[k][row]


def select_rows(table, held):
    _, kinds, rows, width = held[0].shape
    block_in = pl.BlockSpec((2, kinds, rows, LANES), lambda i, t: (0, 0, 0, i))
    block_out = pl.BlockSpec((4, kinds, rows, LANES), lambda i, t: (0, 0, 0, i))
    return pl.pallas_call(
        select_kernel,
        grid_spec=pltpu.PrefetchScalarGridSpec(
            num_scalar_prefetch=1,
            grid=(width // LANES,),
            in_specs=[block_in] * 4,
            out_specs=[block_out] * 4,
        ),
        out_shape=[jax.ShapeDtypeStruct((4, kinds, rows, width), BF)] * 4,
        compiler_params=pltpu.CompilerParams(vmem_limit_bytes=12 * MIB),
        cost_estimate=cost(3),
        name="select_rows",
    )(table.reshape(-1), *held)


def fold_kernel(table, *refs):
    parts, out = refs[:4], refs[4:]
    for k in range(4):
        for row in range(2):
            total = None
            for j in range(4):
                keep = jnp.where(table[j * 4 + k] == row, 1.0, 0.0).astype(F32)
                term = parts[j][k].astype(F32) * keep
                total = term if total is None else total + term
            out[k][row] = total.astype(BF)


def fold_rows(table, parts):
    _, kinds, rows, width = parts[0].shape
    block_in = pl.BlockSpec((4, kinds, rows, LANES), lambda i, t: (0, 0, 0, i))
    block_out = pl.BlockSpec((2, kinds, rows, LANES), lambda i, t: (0, 0, 0, i))
    return pl.pallas_call(
        fold_kernel,
        grid_spec=pltpu.PrefetchScalarGridSpec(
            num_scalar_prefetch=1,
            grid=(width // LANES,),
            in_specs=[block_in] * 4,
            out_specs=[block_out] * 4,
        ),
        out_shape=[jax.ShapeDtypeStruct((2, kinds, rows, width), BF)] * 4,
        compiler_params=pltpu.CompilerParams(vmem_limit_bytes=12 * MIB),
        cost_estimate=cost(4.5),
        name="fold_rows",
    )(table.reshape(-1), *parts)


def total_kernel(*refs):
    out = refs[-1]
    step = pl.program_id(0)
    start = 0
    for chunk, (_, width) in enumerate(CHUNKS):
        parts = refs[4 * chunk : 4 * chunk + 4]
        count = width // LANES

        @pl.when((step >= start) & (step < start + count))
        def _():
            total = parts[0][...].astype(F32)
            for part in parts[1:]:
                total = total + part[...].astype(F32)
            out[...] = total

        start += count


def total_rows(parts):
    owned, kinds, rows, _ = parts[0][0].shape
    specs, start = [], 0
    for _, width in CHUNKS:
        count = width // LANES
        spec = pl.BlockSpec(
            (owned, kinds, rows, LANES),
            lambda i, start=start, count=count: (0, 0, 0, jnp.clip(i - start, 0, count - 1)),
        )
        specs += [spec] * 4
        start += count
    width = start * LANES
    return pl.pallas_call(
        total_kernel,
        grid=(start,),
        in_specs=specs,
        out_specs=pl.BlockSpec((owned, kinds, rows, LANES), lambda i: (0, 0, 0, i)),
        out_shape=jax.ShapeDtypeStruct((owned, kinds, rows, width), F32),
        compiler_params=pltpu.CompilerParams(vmem_limit_bytes=12 * MIB),
        cost_estimate=cost(4),
        name="total_rows",
    )(*[part for group in parts for part in group])


def head_front(keys, values, query, grad_t, head):
    lane = lax.broadcasted_iota(jnp.int32, query.shape, 1) // HD
    feature = lax.broadcasted_iota(jnp.int32, grad_t.shape, 0) // HD
    query = jnp.where(lane == head, query, jnp.zeros_like(query))
    grad_t = jnp.where(feature == head, grad_t, jnp.zeros_like(grad_t))
    return query, grad_t, nt(keys, query), mm(values, grad_t)


def head_softmax(scores, grad_probs, valid_frames):
    frames = scores.shape[1]
    key_row = lax.broadcasted_iota(jnp.int32, (frames, frames), 0)
    own = jnp.where(key_row < valid_frames, scores[:frames], -1e30)
    scores = jnp.concatenate([own, scores[frames:]], 0)
    top = jnp.max(scores, axis=0, keepdims=True)
    expo = jnp.exp2((scores - top) * (HD**-0.5 * LOG2E))
    probs = expo * (1.0 / jnp.sum(expo, axis=0, keepdims=True))
    row_dots = jnp.sum(probs * grad_probs, axis=0, keepdims=True)
    return probs.astype(BF), (probs * (grad_probs - row_dots)).astype(BF)


def attend_kernel(meta, q_ref, ko_ref, vo_ref, g_ref, *refs):
    slots = refs[:4]
    attn_t_ref, dq_ref, dk_ref, dv_ref = refs[-12:-8]
    back, (k_all, v_all, dk_all, dv_all) = refs[-8:-4], refs[-4:]
    frames, width = q_ref.shape
    scale = HD**-0.5
    valid_frames = meta[16] * BLK
    k_all[:frames] = ko_ref[...]
    v_all[:frames] = vo_ref[...]

    def rows_of(place):
        return pl.ds(pl.multiple_of(frames + BLK * jnp.maximum(place, 0), BLK), BLK)

    for j in range(4):
        for k in range(4):
            place = meta[4 * j + k]

            @pl.when(place >= 0)
            def _():
                k_all[rows_of(place)] = slots[j][k, 0]
                v_all[rows_of(place)] = slots[j][k, 1]

    for pair in range(width // LANES):
        lanes = slice(pair * LANES, (pair + 1) * LANES)
        keys, values = k_all[:, lanes], v_all[:, lanes]
        keys_t, values_t = keys.T, values.T
        fronts = [head_front(keys, values, q_ref[:, lanes], g_ref[lanes], h) for h in range(2)]
        outs_t, dqs_t, dks, dvs = [], [], [], []
        for h, (query, grad_t, scores, grad_probs) in enumerate(fronts):
            probs, grad_scores = head_softmax(scores, grad_probs, valid_frames)
            mine = slice(h * HD, (h + 1) * HD)
            outs_t.append(mm(values_t[mine], probs))
            dqs_t.append(mm(keys_t[mine], grad_scores))
            dks.append(mm(grad_scores, query))
            dvs.append(nt(probs, grad_t))
        out_t = jnp.concatenate(outs_t, 0)
        column = lax.broadcasted_iota(jnp.int32, out_t.shape, 1)
        attn_t_ref[lanes] = jnp.where(column < valid_frames, out_t, 0.0).astype(BF)
        dq_ref[:, lanes] = (jnp.concatenate(dqs_t, 0) * scale).T.astype(BF)
        grad_key = ((dks[0] + dks[1]) * scale).astype(BF)
        grad_value = (dvs[0] + dvs[1]).astype(BF)
        dk_ref[:, lanes] = grad_key[:frames]
        dv_ref[:, lanes] = grad_value[:frames]
        dk_all[:, lanes] = grad_key[frames:]
        dv_all[:, lanes] = grad_value[frames:]

    for j in range(4):
        for k in range(4):
            place = meta[4 * j + k]
            rows = pl.ds(pl.multiple_of(BLK * jnp.maximum(place, 0), BLK), BLK)

            @pl.when(place >= 0)
            def _():
                back[j][k, 0] = dk_all[rows]
                back[j][k, 1] = dv_all[rows]

            @pl.when(place < 0)
            def _():
                back[j][k] = jnp.zeros(back[j].shape[1:], BF)


def attend(meta, query, own_keys, own_values, grad_attn, slots, entries, chunk, part, kept):
    frames, features = query.shape
    step = 2 * LANES
    first, offset = part[0] // step, (part[0] - chunk[0]) // step
    wide = pl.BlockSpec((frames, step), lambda i, m: (0, first + i))
    tall = pl.BlockSpec((step, frames), lambda i, m: (first + i, 0))
    slot = pl.BlockSpec((4, 2, BLK, step), lambda i, m: (0, 0, 0, offset + i))
    keys, blocks = frames + entries * BLK, entries * BLK
    rows = jax.ShapeDtypeStruct((frames, features), BF)
    return pl.pallas_call(
        attend_kernel,
        grid_spec=pltpu.PrefetchScalarGridSpec(
            num_scalar_prefetch=1,
            grid=(part[1] // step,),
            in_specs=[wide] * 3 + [tall] + [slot] * 4
            + [pl.BlockSpec(memory_space=pl.ANY)] * len(kept),
            out_specs=[tall] + [wide] * 3 + [slot] * 4,
            scratch_shapes=[pltpu.VMEM((keys, step), BF)] * 2
            + [pltpu.VMEM((blocks, step), BF)] * 2,
        ),
        out_shape=[jax.ShapeDtypeStruct((features, frames), BF)]
        + [rows] * 3
        + [jax.ShapeDtypeStruct((4, 2, BLK, chunk[1]), BF)] * 4,
        input_output_aliases={9 + i: i for i in range(len(kept))},
        compiler_params=pltpu.CompilerParams(vmem_limit_bytes=24 * MIB),
        cost_estimate=cost(part[1] // step * 4.6),
        name="attend",
    )(meta, query, own_keys, own_values, grad_attn, *slots, *kept)


def spread_slab(rows, ids):
    size, features = rows.shape
    note = jnp.pad(ids.astype(BF), (0, features - ids.shape[0]))[None]
    slab = jnp.concatenate([rows, note, jnp.zeros((15 - size, features), BF)], 0)
    return jnp.stack([slab] + [move(slab, 1, k) for k in range(1, 4)])


def gather_weight(slabs, size, place, before_z, before_core):
    z, core = lax.axis_index("z"), lax.axis_index("core")
    features = slabs[0].shape[-1]
    row = jnp.arange(16, dtype=jnp.int32)
    target = jnp.where(row < size, place.reshape(16, 1) * size + row, -1).reshape(1, 256)
    pick = (jnp.arange(16 * size, dtype=jnp.int32)[:, None] == target).astype(BF)
    rows = mm(pick, jnp.concatenate(slabs, 0).reshape(256, features)).astype(BF)
    rows = after(rows, *before_z)
    near = [shift(rows, "z", k) for k in (1, 3)]
    pieces = [rows, near[0], shift(after(rows, *near), "z", 2), near[1]]
    far = shift(after(jnp.stack(pieces), *before_core), "core", 1)
    from_z = (z - jnp.arange(4, dtype=jnp.int32)) % 4
    return pieces, far, jnp.concatenate([from_z * 2 + core, from_z * 2 + 1 - core])


def grad_attn_kernel(meta, grad_ref, *refs):
    pieces, out = [*refs[:4], *(refs[4].at[k] for k in range(4))], refs[5]
    size, frames = pieces[0].shape[0], grad_ref.shape[0]
    column = lax.broadcasted_iota(jnp.int32, (size, frames), 1)
    for i, piece in enumerate(pieces):
        part = jnp.where(column < meta[8] * BLK, nt(piece[...], grad_ref[...]), 0.0)
        out[pl.ds(pl.multiple_of(meta[i] * size, 32), size)] = part.astype(BF)


def grad_attn_rows(where, lengths, grad_rows, pieces, far):
    frames, features = grad_rows.shape
    return pl.pallas_call(
        grad_attn_kernel,
        in_specs=[pl.BlockSpec(memory_space=pltpu.SMEM)]
        + [pl.BlockSpec(memory_space=pltpu.VMEM)] * 6,
        out_specs=pl.BlockSpec(memory_space=pltpu.VMEM),
        out_shape=jax.ShapeDtypeStruct((features, frames), BF),
        compiler_params=pltpu.CompilerParams(vmem_limit_bytes=12 * MIB),
        cost_estimate=cost(4),
        name="grad_attn",
    )(jnp.concatenate([where, lengths]), grad_rows, *pieces, far)


def attended_kernel(where, attn_t_ref, *refs):
    pieces, out = [*refs[:4], *(refs[4].at[k] for k in range(4))], refs[5]
    size = pieces[0].shape[0]
    total = None
    for i, piece in enumerate(pieces):
        rows = attn_t_ref[pl.ds(pl.multiple_of(where[i] * size, 32), size)]
        part = mm(rows.T, piece[...])
        total = part if total is None else total + part
    out[...] = total.astype(BF)


def attended_rows(where, attn_t, pieces, far):
    features, frames = attn_t.shape
    wide = 2 * LANES
    size = features // 8
    return pl.pallas_call(
        attended_kernel,
        grid_spec=pltpu.PrefetchScalarGridSpec(
            num_scalar_prefetch=1,
            grid=(features // wide,),
            in_specs=[pl.BlockSpec((features, frames), lambda i, w: (0, 0))]
            + [pl.BlockSpec((size, wide), lambda i, w: (0, i))] * 4
            + [pl.BlockSpec((4, size, wide), lambda i, w: (0, 0, i))],
            out_specs=pl.BlockSpec((frames, wide), lambda i, w: (0, i)),
        ),
        out_shape=jax.ShapeDtypeStruct((frames, features), BF),
        compiler_params=pltpu.CompilerParams(vmem_limit_bytes=12 * MIB),
        cost_estimate=cost(4),
        name="attended",
    )(where, attn_t, *pieces, far)


def grad_weight_kernel(core, attn_t_ref, grad_ref, far_ref, near_ref):
    step = pl.program_id(0)
    part = mm(attn_t_ref[...], grad_ref[...])

    @pl.when(step < 4)
    def _():
        far_ref[0] = part.astype(BF)

    @pl.when(step >= 4)
    def _():
        near_ref[0] = part


def grad_weight_rows(attn_t, grad_rows, before_z, before_x):
    features, frames = attn_t.shape
    size = features // 8
    core, z = lax.axis_index("core"), lax.axis_index("z")
    far, near = pl.pallas_call(
        grad_weight_kernel,
        grid_spec=pltpu.PrefetchScalarGridSpec(
            num_scalar_prefetch=1,
            grid=(8,),
            in_specs=[
                pl.BlockSpec(
                    (size, frames),
                    lambda i, c: (jnp.where(i < 4, 2 * i + 1 - c[0], 2 * (i - 4) + c[0]), 0),
                ),
                pl.BlockSpec((frames, features), lambda i, c: (0, 0)),
            ],
            out_specs=[
                pl.BlockSpec((1, size, features), lambda i, c: (jnp.minimum(i, 3), 0, 0)),
                pl.BlockSpec((1, size, features), lambda i, c: (jnp.maximum(i - 4, 0), 0, 0)),
            ],
        ),
        out_shape=[
            jax.ShapeDtypeStruct((4, size, features), BF),
            jax.ShapeDtypeStruct((4, size, features), F32),
        ],
        compiler_params=pltpu.CompilerParams(vmem_limit_bytes=12 * MIB),
        cost_estimate=cost(5.5),
        name="grad_weight",
    )(core.reshape(1).astype(jnp.int32), attn_t, grad_rows)
    total = near + shift(far, "core", 1).astype(F32)
    total = after(total, *before_z).reshape(4 * size, features)
    for axis in ("z", "x", "y"):
        if axis == "x":
            total = after(total, *before_x)
        me = lax.axis_index(axis)
        rows = total.shape[0] // 4
        mine = lax.dynamic_slice_in_dim(total, me * rows, rows, 0)
        for k in range(1, 4):
            piece = lax.dynamic_slice_in_dim(total, (me + k) % 4 * rows, rows, 0)
            mine = mine + shift(piece.astype(BF), axis, k).astype(F32)
        total = mine
    return total


def body(queries, own_keys, own_values, lengths, history, cache_blocks, out_weight, grad_out):
    owned = cache_blocks.shape[0]
    x, y, core = (lax.axis_index(axis) for axis in ("x", "y", "core"))
    straight = core == 0
    first, second = jnp.where(straight, x, y), jnp.where(straight, y, x)
    steps = jnp.arange(4, dtype=jnp.int32)
    ids = history[0]
    owners = ids // owned
    owner_x, owner_y = owners // 4, owners % 4
    behind_first = (first - jnp.where(straight, owner_x, owner_y)) % 4
    behind_second = (second - jnp.where(straight, owner_y, owner_x)) % 4
    slot = behind_second * 4 + behind_first
    every = jnp.arange(16, dtype=jnp.int32)[:, None]
    rank = jnp.sum((slot[None, :] < every).astype(jnp.int32), axis=1)
    rank = jnp.where(jnp.any(slot[None, :] == every, axis=1), rank, -1)
    meta = jnp.concatenate([rank, lengths]).astype(jnp.int32)

    slab = spread_slab(out_weight, ids)
    note = slab[:, out_weight.shape[0], : ids.shape[0]].astype(jnp.int32)
    asked = jnp.stack([ids] + [note[4 - j] for j in range(1, 4)])
    along_first, along_second = (first - steps) % 4, (second - steps) % 4
    owner = jnp.where(straight, along_first * 4 + second, second * 4 + along_first)
    match = (asked // owned)[:, None, :] == owner[None, :, None]
    table = jnp.max(jnp.where(match, (asked % owned)[:, None, :], -1), axis=2)

    fetched, sends, arrived = [], [], []
    for number, (start, width) in enumerate(CHUNKS):
        part = lax.slice_in_dim(cache_blocks, start, start + width, axis=3)
        if number:
            part = after(part, slab)
        held = [part] + [move(part, 0, k) for k in range(1, 4)]
        arrived += held[1:]
        sent = select_rows(table, held)
        sends.append(sent[0])
        fetched.append([sent[0]] + [move(sent[j], 1, j) for j in range(1, 4)])

    place = jnp.where(
        straight,
        along_first[:, None] * 4 + along_second[None, :],
        along_second[None, :] * 4 + along_first[:, None],
    )
    slab = after(slab, arrived[0], arrived[2])
    slabs = [slab] + [move(slab, 0, k) for k in range(1, 4)]
    pieces, far, where = gather_weight(
        slabs, out_weight.shape[0], place, sends, fetched[0][1:]
    )
    grad_attn = grad_attn_rows(where, lengths, grad_out[0], pieces, far)

    own = (queries[0], own_keys[0], own_values[0])
    results, backs = (), []
    for chunk, parts, slots in zip(CHUNKS, PARTS, fetched):
        back = ()
        for number, part in enumerate(parts):
            if number == len(parts) - 1 and backs:
                grad_attn = after(grad_attn, *backs[-1][1:])
            out = attend(
                meta, *own, grad_attn, slots, ids.shape[0], chunk, part, (*results, *back)
            )
            results, back = out[:4], out[4:]
        backs.append([back[0]] + [move(back[j], 1, -j) for j in range(1, 4)])
    returned = []
    for back in backs:
        sums = fold_rows(table, back)
        returned.append([sums[0]] + [move(sums[k], 0, -k) for k in range(1, 4)])
    attn_t, *grads = results
    grad_cache = total_rows(returned)
    attended = attended_rows(where, attn_t, pieces, far)
    grad_weight = grad_weight_rows(attn_t, grad_out[0], (attended,), (returned[0][0],))
    return (attended[None], *(grad[None] for grad in grads), grad_cache, grad_weight)


def solution(mesh):
    axes = ("z", "core", "x", "y")
    fine = Mesh(mesh.devices.reshape(4, 2, 4, 4), axes)

    def split(rank):
        return P(axes, *([None] * (rank - 1)))

    return jax.shard_map(
        body,
        mesh=fine,
        in_specs=tuple(split(rank) for rank in (3, 3, 3, 1, 2, 4, 2, 3)),
        out_specs=tuple(split(rank) for rank in (3, 3, 3, 3, 4, 2)),
        check_vma=False,
    )
```

time: 244 us -> 184 us (0.75); the launches traced: 243 us -> 181 us
  starting transfers between devices: 76.4 us -> 51 us
  Pallas kernels: 61.4 us -> 43.4 us
  local copies, waits for them, and re-layouts: 27.1 us -> 15.4 us
  other arithmetic: 16.1 us -> 9.16 us
  matrix products: 5.83 us -> 0.27 us
  waiting for transfers between devices: 54.4 us -> 59.8 us
    ppermute x47 -> x14, starting transfers between devices: 76.4 us -> 24.4 us  [shift(): return lax.ppermute(array, axis, [(i, (i + amount) % n) for i in range(n)])]
    ppermute x0 -> x18, waiting for transfers between devices: none -> 41.4 us  [move(): return lax.ppermute(array, PLANE, pairs)]
    ppermute x47 -> x14, waiting for transfers between devices: 54.4 us -> 18.3 us  [shift(): return lax.ppermute(array, axis, [(i, (i + amount) % n) for i in range(n)])]
    ppermute x0 -> x18, starting transfers between devices: none -> 26.6 us  [move(): return lax.ppermute(array, PLANE, pairs)]
    pallas_call x2 -> x1, Pallas kernels: 33.5 us -> 21.4 us  [attend(): pl.pallas_call(attend_kernel, grid_spec=pltpu.PrefetchScalarGridSpec(num_...]
    gather x4 -> x0, local copies, waits for them, and re-layouts: 8.22 us -> none  [the longest x3 5.71 us: gather_weight(): jnp.take(jnp.take(rows, (x - steps) % 4, axis=0), (y - steps) % 4, axis=1)]
    pallas_call x2 -> x1, Pallas kernels: 9.04 us -> 3.98 us  [fold_rows(): pl.pallas_call(fold_kernel, grid_spec=pltpu.PrefetchScalarGridSpec(num_sc...]
    dot_general x1 -> x0, matrix products: 3.97 us -> none  [nt(): lax.dot_general(a, b, (((1,), (1,)), ((), ())), preferred_element_type=F32)]
  transfers between devices with their start and end apart: 47 -> 32, of which waited for: 14 -> 13; matrix products, arithmetic and copies ran while one was open for 14% -> 4% of each run, Pallas kernels for 16% -> 8%
where the time goes in v2:
time: 184 us; the launch traced here: 181 us
  waiting for transfers between devices  59.8 us (32%)
  starting transfers between devices  51 us (28%)
  Pallas kernels  43.4 us (24%)
  local copies, waits for them, and re-layouts  15.4 us (8%)
  other arithmetic  9.16 us (5%)
    ppermute x18, waiting for transfers between devices, move(): return lax.ppermute(array, PLANE, pairs)  41.4 us
    ppermute x18, starting transfers between devices, move(): return lax.ppermute(array, PLANE, pairs)  26.6 us
    ppermute x14, starting transfers between devices, shift(): return lax.ppermute(array, axis, [(i, (i + amount) % n) for i in range(n)])  24.4 us
    pallas_call x1, Pallas kernels, attend(): pl.pallas_call(attend_kernel, grid_spec=pltpu.PrefetchScalarGridSpec(num_...  21.4 us
    ppermute x14, waiting for transfers between devices, shift(): return lax.ppermute(array, axis, [(i, (i + amount) % n) for i in range(n)])  18.3 us
    unnamed x62, local copies, waits for them, and re-layouts  14.1 us
    pallas_call x1, Pallas kernels, grad_weight_rows(): pl.pallas_call(grad_weight_kernel, grid_spec=pltpu.PrefetchScalarGridSpec...  5.01 us
    pallas_call x1, Pallas kernels, attended_rows(): pl.pallas_call(attended_kernel, grid_spec=pltpu.PrefetchScalarGridSpec(nu...  4.2 us
  transfers between devices with their start and end apart: 32, of which 13 were waited for; matrix products, arithmetic and copies ran while one was open for 4% of the time, Pallas kernels for 8%

profile of v2, /device:TPU:32, one launch (start us, length us, event | category | flops | bytes accessed | tf_op | source)
XLA Modules:
  0.0 180.7 jit_solution(1542754597072461029)
XLA Ops:
  2.4 3.0 %collective-permute-start.2 = (bf16[16,1280]{1,0:T(8,128)(2,1)S(1)}, bf16[16,1280]{1,0:T(8,128)(2,1)S(1)}, u32[]{:S(2)}, u32[]{:S(2)}) collective-permute-start(bf16[16,1280]{1,0:T(8,128)(2,1)S(1)} %maximum_maximum_fusion), channel_id=1, source_target_pairs={{0,3},{1,0},{2,1},{3,2},{4,7},{5,4},{6,5},{7,6},{8,11},{9,8},{10,9... | collective-permute-start | bytes 122888 | tf_op jit(solution)/shard_map/ppermute | solution.py:36
  7.0 1.5 collective-permute-start.3
  8.5 1.7 collective-permute-start.4
  11.5 1.9 %collective-permute-start.8 = (bf16[2,2,64,1280]{3,2,1,0:T(8,128)(2,1)}, bf16[2,2,64,1280]{3,2,1,0:T(8,128)(2,1)S(1)}, u32[]{:S(2)}, u32[]{:S(2)}) collective-permute-start(bf16[2,2,64,1280]{3,2,1,0:T(8,128)(2,1)} %refs_0_.1), channel_id=1, source_target_pairs={{0,8},{1,9},{2,10},{3,11},{4,12},{5,13},{6,14},{7,15},{8,0},{9,1},... | collective-permute-start | bytes 1966088 | tf_op jit(solution)/shard_map/ppermute | solution.py:36
  14.4 4.6 %collective-permute-done.3.refs_1_ = bf16[2,2,64,1280]{3,2,1,0:T(8,128)(2,1)S(1)} collective-permute-done((bf16[2,2,64,1280]{3,2,1,0:T(8,128)(2,1)}, bf16[2,2,64,1280]{3,2,1,0:T(8,128)(2,1)S(1)}, u32[]{:S(2)}, u32[]{:S(2)}) %collective-permute-start.3) | collective-permute-done | bytes 655392 | tf_op jit(solution)/shard_map/ppermute | solution.py:36
  19.0 6.7 %collective-permute-done.4.refs_3_ = bf16[2,2,64,1280]{3,2,1,0:T(8,128)(2,1)S(1)} collective-permute-done((bf16[2,2,64,1280]{3,2,1,0:T(8,128)(2,1)}, bf16[2,2,64,1280]{3,2,1,0:T(8,128)(2,1)S(1)}, u32[]{:S(2)}, u32[]{:S(2)}) %collective-permute-start.4) | collective-permute-done | bytes 655392 | tf_op jit(solution)/shard_map/ppermute | solution.py:36
  25.7 3.6 %collective-permute-start.7 = (bf16[4,16,1280]{2,1,0:T(8,128)(2,1)S(1)}, bf16[4,16,1280]{2,1,0:T(8,128)(2,1)S(1)}, u32[]{:S(2)}, u32[]{:S(2)}) collective-permute-start(bf16[4,16,1280]{2,1,0:T(8,128)(2,1)S(1)} %pad_maximum_fusion.2), channel_id=1, source_target_pairs={{0,12},{1,13},{2,14},{3,15},{4,0},{5,1},{6,2},{7,3},{8,4},{9,5},{1... | collective-permute-start | bytes 491528 | tf_op jit(solution)/shard_map/ppermute | solution.py:36
  30.1 1.1 copy-done.19
  31.2 2.6 %select_rows.1 = (bf16[4,2,64,1280]{3,2,1,0:T(8,128)(2,1)S(1)}, bf16[4,2,64,1280]{3,2,1,0:T(8,128)(2,1)S(1)}, bf16[4,2,64,1280]{3,2,1,0:T(8,128)(2,1)S(1)}, bf16[4,2,64,1280]{3,2,1,0:T(8,128)(2,1)S(1)}) custom-call(s32[16]{0:T(128)S(1)} %reshape.347.table, bf16[2,2,64,1280]{3,2,1,0:T(8,128)(2,1)S(1)} %copy-done.19, ...), custom_call_target="tpu_custom_call" | custom-call | flops 3449999872 | tf_op jit(solution)/shard_map/select_rows/pallas_call | solution.py:67
  33.8 1.0 copy-done.25
  34.9 1.9 %collective-permute-start.12 = (bf16[4,2,64,1280]{3,2,1,0:T(8,128)(2,1)S(1)}, bf16[4,2,64,1280]{3,2,1,0:T(8,128)(2,1)S(1)}, u32[]{:S(2)}, u32[]{:S(2)}) collective-permute-start(bf16[4,2,64,1280]{3,2,1,0:T(8,128)(2,1)S(1)} %get-tuple-element.34), channel_id=1, source_target_pairs={{0,1},{1,2},{2,3},{3,0},{4,5},{5,6},{6,7},{7,4},{8,9},{9,10},{10,1... | collective-permute-start | bytes 3932168 | tf_op jit(solution)/shard_map/ppermute | solution.py:36
  36.8 1.8 %collective-permute-start.13 = (bf16[4,2,64,1280]{3,2,1,0:T(8,128)(2,1)S(1)}, bf16[4,2,64,1280]{3,2,1,0:T(8,128)(2,1)S(1)}, u32[]{:S(2)}, u32[]{:S(2)}) collective-permute-start(bf16[4,2,64,1280]{3,2,1,0:T(8,128)(2,1)S(1)} %get-tuple-element.35), channel_id=1, source_target_pairs={{0,2},{1,3},{2,0},{3,1},{4,6},{5,7},{6,4},{7,5},{8,10},{9,11},{10,... | collective-permute-start | bytes 3932168 | tf_op jit(solution)/shard_map/ppermute | solution.py:36
  39.8 2.0 %collective-permute-start.9 = (bf16[160,1280]{1,0:T(8,128)(2,1)S(1)}, bf16[160,1280]{1,0:T(8,128)(2,1)S(1)}, u32[]{:S(2)}, u32[]{:S(2)}) collective-permute-start(bf16[160,1280]{1,0:T(8,128)(2,1)S(1)} %convolution_convert_fusion.refs_0_), channel_id=1, source_target_pairs={{0,32},{32,64},{64,96},{96,0},{1,33},{33,65},{65,97},{97,1},{2,34}... | collective-permute-start | bytes 1228808 | tf_op jit(solution)/shard_map/ppermute | solution.py:25
  41.9 6.0 %collective-permute-done.9.refs_1_ = bf16[160,1280]{1,0:T(8,128)(2,1)S(1)} collective-permute-done((bf16[160,1280]{1,0:T(8,128)(2,1)S(1)}, bf16[160,1280]{1,0:T(8,128)(2,1)S(1)}, u32[]{:S(2)}, u32[]{:S(2)}) %collective-permute-start.9) | collective-permute-done | bytes 409632 | tf_op jit(solution)/shard_map/ppermute | solution.py:25
  47.9 2.1 %collective-permute-done.10.refs_3_ = bf16[160,1280]{1,0:T(8,128)(2,1)S(1)} collective-permute-done((bf16[160,1280]{1,0:T(8,128)(2,1)S(1)}, bf16[160,1280]{1,0:T(8,128)(2,1)S(1)}, u32[]{:S(2)}, u32[]{:S(2)}) %collective-permute-start.10) | collective-permute-done | bytes 409632 | tf_op jit(solution)/shard_map/ppermute | solution.py:25
  50.1 6.5 %collective-permute-start.11 = (bf16[160,1280]{1,0:T(8,128)(2,1)S(1)}, bf16[160,1280]{1,0:T(8,128)(2,1)S(1)}, u32[]{:S(2)}, u32[]{:S(2)}) collective-permute-start(bf16[160,1280]{1,0:T(8,128)(2,1)S(1)} %convolution_convert_fusion.refs_0_), channel_id=1, source_target_pairs={{0,64},{32,96},{64,0},{96,32},{1,65},{33,97},{65,1},{97,33},{2,66}... | collective-permute-start | bytes 1228808 | tf_op jit(solution)/shard_map/ppermute | solution.py:25
  56.6 5.9 %collective-permute-done.11.refs_2_ = bf16[160,1280]{1,0:T(8,128)(2,1)S(1)} collective-permute-done((bf16[160,1280]{1,0:T(8,128)(2,1)S(1)}, bf16[160,1280]{1,0:T(8,128)(2,1)S(1)}, u32[]{:S(2)}, u32[]{:S(2)}) %collective-permute-start.11) | collective-permute-done | bytes 409632 | tf_op jit(solution)/shard_map/ppermute | solution.py:25
  62.5 1.4 pad_maximum_fusion
  63.9 1.1 copy-done.13
  65.0 3.2 %collective-permute-done.13.refs_2_ = bf16[4,2,64,1280]{3,2,1,0:T(8,128)(2,1)S(1)} collective-permute-done((bf16[4,2,64,1280]{3,2,1,0:T(8,128)(2,1)S(1)}, bf16[4,2,64,1280]{3,2,1,0:T(8,128)(2,1)S(1)}, u32[]{:S(2)}, u32[]{:S(2)}) %collective-permute-start.13) | collective-permute-done | bytes 1310752 | tf_op jit(solution)/shard_map/ppermute | solution.py:36
  68.2 1.0 copy-done.15
  69.3 1.1 copy-done.17
  71.4 2.7 %collective-permute-done.15.refs_4_ = bf16[4,160,1280]{2,1,0:T(8,128)(2,1)S(1)} collective-permute-done((bf16[4,160,1280]{2,1,0:T(8,128)(2,1)}, bf16[4,160,1280]{2,1,0:T(8,128)(2,1)S(1)}, u32[]{:S(2)}, u32[]{:S(2)}) %collective-permute-start.15) | collective-permute-done | bytes 1638432 | tf_op jit(solution)/shard_map/ppermute | solution.py:25
  74.1 1.6 copy-done.23
  75.7 2.4 %grad_attn.1.g_ref = bf16[1280,256]{1,0:T(8,128)(2,1)S(1)} custom-call(s32[9]{0:T(128)S(1)} %pad_add_fusion.3.meta, bf16[256,1280]{1,0:T(8,128)(2,1)S(1)} %bitcast.38, bf16[160,1280]{1,0:T(8,128)(2,1)S(1)} %convolution_convert_fusion.refs_0_, bf16[160,1280]{1,0:T(8,128)(2,1)S(1)} %collective-permute-done.9.refs_1_, ...), custom_call_target="tpu_custom_call" | custom-call | flops 4600000000 | tf_op jit(solution)/shard_map/grad_attn/pallas_call | solution.py:299
  78.8 21.4 %attend.1 = (bf16[1280,256]{1,0:T(8,128)(2,1)S(1)}, bf16[256,1280]{1,0:T(8,128)(2,1)}, bf16[256,1280]{1,0:T(8,128)(2,1)}, bf16[256,1280]{1,0:T(8,128)(2,1)}, bf1...) custom-call(s32[17]{0:T(128)S(1)} %pad_add_fusion.2.meta, ...), custom_call_target="tpu_custom_call" | custom-call | flops 26449999872 | tf_op jit(solution)/shard_map/attend/pallas_call | solution.py:245
  100.2 5.0 %grad_weight.1 = (bf16[4,160,1280]{2,1,0:T(8,128)(2,1)}, f32[4,160,1280]{2,1,0:T(8,128)S(1)}) custom-call(s32[1]{0:T(128)} %bitcast.22.core, bf16[1280,256]{1,0:T(8,128)(2,1)S(1)} %get-tuple-element.38.attn_t_ref, bf16[256,1280]{1,0:T(8,128)(2,1)S(1)} %bitcast.39), custom_call_target="tpu_custom_call" | custom-call | flops 6325000192 | tf_op jit(solution)/shard_map/grad_weight/pallas_call | solution.py:360
  105.7 2.0 %collective-permute-start.16 = (bf16[4,2,64,1280]{3,2,1,0:T(8,128)(2,1)}, bf16[4,2,64,1280]{3,2,1,0:T(8,128)(2,1)S(1)}, u32[]{:S(2)}, u32[]{:S(2)}) collective-permute-start(bf16[4,2,64,1280]{3,2,1,0:T(8,128)(2,1)} %copy-done.12), channel_id=1, source_target_pairs={{0,3},{1,0},{2,1},{3,2},{4,7},{5,4},{6,5},{7,6},{8,11},{9,8},{10,9... | collective-permute-start | bytes 3932168 | tf_op jit(solution)/shard_map/ppermute | solution.py:36
  108.8 1.0 copy-done.1
  109.8 1.0 copy-done.3
  112.8 1.4 copy-done.9
  114.3 1.1 copy-done.30
  115.3 4.2 %attended.1 = bf16[256,1280]{1,0:T(8,128)(2,1)} custom-call(s32[8]{0:T(128)S(1)} %pad_add_fusion.1.where, bf16[1280,256]{1,0:T(8,128)(2,1)S(1)} %copy-done.30, bf16[160,1280]{1,0:T(8,128)(2,1)S(1)} %copy-done.1, bf16[160,1280]{1,0:T(8,128)(2,1)S(1)} %copy-done.3, bf16[160,1280]{1,0:T(8,128)(2,1)S(1)} %copy-done.7, bf16[160,1280]{1,0:T(8,128)(2,1)S(1)} %copy-done.5, ...), custom_call_target="tpu_custom_call" | custom-call | flops 4600000000 | tf_op jit(solution)/shard_map/attended/pallas_call | solution.py:326
  119.5 1.8 %convert_add_fusion = f32[4,160,1280]{2,1,0:T(8,128)S(1)} fusion(f32[4,160,1280]{2,1,0:T(8,128)S(1)} %get-tuple-element.50, bf16[4,160,1280]{2,1,0:T(8,128)(2,1)} %collective-permute-done.22), kind=kLoop, calls=%fused_computation | loop fusion | flops 1638400 | bytes 8192000 | tf_op jit(solution)/shard_map/add | solution.py:385
  121.7 3.3 %collective-permute-start.24 = (bf16[160,1280]{1,0:T(8,128)(2,1)S(1)}, bf16[160,1280]{1,0:T(8,128)(2,1)S(1)}, u32[]{:S(2)}, u32[]{:S(2)}) collective-permute-start(bf16[160,1280]{1,0:T(8,128)(2,1)S(1)} %get-tuple-element.56), channel_id=1, source_target_pairs={{0,64},{32,96},{64,0},{96,32},{1,65},{33,97},{65,1},{97,33},{2,66}... | collective-permute-start | bytes 1228808 | tf_op jit(solution)/shard_map/ppermute | solution.py:25
  125.0 12.2 %collective-permute-done.16.refs_1_ = bf16[4,2,64,1280]{3,2,1,0:T(8,128)(2,1)S(1)} collective-permute-done((bf16[4,2,64,1280]{3,2,1,0:T(8,128)(2,1)}, bf16[4,2,64,1280]{3,2,1,0:T(8,128)(2,1)S(1)}, u32[]{:S(2)}, u32[]{:S(2)}) %collective-permute-start.16) | collective-permute-done | bytes 1310752 | tf_op jit(solution)/shard_map/ppermute | solution.py:36
  137.2 1.9 %collective-permute-start.23 = (bf16[160,1280]{1,0:T(8,128)(2,1)S(1)}, bf16[160,1280]{1,0:T(8,128)(2,1)S(1)}, u32[]{:S(2)}, u32[]{:S(2)}) collective-permute-start(bf16[160,1280]{1,0:T(8,128)(2,1)S(1)} %get-tuple-element.54), channel_id=1, source_target_pairs={{0,32},{32,64},{64,96},{96,0},{1,33},{33,65},{65,97},{97,1},{2,34}... | collective-permute-start | bytes 1228808 | tf_op jit(solution)/shard_map/ppermute | solution.py:25
  139.1 1.9 %collective-permute-done.18.refs_3_ = bf16[4,2,64,1280]{3,2,1,0:T(8,128)(2,1)S(1)} collective-permute-done((bf16[4,2,64,1280]{3,2,1,0:T(8,128)(2,1)}, bf16[4,2,64,1280]{3,2,1,0:T(8,128)(2,1)S(1)}, u32[]{:S(2)}, u32[]{:S(2)}) %collective-permute-start.18) | collective-permute-done | bytes 1310752 | tf_op jit(solution)/shard_map/ppermute | solution.py:36
  141.1 4.0 %fold_rows.1 = (bf16[2,2,64,1280]{3,2,1,0:T(8,128)(2,1)S(1)}, bf16[2,2,64,1280]{3,2,1,0:T(8,128)(2,1)S(1)}, bf16[2,2,64,1280]{3,2,1,0:T(8,128)(2,1)S(1)}, bf16[2,2,64,1280]{3,2,1,0:T(8,128)(2,1)S(1)}) custom-call(s32[16]{0:T(128)S(1)} %reshape.347.table, bf16[4,2,64,1280]{3,2,1,0:T(8,128)(2,1)S(1)} %copy-done.28, ...), custom_call_target="tpu_custom_call" | custom-call | flops 5175000064 | tf_op jit(solution)/shard_map/fold_rows/pallas_call | solution.py:98
  146.1 2.4 %collective-permute-start.28 = (bf16[40,1280]{1,0:T(8,128)(2,1)}, bf16[40,1280]{1,0:T(8,128)(2,1)S(1)}, u32[]{:S(2)}, u32[]{:S(2)}) collective-permute-start(bf16[40,1280]{1,0:T(8,128)(2,1)} %get-tuple-element.58), channel_id=1, source_target_pairs={{0,12},{4,0},{8,4},{12,8},{1,13},{5,1},{9,5},{13,9},{2,14},{6,2},{... | collective-permute-start | bytes 307208 | tf_op jit(solution)/shard_map/ppermute | solution.py:25
  148.5 5.6 %collective-permute-start.27 = (bf16[40,1280]{1,0:T(8,128)(2,1)}, bf16[40,1280]{1,0:T(8,128)(2,1)}, u32[]{:S(2)}, u32[]{:S(2)}) collective-permute-start(bf16[40,1280]{1,0:T(8,128)(2,1)} %get-tuple-element.59), channel_id=1, source_target_pairs={{0,8},{4,12},{8,0},{12,4},{1,9},{5,13},{9,1},{13,5},{2,10},{6,14},... | collective-permute-start | bytes 307208 | tf_op jit(solution)/shard_map/ppermute | solution.py:25
  154.1 3.2 %collective-permute-start.19 = (bf16[2,2,64,1280]{3,2,1,0:T(8,128)(2,1)S(1)}, bf16[2,2,64,1280]{3,2,1,0:T(8,128)(2,1)S(1)}, u32[]{:S(2)}, u32[]{:S(2)}) collective-permute-start(bf16[2,2,64,1280]{3,2,1,0:T(8,128)(2,1)S(1)} %get-tuple-element.47), channel_id=1, source_target_pairs={{0,12},{1,13},{2,14},{3,15},{4,0},{5,1},{6,2},{7,3},{8,4},{9,5},{1... | collective-permute-start | bytes 1966088 | tf_op jit(solution)/shard_map/ppermute | solution.py:36
  157.3 1.5 collective-permute-start.21
  158.8 1.5 collective-permute-done.26
  161.3 2.1 %collective-permute-start.31 = (bf16[10,1280]{1,0:T(8,128)(2,1)S(1)}, bf16[10,1280]{1,0:T(8,128)(2,1)S(1)}, u32[]{:S(2)}, u32[]{:S(2)}) collective-permute-start(bf16[10,1280]{1,0:T(8,128)(2,1)S(1)} %get-tuple-element.61), channel_id=1, source_target_pairs={{0,3},{1,0},{2,1},{3,2},{4,7},{5,4},{6,5},{7,6},{8,11},{9,8},{10,9... | collective-permute-start | bytes 76808 | tf_op jit(solution)/shard_map/ppermute | solution.py:25
  163.4 9.1 %collective-permute-done.19.refs_1_ = bf16[2,2,64,1280]{3,2,1,0:T(8,128)(2,1)S(1)} collective-permute-done((bf16[2,2,64,1280]{3,2,1,0:T(8,128)(2,1)S(1)}, bf16[2,2,64,1280]{3,2,1,0:T(8,128)(2,1)S(1)}, u32[]{:S(2)}, u32[]{:S(2)}) %collective-permute-start.19) | collective-permute-done | bytes 655392 | tf_op jit(solution)/shard_map/ppermute | solution.py:36
  172.4 3.7 %collective-permute-done.21.refs_3_ = bf16[2,2,64,1280]{3,2,1,0:T(8,128)(2,1)S(1)} collective-permute-done((bf16[2,2,64,1280]{3,2,1,0:T(8,128)(2,1)S(1)}, bf16[2,2,64,1280]{3,2,1,0:T(8,128)(2,1)S(1)}, u32[]{:S(2)}, u32[]{:S(2)}) %collective-permute-start.21) | collective-permute-done | bytes 655392 | tf_op jit(solution)/shard_map/ppermute | solution.py:36
  176.1 3.8 %total_rows.1 = f32[2,2,64,1280]{3,2,1,0:T(8,128)} custom-call(bf16[2,2,64,1280]{3,2,1,0:T(8,128)(2,1)S(1)} %get-tuple-element.46.refs_0_, bf16[2,2,64,1280]{3,2,1,0:T(8,128)(2,1)S(1)} %collective-permute-done.19.refs_1_, bf16[2,2,64,1280]{3,2,1,0:T(8,128)(2,1)S(1)} %collective-permute-done.20.refs_2_, ...), custom_call_target="tpu_custom_call" | custom-call | flops 4600000000 | tf_op jit(solution)/shard_map/total_rows/pallas_call | solution.py:143
  (123 shorter events, 15.4 us)
Async XLA Ops:
  2.4 9.1 %collective-permute-start.2 = (bf16[16,1280]{1,0:T(8,128)(2,1)S(1)}, bf16[16,1280]{1,0:T(8,128)(2,1)S(1)}, u32[]{:S(2)}, u32[]{:S(2)}) collective-permute-start(bf16[16,1280]{1,0:T(8,128)(2,1)S(1)} %maximum_maximum_fusion), channel_id=1, source_target_pairs={{0,3},{1,0},{2,1},{3,2},{4,7},{5,4},{6,5},{7,6},{8,11},{9,8},{10,9... | collective-permute-start | bytes 122888 | tf_op jit(solution)/shard_map/ppermute | solution.py:36
  5.4 8.0 %collective-permute-start.1 = (bf16[16,1280]{1,0:T(8,128)(2,1)S(1)}, bf16[16,1280]{1,0:T(8,128)(2,1)S(1)}, u32[]{:S(2)}, u32[]{:S(2)}) collective-permute-start(bf16[16,1280]{1,0:T(8,128)(2,1)S(1)} %maximum_maximum_fusion), channel_id=1, source_target_pairs={{0,2},{1,3},{2,0},{3,1},{4,6},{5,7},{6,4},{7,5},{8,10},{9,11},{10,... | collective-permute-start | bytes 122888 | tf_op jit(solution)/shard_map/ppermute | solution.py:36
  6.0 7.4 %collective-permute-start = (bf16[16,1280]{1,0:T(8,128)(2,1)S(1)}, bf16[16,1280]{1,0:T(8,128)(2,1)S(1)}, u32[]{:S(2)}, u32[]{:S(2)}) collective-permute-start(bf16[16,1280]{1,0:T(8,128)(2,1)S(1)} %maximum_maximum_fusion), channel_id=1, source_target_pairs={{0,1},{1,2},{2,3},{3,0},{4,5},{5,6},{6,7},{7,4},{8,9},{9,10},{10,1... | collective-permute-start | bytes 122888 | tf_op jit(solution)/shard_map/ppermute | solution.py:36
  7.0 12.0 %collective-permute-start.3 = (bf16[2,2,64,1280]{3,2,1,0:T(8,128)(2,1)}, bf16[2,2,64,1280]{3,2,1,0:T(8,128)(2,1)S(1)}, u32[]{:S(2)}, u32[]{:S(2)}) collective-permute-start(bf16[2,2,64,1280]{3,2,1,0:T(8,128)(2,1)} %refs_0_.1), channel_id=1, source_target_pairs={{0,4},{1,5},{2,6},{3,7},{4,8},{5,9},{6,10},{7,11},{8,12},{9,13},{1... | collective-permute-start | bytes 1966088 | tf_op jit(solution)/shard_map/ppermute | solution.py:36
  8.5 17.2 %collective-permute-start.4 = (bf16[2,2,64,1280]{3,2,1,0:T(8,128)(2,1)}, bf16[2,2,64,1280]{3,2,1,0:T(8,128)(2,1)S(1)}, u32[]{:S(2)}, u32[]{:S(2)}) collective-permute-start(bf16[2,2,64,1280]{3,2,1,0:T(8,128)(2,1)} %refs_0_.1), channel_id=1, source_target_pairs={{0,12},{1,13},{2,14},{3,15},{4,0},{5,1},{6,2},{7,3},{8,4},{9,5},{1... | collective-permute-start | bytes 1966088 | tf_op jit(solution)/shard_map/ppermute | solution.py:36
  11.5 18.6 %collective-permute-start.8 = (bf16[2,2,64,1280]{3,2,1,0:T(8,128)(2,1)}, bf16[2,2,64,1280]{3,2,1,0:T(8,128)(2,1)S(1)}, u32[]{:S(2)}, u32[]{:S(2)}) collective-permute-start(bf16[2,2,64,1280]{3,2,1,0:T(8,128)(2,1)} %refs_0_.1), channel_id=1, source_target_pairs={{0,8},{1,9},{2,10},{3,11},{4,12},{5,13},{6,14},{7,15},{8,0},{9,1},... | collective-permute-start | bytes 1966088 | tf_op jit(solution)/shard_map/ppermute | solution.py:36
  25.7 12.9 %collective-permute-start.7 = (bf16[4,16,1280]{2,1,0:T(8,128)(2,1)S(1)}, bf16[4,16,1280]{2,1,0:T(8,128)(2,1)S(1)}, u32[]{:S(2)}, u32[]{:S(2)}) collective-permute-start(bf16[4,16,1280]{2,1,0:T(8,128)(2,1)S(1)} %pad_maximum_fusion.2), channel_id=1, source_target_pairs={{0,12},{1,13},{2,14},{3,15},{4,0},{5,1},{6,2},{7,3},{8,4},{9,5},{1... | collective-permute-start | bytes 491528 | tf_op jit(solution)/shard_map/ppermute | solution.py:36
  29.3 10.2 %collective-permute-start.6 = (bf16[4,16,1280]{2,1,0:T(8,128)(2,1)S(1)}, bf16[4,16,1280]{2,1,0:T(8,128)(2,1)S(1)}, u32[]{:S(2)}, u32[]{:S(2)}) collective-permute-start(bf16[4,16,1280]{2,1,0:T(8,128)(2,1)S(1)} %pad_maximum_fusion.2), channel_id=1, source_target_pairs={{0,8},{1,9},{2,10},{3,11},{4,12},{5,13},{6,14},{7,15},{8,0},{9,1},... | collective-permute-start | bytes 491528 | tf_op jit(solution)/shard_map/ppermute | solution.py:36
  29.3 10.2 %collective-permute-start.5 = (bf16[4,16,1280]{2,1,0:T(8,128)(2,1)S(1)}, bf16[4,16,1280]{2,1,0:T(8,128)(2,1)S(1)}, u32[]{:S(2)}, u32[]{:S(2)}) collective-permute-start(bf16[4,16,1280]{2,1,0:T(8,128)(2,1)S(1)} %pad_maximum_fusion.2), channel_id=1, source_target_pairs={{0,4},{1,5},{2,6},{3,7},{4,8},{5,9},{6,10},{7,11},{8,12},{9,13},{1... | collective-permute-start | bytes 491528 | tf_op jit(solution)/shard_map/ppermute | solution.py:36
  34.9 29.1 %collective-permute-start.12 = (bf16[4,2,64,1280]{3,2,1,0:T(8,128)(2,1)S(1)}, bf16[4,2,64,1280]{3,2,1,0:T(8,128)(2,1)S(1)}, u32[]{:S(2)}, u32[]{:S(2)}) collective-permute-start(bf16[4,2,64,1280]{3,2,1,0:T(8,128)(2,1)S(1)} %get-tuple-element.34), channel_id=1, source_target_pairs={{0,1},{1,2},{2,3},{3,0},{4,5},{5,6},{6,7},{7,4},{8,9},{9,10},{10,1... | collective-permute-start | bytes 3932168 | tf_op jit(solution)/shard_map/ppermute | solution.py:36
  36.8 31.5 %collective-permute-start.13 = (bf16[4,2,64,1280]{3,2,1,0:T(8,128)(2,1)S(1)}, bf16[4,2,64,1280]{3,2,1,0:T(8,128)(2,1)S(1)}, u32[]{:S(2)}, u32[]{:S(2)}) collective-permute-start(bf16[4,2,64,1280]{3,2,1,0:T(8,128)(2,1)S(1)} %get-tuple-element.35), channel_id=1, source_target_pairs={{0,2},{1,3},{2,0},{3,1},{4,6},{5,7},{6,4},{7,5},{8,10},{9,11},{10,... | collective-permute-start | bytes 3932168 | tf_op jit(solution)/shard_map/ppermute | solution.py:36
  38.6 30.7 %collective-permute-start.14 = (bf16[4,2,64,1280]{3,2,1,0:T(8,128)(2,1)S(1)}, bf16[4,2,64,1280]{3,2,1,0:T(8,128)(2,1)S(1)}, u32[]{:S(2)}, u32[]{:S(2)}) collective-permute-start(bf16[4,2,64,1280]{3,2,1,0:T(8,128)(2,1)S(1)} %get-tuple-element.36), channel_id=1, source_target_pairs={{0,3},{1,0},{2,1},{3,2},{4,7},{5,4},{6,5},{7,6},{8,11},{9,8},{10,9... | collective-permute-start | bytes 3932168 | tf_op jit(solution)/shard_map/ppermute | solution.py:36
  39.8 34.3 %copy-start = (bf16[160,1280]{1,0:T(8,128)(2,1)}, bf16[160,1280]{1,0:T(8,128)(2,1)S(1)}, u32[]{:S(2)}) copy-start(bf16[160,1280]{1,0:T(8,128)(2,1)S(1)} %convolution_convert_fusion.refs_0_) | copy-start | bytes 1228804
  39.8 8.1 %collective-permute-start.9 = (bf16[160,1280]{1,0:T(8,128)(2,1)S(1)}, bf16[160,1280]{1,0:T(8,128)(2,1)S(1)}, u32[]{:S(2)}, u32[]{:S(2)}) collective-permute-start(bf16[160,1280]{1,0:T(8,128)(2,1)S(1)} %convolution_convert_fusion.refs_0_), channel_id=1, source_target_pairs={{0,32},{32,64},{64,96},{96,0},{1,33},{33,65},{65,97},{97,1},{2,34}... | collective-permute-start | bytes 1228808 | tf_op jit(solution)/shard_map/ppermute | solution.py:25
  41.8 8.2 %collective-permute-start.10 = (bf16[160,1280]{1,0:T(8,128)(2,1)S(1)}, bf16[160,1280]{1,0:T(8,128)(2,1)S(1)}, u32[]{:S(2)}, u32[]{:S(2)}) collective-permute-start(bf16[160,1280]{1,0:T(8,128)(2,1)S(1)} %convolution_convert_fusion.refs_0_), channel_id=1, source_target_pairs={{0,96},{32,0},{64,32},{96,64},{1,97},{33,1},{65,33},{97,65},{2,98}... | collective-permute-start | bytes 1228808 | tf_op jit(solution)/shard_map/ppermute | solution.py:25
  47.9 26.2 %copy-start.2 = (bf16[160,1280]{1,0:T(8,128)(2,1)}, bf16[160,1280]{1,0:T(8,128)(2,1)S(1)}, u32[]{:S(2)}) copy-start(bf16[160,1280]{1,0:T(8,128)(2,1)S(1)} %collective-permute-done.9.refs_1_) | copy-start | bytes 1228804
  50.1 24.0 %copy-start.4 = (bf16[160,1280]{1,0:T(8,128)(2,1)}, bf16[160,1280]{1,0:T(8,128)(2,1)S(1)}, u32[]{:S(2)}) copy-start(bf16[160,1280]{1,0:T(8,128)(2,1)S(1)} %collective-permute-done.10.refs_3_) | copy-start | bytes 1228804
  50.1 12.5 %collective-permute-start.11 = (bf16[160,1280]{1,0:T(8,128)(2,1)S(1)}, bf16[160,1280]{1,0:T(8,128)(2,1)S(1)}, u32[]{:S(2)}, u32[]{:S(2)}) collective-permute-start(bf16[160,1280]{1,0:T(8,128)(2,1)S(1)} %convolution_convert_fusion.refs_0_), channel_id=1, source_target_pairs={{0,64},{32,96},{64,0},{96,32},{1,65},{33,97},{65,1},{97,33},{2,66}... | collective-permute-start | bytes 1228808 | tf_op jit(solution)/shard_map/ppermute | solution.py:25
  62.5 11.6 %copy-start.6 = (bf16[160,1280]{1,0:T(8,128)(2,1)}, bf16[160,1280]{1,0:T(8,128)(2,1)S(1)}, u32[]{:S(2)}) copy-start(bf16[160,1280]{1,0:T(8,128)(2,1)S(1)} %collective-permute-done.11.refs_2_) | copy-start | bytes 1228804
  70.4 3.7 %collective-permute-start.15 = (bf16[4,160,1280]{2,1,0:T(8,128)(2,1)}, bf16[4,160,1280]{2,1,0:T(8,128)(2,1)S(1)}, u32[]{:S(2)}, u32[]{:S(2)}) collective-permute-start(bf16[4,160,1280]{2,1,0:T(8,128)(2,1)} %pad_maximum_fusion), channel_id=1, source_target_pairs={{0,16},{16,0},{1,17},{17,1},{2,18},{18,2},{3,19},{19,3},{4,20},{20... | collective-permute-start | bytes 4915208 | tf_op jit(solution)/shard_map/ppermute | solution.py:25
  74.1 4.1 %copy-start.8 = (bf16[4,160,1280]{2,1,0:T(8,128)(2,1)}, bf16[4,160,1280]{2,1,0:T(8,128)(2,1)S(1)}, u32[]{:S(2)}) copy-start(bf16[4,160,1280]{2,1,0:T(8,128)(2,1)S(1)} %collective-permute-done.15.refs_4_) | copy-start | bytes 4915204
  75.7 2.5 %copy-start.20 = (bf16[1,256,1280]{2,1,0:T(8,128)(2,1)S(1)}, bf16[1,256,1280]{2,1,0:T(8,128)(2,1)}, u32[]{:S(2)}) copy-start(bf16[1,256,1280]{2,1,0:T(8,128)(2,1)} %param.8) | copy-start | bytes 1966084
  75.7 2.5 %copy-start.21 = (bf16[1,256,1280]{2,1,0:T(8,128)(2,1)S(1)}, bf16[1,256,1280]{2,1,0:T(8,128)(2,1)}, u32[]{:S(2)}) copy-start(bf16[1,256,1280]{2,1,0:T(8,128)(2,1)} %param.9) | copy-start | bytes 1966084
  75.7 2.6 %copy-start.22 = (bf16[1,256,1280]{2,1,0:T(8,128)(2,1)S(1)}, bf16[1,256,1280]{2,1,0:T(8,128)(2,1)}, u32[]{:S(2)}) copy-start(bf16[1,256,1280]{2,1,0:T(8,128)(2,1)} %param.10) | copy-start | bytes 1966084
  75.7 3.1 %copy-start.26 = (bf16[4,2,64,1280]{3,2,1,0:T(8,128)(2,1)S(1)}, bf16[4,2,64,1280]{3,2,1,0:T(8,128)(2,1)}, u32[]{:S(2)}) copy-start(bf16[4,2,64,1280]{3,2,1,0:T(8,128)(2,1)} %copy-done.25) | copy-start | bytes 3932164
  78.8 21.4 %copy-start.24 = (bf16[1,256,1280]{2,1,0:T(8,128)(2,1)S(1)}, bf16[1,256,1280]{2,1,0:T(8,128)(2,1)}, u32[]{:S(2)}) copy-start(bf16[1,256,1280]{2,1,0:T(8,128)(2,1)} %param.15) | copy-start | bytes 1966084
  100.1 5.1 %copy-start.10 = (bf16[4,2,64,1280]{3,2,1,0:T(8,128)(2,1)}, bf16[4,2,64,1280]{3,2,1,0:T(8,128)(2,1)S(1)}, u32[]{:S(2)}) copy-start(bf16[4,2,64,1280]{3,2,1,0:T(8,128)(2,1)S(1)} %get-tuple-element.45) | copy-start | bytes 3932164
  100.1 5.1 %copy-start.11 = (bf16[4,2,64,1280]{3,2,1,0:T(8,128)(2,1)}, bf16[4,2,64,1280]{3,2,1,0:T(8,128)(2,1)S(1)}, u32[]{:S(2)}) copy-start(bf16[4,2,64,1280]{3,2,1,0:T(8,128)(2,1)S(1)} %get-tuple-element.44) | copy-start | bytes 3932164
  100.1 5.1 %copy-start.12 = (bf16[4,2,64,1280]{3,2,1,0:T(8,128)(2,1)}, bf16[4,2,64,1280]{3,2,1,0:T(8,128)(2,1)S(1)}, u32[]{:S(2)}) copy-start(bf16[4,2,64,1280]{3,2,1,0:T(8,128)(2,1)S(1)} %get-tuple-element.43) | copy-start | bytes 3932164
  100.2 5.1 %copy-start.27 = (bf16[4,2,64,1280]{3,2,1,0:T(8,128)(2,1)}, bf16[4,2,64,1280]{3,2,1,0:T(8,128)(2,1)S(1)}, u32[]{:S(2)}) copy-start(bf16[4,2,64,1280]{3,2,1,0:T(8,128)(2,1)S(1)} %get-tuple-element.42.refs_0_) | copy-start | bytes 3932164
  100.2 5.1 %copy-start.29 = (bf16[1280,256]{1,0:T(8,128)(2,1)}, bf16[1280,256]{1,0:T(8,128)(2,1)S(1)}, u32[]{:S(2)}) copy-start(bf16[1280,256]{1,0:T(8,128)(2,1)S(1)} %get-tuple-element.38.attn_t_ref) | copy-start | bytes 1966084
  105.2 14.3 %collective-permute-start.22 = (bf16[4,160,1280]{2,1,0:T(8,128)(2,1)}, bf16[4,160,1280]{2,1,0:T(8,128)(2,1)}, u32[]{:S(2)}, u32[]{:S(2)}) collective-permute-start(bf16[4,160,1280]{2,1,0:T(8,128)(2,1)} %get-tuple-element.51), channel_id=1, source_target_pairs={{0,16},{16,0},{1,17},{17,1},{2,18},{18,2},{3,19},{19,3},{4,20},{20... | collective-permute-start | bytes 4915208 | tf_op jit(solution)/shard_map/ppermute | solution.py:25
  105.7 31.5 %collective-permute-start.16 = (bf16[4,2,64,1280]{3,2,1,0:T(8,128)(2,1)}, bf16[4,2,64,1280]{3,2,1,0:T(8,128)(2,1)S(1)}, u32[]{:S(2)}, u32[]{:S(2)}) collective-permute-start(bf16[4,2,64,1280]{3,2,1,0:T(8,128)(2,1)} %copy-done.12), channel_id=1, source_target_pairs={{0,3},{1,0},{2,1},{3,2},{4,7},{5,4},{6,5},{7,6},{8,11},{9,8},{10,9... | collective-permute-start | bytes 3932168 | tf_op jit(solution)/shard_map/ppermute | solution.py:36
  107.7 31.4 %collective-permute-start.17 = (bf16[4,2,64,1280]{3,2,1,0:T(8,128)(2,1)}, bf16[4,2,64,1280]{3,2,1,0:T(8,128)(2,1)S(1)}, u32[]{:S(2)}, u32[]{:S(2)}) collective-permute-start(bf16[4,2,64,1280]{3,2,1,0:T(8,128)(2,1)} %copy-done.11), channel_id=1, source_target_pairs={{0,2},{1,3},{2,0},{3,1},{4,6},{5,7},{6,4},{7,5},{8,10},{9,11},{10,... | collective-permute-start | bytes 3932168 | tf_op jit(solution)/shard_map/ppermute | solution.py:36
  108.4 32.6 %collective-permute-start.18 = (bf16[4,2,64,1280]{3,2,1,0:T(8,128)(2,1)}, bf16[4,2,64,1280]{3,2,1,0:T(8,128)(2,1)S(1)}, u32[]{:S(2)}, u32[]{:S(2)}) collective-permute-start(bf16[4,2,64,1280]{3,2,1,0:T(8,128)(2,1)} %copy-done.10), channel_id=1, source_target_pairs={{0,1},{1,2},{2,3},{3,0},{4,5},{5,6},{6,7},{7,4},{8,9},{9,10},{10,1... | collective-permute-start | bytes 3932168 | tf_op jit(solution)/shard_map/ppermute | solution.py:36
  121.4 19.7 %copy-start.28 = (bf16[4,2,64,1280]{3,2,1,0:T(8,128)(2,1)S(1)}, bf16[4,2,64,1280]{3,2,1,0:T(8,128)(2,1)}, u32[]{:S(2)}) copy-start(bf16[4,2,64,1280]{3,2,1,0:T(8,128)(2,1)} %copy-done.27) | copy-start | bytes 3932164
  121.5 23.5 %collective-permute-start.25 = (bf16[160,1280]{1,0:T(8,128)(2,1)S(1)}, bf16[160,1280]{1,0:T(8,128)(2,1)S(1)}, u32[]{:S(2)}, u32[]{:S(2)}) collective-permute-start(bf16[160,1280]{1,0:T(8,128)(2,1)S(1)} %get-tuple-element.55), channel_id=1, source_target_pairs={{0,96},{32,0},{64,32},{96,64},{1,97},{33,1},{65,33},{97,65},{2,98}... | collective-permute-start | bytes 1228808 | tf_op jit(solution)/shard_map/ppermute | solution.py:25
  121.7 23.4 %collective-permute-start.24 = (bf16[160,1280]{1,0:T(8,128)(2,1)S(1)}, bf16[160,1280]{1,0:T(8,128)(2,1)S(1)}, u32[]{:S(2)}, u32[]{:S(2)}) collective-permute-start(bf16[160,1280]{1,0:T(8,128)(2,1)S(1)} %get-tuple-element.56), channel_id=1, source_target_pairs={{0,64},{32,96},{64,0},{96,32},{1,65},{33,97},{65,1},{97,33},{2,66}... | collective-permute-start | bytes 1228808 | tf_op jit(solution)/shard_map/ppermute | solution.py:25
  137.2 8.0 %collective-permute-start.23 = (bf16[160,1280]{1,0:T(8,128)(2,1)S(1)}, bf16[160,1280]{1,0:T(8,128)(2,1)S(1)}, u32[]{:S(2)}, u32[]{:S(2)}) collective-permute-start(bf16[160,1280]{1,0:T(8,128)(2,1)S(1)} %get-tuple-element.54), channel_id=1, source_target_pairs={{0,32},{32,64},{64,96},{96,0},{1,33},{33,65},{65,97},{97,1},{2,34}... | collective-permute-start | bytes 1228808 | tf_op jit(solution)/shard_map/ppermute | solution.py:25
  146.1 11.2 %collective-permute-start.28 = (bf16[40,1280]{1,0:T(8,128)(2,1)}, bf16[40,1280]{1,0:T(8,128)(2,1)S(1)}, u32[]{:S(2)}, u32[]{:S(2)}) collective-permute-start(bf16[40,1280]{1,0:T(8,128)(2,1)} %get-tuple-element.58), channel_id=1, source_target_pairs={{0,12},{4,0},{8,4},{12,8},{1,13},{5,1},{9,5},{13,9},{2,14},{6,2},{... | collective-permute-start | bytes 307208 | tf_op jit(solution)/shard_map/ppermute | solution.py:25
  148.5 10.3 %collective-permute-start.27 = (bf16[40,1280]{1,0:T(8,128)(2,1)}, bf16[40,1280]{1,0:T(8,128)(2,1)}, u32[]{:S(2)}, u32[]{:S(2)}) collective-permute-start(bf16[40,1280]{1,0:T(8,128)(2,1)} %get-tuple-element.59), channel_id=1, source_target_pairs={{0,8},{4,12},{8,0},{12,4},{1,9},{5,13},{9,1},{13,5},{2,10},{6,14},... | collective-permute-start | bytes 307208 | tf_op jit(solution)/shard_map/ppermute | solution.py:25
  154.1 6.2 %collective-permute-start.26 = (bf16[40,1280]{1,0:T(8,128)(2,1)}, bf16[40,1280]{1,0:T(8,128)(2,1)}, u32[]{:S(2)}, u32[]{:S(2)}) collective-permute-start(bf16[40,1280]{1,0:T(8,128)(2,1)} %get-tuple-element.57), channel_id=1, source_target_pairs={{0,4},{4,8},{8,12},{12,0},{1,5},{5,9},{9,13},{13,1},{2,6},{6,10},{... | collective-permute-start | bytes 307208 | tf_op jit(solution)/shard_map/ppermute | solution.py:25
  154.1 18.4 %collective-permute-start.19 = (bf16[2,2,64,1280]{3,2,1,0:T(8,128)(2,1)S(1)}, bf16[2,2,64,1280]{3,2,1,0:T(8,128)(2,1)S(1)}, u32[]{:S(2)}, u32[]{:S(2)}) collective-permute-start(bf16[2,2,64,1280]{3,2,1,0:T(8,128)(2,1)S(1)} %get-tuple-element.47), channel_id=1, source_target_pairs={{0,12},{1,13},{2,14},{3,15},{4,0},{5,1},{6,2},{7,3},{8,4},{9,5},{1... | collective-permute-start | bytes 1966088 | tf_op jit(solution)/shard_map/ppermute | solution.py:36
  157.3 15.1 %collective-permute-start.20 = (bf16[2,2,64,1280]{3,2,1,0:T(8,128)(2,1)S(1)}, bf16[2,2,64,1280]{3,2,1,0:T(8,128)(2,1)S(1)}, u32[]{:S(2)}, u32[]{:S(2)}) collective-permute-start(bf16[2,2,64,1280]{3,2,1,0:T(8,128)(2,1)S(1)} %get-tuple-element.48), channel_id=1, source_target_pairs={{0,8},{1,9},{2,10},{3,11},{4,12},{5,13},{6,14},{7,15},{8,0},{9,1},... | collective-permute-start | bytes 1966088 | tf_op jit(solution)/shard_map/ppermute | solution.py:36
  157.3 18.8 %collective-permute-start.21 = (bf16[2,2,64,1280]{3,2,1,0:T(8,128)(2,1)S(1)}, bf16[2,2,64,1280]{3,2,1,0:T(8,128)(2,1)S(1)}, u32[]{:S(2)}, u32[]{:S(2)}) collective-permute-start(bf16[2,2,64,1280]{3,2,1,0:T(8,128)(2,1)S(1)} %get-tuple-element.49), channel_id=1, source_target_pairs={{0,4},{1,5},{2,6},{3,7},{4,8},{5,9},{6,10},{7,11},{8,12},{9,13},{1... | collective-permute-start | bytes 1966088 | tf_op jit(solution)/shard_map/ppermute | solution.py:36
  161.3 18.7 %collective-permute-start.31 = (bf16[10,1280]{1,0:T(8,128)(2,1)S(1)}, bf16[10,1280]{1,0:T(8,128)(2,1)S(1)}, u32[]{:S(2)}, u32[]{:S(2)}) collective-permute-start(bf16[10,1280]{1,0:T(8,128)(2,1)S(1)} %get-tuple-element.61), channel_id=1, source_target_pairs={{0,3},{1,0},{2,1},{3,2},{4,7},{5,4},{6,5},{7,6},{8,11},{9,8},{10,9... | collective-permute-start | bytes 76808 | tf_op jit(solution)/shard_map/ppermute | solution.py:25
  163.4 16.6 %collective-permute-start.30 = (bf16[10,1280]{1,0:T(8,128)(2,1)S(1)}, bf16[10,1280]{1,0:T(8,128)(2,1)S(1)}, u32[]{:S(2)}, u32[]{:S(2)}) collective-permute-start(bf16[10,1280]{1,0:T(8,128)(2,1)S(1)} %get-tuple-element.62), channel_id=1, source_target_pairs={{0,2},{1,3},{2,0},{3,1},{4,6},{5,7},{6,4},{7,5},{8,10},{9,11},{10,... | collective-permute-start | bytes 76808 | tf_op jit(solution)/shard_map/ppermute | solution.py:25
  172.4 7.5 %collective-permute-start.29 = (bf16[10,1280]{1,0:T(8,128)(2,1)S(1)}, bf16[10,1280]{1,0:T(8,128)(2,1)S(1)}, u32[]{:S(2)}, u32[]{:S(2)}) collective-permute-start(bf16[10,1280]{1,0:T(8,128)(2,1)S(1)} %get-tuple-element.60), channel_id=1, source_target_pairs={{0,1},{1,2},{2,3},{3,0},{4,5},{5,6},{6,7},{7,4},{8,9},{9,10},{10,1... | collective-permute-start | bytes 76808 | tf_op jit(solution)/shard_map/ppermute | solution.py:25
  (15 other events, 20.9 us)

commit v3 on v2

--- a/solution.py
+++ b/solution.py
@@ -15,8 +15,8 @@
 BF = jnp.bfloat16
 F32 = jnp.float32
 MIB = 1024 * 1024
-CHUNKS = ((0, 1280),)
-PARTS = (((0, 1280),),)
+PARTS = ((0, 512), (512, 768))
+STEP = 2 * LANES
 PLANE = ("core", "x", "y")
 
 
@@ -62,13 +62,13 @@
 
 def select_rows(table, held):
     _, kinds, rows, width = held[0].shape
-    block_in = pl.BlockSpec((2, kinds, rows, LANES), lambda i, t: (0, 0, 0, i))
-    block_out = pl.BlockSpec((4, kinds, rows, LANES), lambda i, t: (0, 0, 0, i))
+    block_in = pl.BlockSpec((2, kinds, rows, STEP), lambda i, t: (0, 0, 0, i))
+    block_out = pl.BlockSpec((4, kinds, rows, STEP), lambda i, t: (0, 0, 0, i))
     return pl.pallas_call(
         select_kernel,
         grid_spec=pltpu.PrefetchScalarGridSpec(
             num_scalar_prefetch=1,
-            grid=(width // LANES,),
+            grid=(width // STEP,),
             in_specs=[block_in] * 4,
             out_specs=[block_out] * 4,
         ),
@@ -80,76 +80,70 @@
 
 
 def fold_kernel(table, *refs):
-    parts, out = refs[:4], refs[4:]
-    for k in range(4):
-        for row in range(2):
-            total = None
-            for j in range(4):
-                keep = jnp.where(table[j * 4 + k] == row, 1.0, 0.0).astype(F32)
-                term = parts[j][k].astype(F32) * keep
-                total = term if total is None else total + term
-            out[k][row] = total.astype(BF)
-
-
-def fold_rows(table, parts):
-    _, kinds, rows, width = parts[0].shape
-    block_in = pl.BlockSpec((4, kinds, rows, LANES), lambda i, t: (0, 0, 0, i))
-    block_out = pl.BlockSpec((2, kinds, rows, LANES), lambda i, t: (0, 0, 0, i))
+    out = refs[-4:]
+    step = pl.program_id(0)
+    for number, (start, width) in enumerate(PARTS):
+        parts = refs[4 * number : 4 * number + 4]
+
+        @pl.when((step >= start // STEP) & (step < (start + width) // STEP))
+        def _():
+            for k in range(4):
+                for row in range(2):
+                    total = None
+                    for j in range(4):
+                        keep = jnp.where(table[j * 4 + k] == row, 1.0, 0.0).astype(F32)
+                        term = parts[j][k].astype(F32) * keep
+                        total = term if total is None else total + term
+                    out[k][row] = total.astype(BF)
+
+
+def fold_rows(table, backs):
+    _, kinds, rows, _ = backs[0][0].shape
+    columns = sum(width for _, width in PARTS)
+    blocks = []
+    for start, width in PARTS:
+        first, last = start // STEP, width // STEP - 1
+        blocks += [
+            pl.BlockSpec(
+                (4, kinds, rows, STEP),
+                lambda i, t, first=first, last=last: (0, 0, 0, jnp.clip(i - first, 0, last)),
+            )
+        ] * 4
     return pl.pallas_call(
         fold_kernel,
         grid_spec=pltpu.PrefetchScalarGridSpec(
             num_scalar_prefetch=1,
-            grid=(width // LANES,),
-            in_specs=[block_in] * 4,
-            out_specs=[block_out] * 4,
+            grid=(columns // STEP,),
+            in_specs=blocks,
+            out_specs=[pl.BlockSpec((2, kinds, rows, STEP), lambda i, t: (0, 0, 0, i))] * 4,
         ),
-        out_shape=[jax.ShapeDtypeStruct((2, kinds, rows, width), BF)] * 4,
-        compiler_params=pltpu.CompilerParams(vmem_limit_bytes=12 * MIB),
-        cost_estimate=cost(4.5),
+        out_shape=[jax.ShapeDtypeStruct((2, kinds, rows, columns), BF)] * 4,
+        compiler_params=pltpu.CompilerParams(vmem_limit_bytes=16 * MIB),
+        cost_estimate=cost(4),
         name="fold_rows",
-    )(table.reshape(-1), *parts)
+    )(table.reshape(-1), *backs[0], *backs[1])
 
 
 def total_kernel(*refs):
-    out = refs[-1]
-    step = pl.program_id(0)
-    start = 0
-    for chunk, (_, width) in enumerate(CHUNKS):
-        parts = refs[4 * chunk : 4 * chunk + 4]
-        count = width // LANES
-
-        @pl.when((step >= start) & (step < start + count))
-        def _():
-            total = parts[0][...].astype(F32)
-            for part in parts[1:]:
-                total = total + part[...].astype(F32)
-            out[...] = total
-
-        start += count
+    total = refs[0][...].astype(F32)
+    for part in refs[1:-1]:
+        total = total + part[...].astype(F32)
+    refs[-1][...] = total
 
 
 def total_rows(parts):
-    owned, kinds, rows, _ = parts[0][0].shape
-    specs, start = [], 0
-    for _, width in CHUNKS:
-        count = width // LANES
-        spec = pl.BlockSpec(
-            (owned, kinds, rows, LANES),
-            lambda i, start=start, count=count: (0, 0, 0, jnp.clip(i - start, 0, count - 1)),
-        )
-        specs += [spec] * 4
-        start += count
-    width = start * LANES
+    owned, kinds, rows, width = parts[0].shape
+    block = pl.BlockSpec((owned, kinds, rows, STEP), lambda i: (0, 0, 0, i))
     return pl.pallas_call(
         total_kernel,
-        grid=(start,),
-        in_specs=specs,
-        out_specs=pl.BlockSpec((owned, kinds, rows, LANES), lambda i: (0, 0, 0, i)),
+        grid=(width // STEP,),
+        in_specs=[block] * 4,
+        out_specs=block,
         out_shape=jax.ShapeDtypeStruct((owned, kinds, rows, width), F32),
         compiler_params=pltpu.CompilerParams(vmem_limit_bytes=12 * MIB),
         cost_estimate=cost(4),
         name="total_rows",
-    )(*[part for group in parts for part in group])
+    )(*parts)
 
 
 def head_front(keys, values, query, grad_t, head):
@@ -233,32 +227,32 @@
                 back[j][k] = jnp.zeros(back[j].shape[1:], BF)
 
 
-def attend(meta, query, own_keys, own_values, grad_attn, slots, entries, chunk, part, kept):
+def attend(meta, query, own_keys, own_values, grad_attn, slots, entries, part, kept):
     frames, features = query.shape
-    step = 2 * LANES
-    first, offset = part[0] // step, (part[0] - chunk[0]) // step
-    wide = pl.BlockSpec((frames, step), lambda i, m: (0, first + i))
-    tall = pl.BlockSpec((step, frames), lambda i, m: (first + i, 0))
-    slot = pl.BlockSpec((4, 2, BLK, step), lambda i, m: (0, 0, 0, offset + i))
+    first = part[0] // STEP
+    wide = pl.BlockSpec((frames, STEP), lambda i, m: (0, first + i))
+    tall = pl.BlockSpec((STEP, frames), lambda i, m: (first + i, 0))
+    slot = pl.BlockSpec((4, 2, BLK, STEP), lambda i, m: (0, 0, 0, first + i))
+    back = pl.BlockSpec((4, 2, BLK, STEP), lambda i, m: (0, 0, 0, i))
     keys, blocks = frames + entries * BLK, entries * BLK
     rows = jax.ShapeDtypeStruct((frames, features), BF)
     return pl.pallas_call(
         attend_kernel,
         grid_spec=pltpu.PrefetchScalarGridSpec(
             num_scalar_prefetch=1,
-            grid=(part[1] // step,),
+            grid=(part[1] // STEP,),
             in_specs=[wide] * 3 + [tall] + [slot] * 4
             + [pl.BlockSpec(memory_space=pl.ANY)] * len(kept),
-            out_specs=[tall] + [wide] * 3 + [slot] * 4,
-            scratch_shapes=[pltpu.VMEM((keys, step), BF)] * 2
-            + [pltpu.VMEM((blocks, step), BF)] * 2,
+            out_specs=[tall] + [wide] * 3 + [back] * 4,
+            scratch_shapes=[pltpu.VMEM((keys, STEP), BF)] * 2
+            + [pltpu.VMEM((blocks, STEP), BF)] * 2,
         ),
         out_shape=[jax.ShapeDtypeStruct((features, frames), BF)]
         + [rows] * 3
-        + [jax.ShapeDtypeStruct((4, 2, BLK, chunk[1]), BF)] * 4,
+        + [jax.ShapeDtypeStruct((4, 2, BLK, part[1]), BF)] * 4,
         input_output_aliases={9 + i: i for i in range(len(kept))},
         compiler_params=pltpu.CompilerParams(vmem_limit_bytes=24 * MIB),
-        cost_estimate=cost(part[1] // step * 4.6),
+        cost_estimate=cost(part[1] // STEP * 4.6),
         name="attend",
     )(meta, query, own_keys, own_values, grad_attn, *slots, *kept)
 
@@ -278,15 +272,14 @@
     pick = (jnp.arange(16 * size, dtype=jnp.int32)[:, None] == target).astype(BF)
     rows = mm(pick, jnp.concatenate(slabs, 0).reshape(256, features)).astype(BF)
     rows = after(rows, *before_z)
-    near = [shift(rows, "z", k) for k in (1, 3)]
-    pieces = [rows, near[0], shift(after(rows, *near), "z", 2), near[1]]
-    far = shift(after(jnp.stack(pieces), *before_core), "core", 1)
+    pieces = [rows] + [shift(rows, "z", k) for k in range(1, 4)]
+    far = [shift(piece, "core", 1) for piece in pieces]
     from_z = (z - jnp.arange(4, dtype=jnp.int32)) % 4
     return pieces, far, jnp.concatenate([from_z * 2 + core, from_z * 2 + 1 - core])
 
 
 def grad_attn_kernel(meta, grad_ref, *refs):
-    pieces, out = [*refs[:4], *(refs[4].at[k] for k in range(4))], refs[5]
+    pieces, out = refs[:8], refs[8]
     size, frames = pieces[0].shape[0], grad_ref.shape[0]
     column = lax.broadcasted_iota(jnp.int32, (size, frames), 1)
     for i, piece in enumerate(pieces):
@@ -299,17 +292,17 @@
     return pl.pallas_call(
         grad_attn_kernel,
         in_specs=[pl.BlockSpec(memory_space=pltpu.SMEM)]
-        + [pl.BlockSpec(memory_space=pltpu.VMEM)] * 6,
+        + [pl.BlockSpec(memory_space=pltpu.VMEM)] * 9,
         out_specs=pl.BlockSpec(memory_space=pltpu.VMEM),
         out_shape=jax.ShapeDtypeStruct((features, frames), BF),
         compiler_params=pltpu.CompilerParams(vmem_limit_bytes=12 * MIB),
         cost_estimate=cost(4),
         name="grad_attn",
-    )(jnp.concatenate([where, lengths]), grad_rows, *pieces, far)
+    )(jnp.concatenate([where, lengths]), grad_rows, *pieces, *far)
 
 
 def attended_kernel(where, attn_t_ref, *refs):
-    pieces, out = [*refs[:4], *(refs[4].at[k] for k in range(4))], refs[5]
+    pieces, out = refs[:8], refs[8]
     size = pieces[0].shape[0]
     total = None
     for i, piece in enumerate(pieces):
@@ -329,15 +322,14 @@
             num_scalar_prefetch=1,
             grid=(features // wide,),
             in_specs=[pl.BlockSpec((features, frames), lambda i, w: (0, 0))]
-            + [pl.BlockSpec((size, wide), lambda i, w: (0, i))] * 4
-            + [pl.BlockSpec((4, size, wide), lambda i, w: (0, 0, i))],
+            + [pl.BlockSpec((size, wide), lambda i, w: (0, i))] * 8,
             out_specs=pl.BlockSpec((frames, wide), lambda i, w: (0, i)),
         ),
         out_shape=jax.ShapeDtypeStruct((frames, features), BF),
-        compiler_params=pltpu.CompilerParams(vmem_limit_bytes=12 * MIB),
-        cost_estimate=cost(4),
+        compiler_params=pltpu.CompilerParams(vmem_limit_bytes=58 * MIB),
+        cost_estimate=cost(0.1),
         name="attended",
-    )(where, attn_t, *pieces, far)
+    )(where, attn_t, *pieces, *far)
 
 
 def grad_weight_kernel(core, attn_t_ref, grad_ref, far_ref, near_ref):
@@ -353,7 +345,7 @@
         near_ref[0] = part
 
 
-def grad_weight_rows(attn_t, grad_rows, before_z, before_x):
+def grad_weight_rows(attn_t, grad_rows):
     features, frames = attn_t.shape
     size = features // 8
     core, z = lax.axis_index("core"), lax.axis_index("z")
@@ -379,22 +371,24 @@
             jax.ShapeDtypeStruct((4, size, features), F32),
         ],
         compiler_params=pltpu.CompilerParams(vmem_limit_bytes=12 * MIB),
-        cost_estimate=cost(5.5),
+        cost_estimate=cost(0.1),
         name="grad_weight",
     )(core.reshape(1).astype(jnp.int32), attn_t, grad_rows)
     total = near + shift(far, "core", 1).astype(F32)
-    total = after(total, *before_z).reshape(4 * size, features)
-    for axis in ("z", "x", "y"):
-        if axis == "x":
-            total = after(total, *before_x)
-        me = lax.axis_index(axis)
-        rows = total.shape[0] // 4
-        mine = lax.dynamic_slice_in_dim(total, me * rows, rows, 0)
-        for k in range(1, 4):
-            piece = lax.dynamic_slice_in_dim(total, (me + k) % 4 * rows, rows, 0)
-            mine = mine + shift(piece.astype(BF), axis, k).astype(F32)
-        total = mine
-    return total
+    return total.reshape(4 * size, features)
+
+
+def begin_sum(total, axis):
+    me = lax.axis_index(axis)
+    rows = total.shape[0] // 4
+    pieces = [lax.dynamic_slice_in_dim(total, (me + k) % 4 * rows, rows, 0) for k in range(4)]
+    return pieces[0], pieces[2].astype(BF), [shift(pieces[k].astype(BF), axis, k) for k in (1, 3)]
+
+
+def end_sum(own, opposite, near, axis):
+    for piece in (*near, shift(opposite, axis, 2)):
+        own = own + piece.astype(F32)
+    return own
 
 
 def body(queries, own_keys, own_values, lengths, history, cache_blocks, out_weight, grad_out):
@@ -422,49 +416,38 @@
     match = (asked // owned)[:, None, :] == owner[None, :, None]
     table = jnp.max(jnp.where(match, (asked % owned)[:, None, :], -1), axis=2)
 
-    fetched, sends, arrived = [], [], []
-    for number, (start, width) in enumerate(CHUNKS):
-        part = lax.slice_in_dim(cache_blocks, start, start + width, axis=3)
-        if number:
-            part = after(part, slab)
-        held = [part] + [move(part, 0, k) for k in range(1, 4)]
-        arrived += held[1:]
-        sent = select_rows(table, held)
-        sends.append(sent[0])
-        fetched.append([sent[0]] + [move(sent[j], 1, j) for j in range(1, 4)])
+    held = [cache_blocks] + [move(cache_blocks, 0, k) for k in range(1, 4)]
+    sent = select_rows(table, held)
+    slots = [sent[0]] + [move(sent[j], 1, j) for j in range(1, 4)]
 
     place = jnp.where(
         straight,
         along_first[:, None] * 4 + along_second[None, :],
         along_second[None, :] * 4 + along_first[:, None],
     )
-    slab = after(slab, arrived[0], arrived[2])
+    slab = after(slab, held[1])
     slabs = [slab] + [move(slab, 0, k) for k in range(1, 4)]
     pieces, far, where = gather_weight(
-        slabs, out_weight.shape[0], place, sends, fetched[0][1:]
+        slabs, out_weight.shape[0], place, sent[:1], ()
     )
-    grad_attn = grad_attn_rows(where, lengths, grad_out[0], pieces, far)
+    grad_attn = grad_attn_rows(where, lengths, after(grad_out[0], *slots[1:]), pieces, far)
 
     own = (queries[0], own_keys[0], own_values[0])
     results, backs = (), []
-    for chunk, parts, slots in zip(CHUNKS, PARTS, fetched):
-        back = ()
-        for number, part in enumerate(parts):
-            if number == len(parts) - 1 and backs:
-                grad_attn = after(grad_attn, *backs[-1][1:])
-            out = attend(
-                meta, *own, grad_attn, slots, ids.shape[0], chunk, part, (*results, *back)
-            )
-            results, back = out[:4], out[4:]
+    for part in PARTS:
+        out = attend(meta, *own, grad_attn, slots, ids.shape[0], part, results)
+        results, back = out[:4], out[4:]
         backs.append([back[0]] + [move(back[j], 1, -j) for j in range(1, 4)])
-    returned = []
-    for back in backs:
-        sums = fold_rows(table, back)
-        returned.append([sums[0]] + [move(sums[k], 0, -k) for k in range(1, 4)])
     attn_t, *grads = results
-    grad_cache = total_rows(returned)
-    attended = attended_rows(where, attn_t, pieces, far)
-    grad_weight = grad_weight_rows(attn_t, grad_out[0], (attended,), (returned[0][0],))
+    total = grad_weight_rows(after(attn_t, *backs[0][1:]), grad_out[0])
+    own, opposite, near = begin_sum(total, "z")
+    sums = fold_rows(table, backs)
+    total = end_sum(after(own, sums[0]), opposite, near, "z")
+    total = end_sum(*begin_sum(total, "x"), "x")
+    attended = attended_rows(where, after(attn_t, total), pieces, far)
+    grad_weight = end_sum(*begin_sum(total, "y"), "y")
+    mine = after(sums[0], attended)
+    grad_cache = total_rows([mine] + [move(sums[k], 0, -k) for k in range(1, 4)])
     return (attended[None], *(grad[None] for grad in grads), grad_cache, grad_weight)
 
 

time: 184 us -> 170 us (0.924)
  local copies, waits for them, and re-layouts: 15.4 us -> 8.4 us
  starting transfers between devices: 51 us -> 44.3 us
  Pallas kernels: 43.4 us -> 47.9 us
  waiting for transfers between devices: 59.8 us -> 57.5 us
  other arithmetic: 9.16 us -> 7.28 us
    ppermute x18 -> x21, waiting for transfers between devices: 41.4 us -> 28.2 us  [move(): return lax.ppermute(array, PLANE, pairs)]
    ppermute x14 -> x17, waiting for transfers between devices: 18.3 us -> 29.3 us  [shift(): return lax.ppermute(array, axis, [(i, (i + amount) % n) for i in range(n)])]
    ppermute x14 -> x17, starting transfers between devices: 24.4 us -> 14.9 us  [shift(): return lax.ppermute(array, axis, [(i, (i + amount) % n) for i in range(n)])]
    unnamed x62 -> x66, local copies, waits for them, and re-layouts: 14.1 us -> 7.78 us
    ppermute x18 -> x21, starting transfers between devices: 26.6 us -> 29.4 us  [move(): return lax.ppermute(array, PLANE, pairs)]
    pallas_call x1 -> x2, Pallas kernels: 21.4 us -> 24.1 us  [attend(): pl.pallas_call(attend_kernel, grid_spec=pltpu.PrefetchScalarGridSpec(num_...]
    pallas_call x1, Pallas kernels: 4.2 us -> 6.81 us  [attended_rows(): pl.pallas_call(attended_kernel, grid_spec=pltpu.PrefetchScalarGridSpec(nu...]
  transfers between devices with their start and end apart: 32 -> 38, of which waited for: 13 -> 14; matrix products, arithmetic and copies ran while one was open for 4% -> 3% of each run, Pallas kernels for 8% -> 18%
where the time goes in v3:
time: 170 us; the launch traced here: 167 us
  waiting for transfers between devices  57.5 us (34%)
  Pallas kernels  47.9 us (28%)
  starting transfers between devices  44.3 us (26%)
  local copies, waits for them, and re-layouts  8.4 us (5%)
  other arithmetic  7.28 us (4%)
  between operations  1.81 us (1%)
    ppermute x21, starting transfers between devices, move(): return lax.ppermute(array, PLANE, pairs)  29.4 us
    ppermute x17, waiting for transfers between devices, shift(): return lax.ppermute(array, axis, [(i, (i + amount) % n) for i in range(n)])  29.3 us
    ppermute x21, waiting for transfers between devices, move(): return lax.ppermute(array, PLANE, pairs)  28.2 us
    pallas_call x2, Pallas kernels, attend(): pl.pallas_call(attend_kernel, grid_spec=pltpu.PrefetchScalarGridSpec(num_...  24.1 us
    ppermute x17, starting transfers between devices, shift(): return lax.ppermute(array, axis, [(i, (i + amount) % n) for i in range(n)])  14.9 us
    unnamed x66, local copies, waits for them, and re-layouts  7.78 us
    pallas_call x1, Pallas kernels, attended_rows(): pl.pallas_call(attended_kernel, grid_spec=pltpu.PrefetchScalarGridSpec(nu...  6.81 us
    pallas_call x1, Pallas kernels, grad_weight_rows(): pl.pallas_call(grad_weight_kernel, grid_spec=pltpu.PrefetchScalarGridSpec...  4.28 us
  transfers between devices with their start and end apart: 38, of which 14 were waited for; matrix products, arithmetic and copies ran while one was open for 3% of the time, Pallas kernels for 18%

profile of v3, /device:TPU:32, one launch (start us, length us, event | category | flops | bytes accessed | tf_op | source)
XLA Modules:
  0.0 167.5 jit_solution(14457615568596494681)
XLA Ops:
  2.4 3.0 %collective-permute-start.2 = (bf16[16,1280]{1,0:T(8,128)(2,1)S(1)}, bf16[16,1280]{1,0:T(8,128)(2,1)S(1)}, u32[]{:S(2)}, u32[]{:S(2)}) collective-permute-start(bf16[16,1280]{1,0:T(8,128)(2,1)S(1)} %maximum_maximum_fusion), channel_id=1, source_target_pairs={{0,3},{1,0},{2,1},{3,2},{4,7},{5,4},{6,5},{7,6},{8,11},{9,8},{10,9... | collective-permute-start | bytes 122888 | tf_op jit(solution)/shard_map/ppermute | solution.py:36
  6.0 1.0 collective-permute-start
  7.0 1.5 collective-permute-start.3
  8.5 2.7 %collective-permute-start.4 = (bf16[2,2,64,1280]{3,2,1,0:T(8,128)(2,1)}, bf16[2,2,64,1280]{3,2,1,0:T(8,128)(2,1)S(1)}, u32[]{:S(2)}, u32[]{:S(2)}) collective-permute-start(bf16[2,2,64,1280]{3,2,1,0:T(8,128)(2,1)} %refs_0_.1), channel_id=1, source_target_pairs={{0,8},{1,9},{2,10},{3,11},{4,12},{5,13},{6,14},{7,15},{8,0},{9,1},... | collective-permute-start | bytes 1966088 | tf_op jit(solution)/shard_map/ppermute | solution.py:36
  12.5 1.5 collective-permute-start.5
  15.0 4.0 %collective-permute-done.3.refs_1_ = bf16[2,2,64,1280]{3,2,1,0:T(8,128)(2,1)S(1)} collective-permute-done((bf16[2,2,64,1280]{3,2,1,0:T(8,128)(2,1)}, bf16[2,2,64,1280]{3,2,1,0:T(8,128)(2,1)S(1)}, u32[]{:S(2)}, u32[]{:S(2)}) %collective-permute-start.3) | collective-permute-done | bytes 655392 | tf_op jit(solution)/shard_map/ppermute | solution.py:36
  19.0 1.5 collective-permute-start.11
  22.3 4.9 %collective-permute-done.4.refs_2_ = bf16[2,2,64,1280]{3,2,1,0:T(8,128)(2,1)S(1)} collective-permute-done((bf16[2,2,64,1280]{3,2,1,0:T(8,128)(2,1)}, bf16[2,2,64,1280]{3,2,1,0:T(8,128)(2,1)S(1)}, u32[]{:S(2)}, u32[]{:S(2)}) %collective-permute-start.4) | collective-permute-done | bytes 655392 | tf_op jit(solution)/shard_map/ppermute | solution.py:36
  27.1 1.1 copy-done.17
  28.2 3.2 %select_rows.1 = (bf16[4,2,64,1280]{3,2,1,0:T(8,128)(2,1)S(1)}, bf16[4,2,64,1280]{3,2,1,0:T(8,128)(2,1)S(1)}, bf16[4,2,64,1280]{3,2,1,0:T(8,128)(2,1)S(1)}, bf16[4,2,64,1280]{3,2,1,0:T(8,128)(2,1)}) custom-call(s32[16]{0:T(128)S(1)} %reshape.346.table, bf16[2,2,64,1280]{3,2,1,0:T(8,128)(2,1)S(1)} %copy-done.17, ...), custom_call_target="tpu_custom_call" | custom-call | flops 3449999872 | tf_op jit(solution)/shard_map/select_rows/pallas_call | solution.py:67
  31.4 1.9 %collective-permute-start.6 = (bf16[4,2,64,1280]{3,2,1,0:T(8,128)(2,1)S(1)}, bf16[4,2,64,1280]{3,2,1,0:T(8,128)(2,1)S(1)}, u32[]{:S(2)}, u32[]{:S(2)}) collective-permute-start(bf16[4,2,64,1280]{3,2,1,0:T(8,128)(2,1)S(1)} %get-tuple-element.39), channel_id=1, source_target_pairs={{0,1},{1,2},{2,3},{3,0},{4,5},{5,6},{6,7},{7,4},{8,9},{9,10},{10,1... | collective-permute-start | bytes 3932168 | tf_op jit(solution)/shard_map/ppermute | solution.py:36
  33.3 1.8 %collective-permute-start.7 = (bf16[4,2,64,1280]{3,2,1,0:T(8,128)(2,1)S(1)}, bf16[4,2,64,1280]{3,2,1,0:T(8,128)(2,1)S(1)}, u32[]{:S(2)}, u32[]{:S(2)}) collective-permute-start(bf16[4,2,64,1280]{3,2,1,0:T(8,128)(2,1)S(1)} %get-tuple-element.40), channel_id=1, source_target_pairs={{0,2},{1,3},{2,0},{3,1},{4,6},{5,7},{6,4},{7,5},{8,10},{9,11},{10,... | collective-permute-start | bytes 3932168 | tf_op jit(solution)/shard_map/ppermute | solution.py:36
  35.5 2.0 %collective-permute-start.12 = (bf16[160,1280]{1,0:T(8,128)(2,1)S(1)}, bf16[160,1280]{1,0:T(8,128)(2,1)S(1)}, u32[]{:S(2)}, u32[]{:S(2)}) collective-permute-start(bf16[160,1280]{1,0:T(8,128)(2,1)S(1)} %convolution_convert_fusion.refs_0_), channel_id=1, source_target_pairs={{0,32},{32,64},{64,96},{96,0},{1,33},{33,65},{65,97},{97,1},{2,34}... | collective-permute-start | bytes 1228808 | tf_op jit(solution)/shard_map/ppermute | solution.py:25
  37.5 0.9 collective-permute-start.8
  38.4 1.1 collective-permute-start.13
  39.6 14.2 %collective-permute-done.12.refs_1_ = bf16[160,1280]{1,0:T(8,128)(2,1)S(1)} collective-permute-done((bf16[160,1280]{1,0:T(8,128)(2,1)S(1)}, bf16[160,1280]{1,0:T(8,128)(2,1)S(1)}, u32[]{:S(2)}, u32[]{:S(2)}) %collective-permute-start.12) | collective-permute-done | bytes 409632 | tf_op jit(solution)/shard_map/ppermute | solution.py:25
  54.0 8.1 %collective-permute-done.14.refs_3_ = bf16[160,1280]{1,0:T(8,128)(2,1)S(1)} collective-permute-done((bf16[160,1280]{1,0:T(8,128)(2,1)S(1)}, bf16[160,1280]{1,0:T(8,128)(2,1)S(1)}, u32[]{:S(2)}, u32[]{:S(2)}) %collective-permute-start.14) | collective-permute-done | bytes 409632 | tf_op jit(solution)/shard_map/ppermute | solution.py:25
  62.1 1.1 copy-done.10
  63.7 1.0 collective-permute-done.7.refs_2_
  64.7 1.1 copy-done.12
  66.8 0.9 collective-permute-done.18.refs_7_
  67.7 3.7 %grad_attn.1.g_ref = bf16[1280,256]{1,0:T(8,128)(2,1)S(1)} custom-call(s32[9]{0:T(128)S(1)} %pad_add_fusion.3.meta, bf16[256,1280]{1,0:T(8,128)(2,1)S(1)} %bitcast.27, bf16[160,1280]{1,0:T(8,128)(2,1)S(1)} %convolution_convert_fusion.refs_0_, bf16[160,1280]{1,0:T(8,128)(2,1)S(1)} %collective-permute-done.12.refs_1_, ...), custom_call_target="tpu_custom_call" | custom-call | flops 4600000000 | tf_op jit(solution)/shard_map/grad_attn/pallas_call | solution.py:292
  71.5 10.0 %attend.2 = (bf16[1280,256]{1,0:T(8,128)(2,1)S(1)}, bf16[256,1280]{1,0:T(8,128)(2,1)}, bf16[256,1280]{1,0:T(8,128)(2,1)}, bf16[256,1280]{1,0:T(8,128)(2,1)}, bf1...) custom-call(s32[17]{0:T(128)S(1)} %pad_add_fusion.2.meta, ...), custom_call_target="tpu_custom_call" | custom-call | flops 10579999744 | tf_op jit(solution)/shard_map/attend/pallas_call | solution.py:239
  82.4 1.1 collective-permute-start.19
  83.4 1.0 collective-permute-start.20
  84.5 1.0 collective-permute-start.21
  85.5 14.1 %attend.3 = (bf16[1280,256]{1,0:T(8,128)(2,1)S(1)}, bf16[256,1280]{1,0:T(8,128)(2,1)}, bf16[256,1280]{1,0:T(8,128)(2,1)}, bf16[256,1280]{1,0:T(8,128)(2,1)}, bf1...) custom-call(s32[17]{0:T(128)S(1)} %pad_add_fusion.2.meta, ...), custom_call_target="tpu_custom_call", output_to_operand_aliasing={{0}: (9, {}), {1}: (10, {}), {2}: (11, {}), {3}: (12, {})} | custom-call | flops 15870000128 | tf_op jit(solution)/shard_map/attend/pallas_call | solution.py:239
  101.3 1.0 copy-done.25
  102.3 4.3 %grad_weight.1 = (bf16[4,160,1280]{2,1,0:T(8,128)(2,1)}, f32[4,160,1280]{2,1,0:T(8,128)S(1)}) custom-call(s32[1]{0:T(128)} %bitcast.14.core, bf16[1280,256]{1,0:T(8,128)(2,1)S(1)} %get-tuple-element.64.attn_t_ref, bf16[256,1280]{1,0:T(8,128)(2,1)S(1)} %bitcast.28), custom_call_target="tpu_custom_call" | custom-call | flops 115000000 | tf_op jit(solution)/shard_map/grad_weight/pallas_call | solution.py:352
  108.3 1.8 %collective-permute-start.23 = (bf16[4,2,64,768]{3,2,1,0:T(8,128)(2,1)}, bf16[4,2,64,768]{3,2,1,0:T(8,128)(2,1)S(1)}, u32[]{:S(2)}, u32[]{:S(2)}) collective-permute-start(bf16[4,2,64,768]{3,2,1,0:T(8,128)(2,1)} %copy-done.16), channel_id=1, source_target_pairs={{0,3},{1,0},{2,1},{3,2},{4,7},{5,4},{6,5},{7,6},{8,11},{9,8},{10,9... | collective-permute-start | bytes 2359304 | tf_op jit(solution)/shard_map/ppermute | solution.py:36
  110.0 1.3 collective-permute-start.24
  111.3 0.9 collective-permute-start.25
  112.3 1.8 %convert_add_fusion = f32[4,160,1280]{2,1,0:T(8,128)S(1)} fusion(f32[4,160,1280]{2,1,0:T(8,128)S(1)} %get-tuple-element.55, bf16[4,160,1280]{2,1,0:T(8,128)(2,1)} %collective-permute-done.22), kind=kLoop, calls=%fused_computation | loop fusion | flops 1638400 | bytes 8192000 | tf_op jit(solution)/shard_map/add | solution.py:377
  114.3 3.1 %collective-permute-start.28 = (bf16[160,1280]{1,0:T(8,128)(2,1)S(1)}, bf16[160,1280]{1,0:T(8,128)(2,1)S(1)}, u32[]{:S(2)}, u32[]{:S(2)}) collective-permute-start(bf16[160,1280]{1,0:T(8,128)(2,1)S(1)} %get-tuple-element.73), channel_id=1, source_target_pairs={{0,64},{32,96},{64,0},{96,32},{1,65},{33,97},{65,1},{97,33},{2,66}... | collective-permute-start | bytes 1228808 | tf_op jit(solution)/shard_map/ppermute | solution.py:25
  117.3 1.0 collective-permute-start.27
  118.3 10.0 %collective-permute-done.23.refs_5_ = bf16[4,2,64,768]{3,2,1,0:T(8,128)(2,1)S(1)} collective-permute-done((bf16[4,2,64,768]{3,2,1,0:T(8,128)(2,1)}, bf16[4,2,64,768]{3,2,1,0:T(8,128)(2,1)S(1)}, u32[]{:S(2)}, u32[]{:S(2)}) %collective-permute-start.23) | collective-permute-done | bytes 786464 | tf_op jit(solution)/shard_map/ppermute | solution.py:36
  128.3 2.0 %collective-permute-start.26 = (bf16[160,1280]{1,0:T(8,128)(2,1)S(1)}, bf16[160,1280]{1,0:T(8,128)(2,1)S(1)}, u32[]{:S(2)}, u32[]{:S(2)}) collective-permute-start(bf16[160,1280]{1,0:T(8,128)(2,1)S(1)} %get-tuple-element.72), channel_id=1, source_target_pairs={{0,32},{32,64},{64,96},{96,0},{1,33},{33,65},{65,97},{97,1},{2,34}... | collective-permute-start | bytes 1228808 | tf_op jit(solution)/shard_map/ppermute | solution.py:25
  130.4 1.8 %collective-permute-done.25.refs_7_ = bf16[4,2,64,768]{3,2,1,0:T(8,128)(2,1)S(1)} collective-permute-done((bf16[4,2,64,768]{3,2,1,0:T(8,128)(2,1)}, bf16[4,2,64,768]{3,2,1,0:T(8,128)(2,1)S(1)}, u32[]{:S(2)}, u32[]{:S(2)}) %collective-permute-start.25) | collective-permute-done | bytes 786464 | tf_op jit(solution)/shard_map/ppermute | solution.py:36
  132.2 3.5 %fold_rows.1 = (bf16[2,2,64,1280]{3,2,1,0:T(8,128)(2,1)S(1)}, bf16[2,2,64,1280]{3,2,1,0:T(8,128)(2,1)S(1)}, bf16[2,2,64,1280]{3,2,1,0:T(8,128)(2,1)S(1)}, bf16[2,2,64,1280]{3,2,1,0:T(8,128)(2,1)S(1)}) custom-call(s32[16]{0:T(128)S(1)} %reshape.346.table, bf16[4,2,64,512]{3,2,1,0:T(8,128)(2,1)S(1)} %copy-done.32, bf16[4,2,64,512]{3,2,1,0:T(8,128)(2,1)S(1)} %copy-done.22, ...), custom_call_target="tpu_custom_call" | custom-call | flops 4600000000 | tf_op jit(solution)/shard_map/fold_rows/pallas_call | solution.py:112
  135.8 4.4 %collective-permute-done.26 = bf16[160,1280]{1,0:T(8,128)(2,1)S(1)} collective-permute-done((bf16[160,1280]{1,0:T(8,128)(2,1)S(1)}, bf16[160,1280]{1,0:T(8,128)(2,1)S(1)}, u32[]{:S(2)}, u32[]{:S(2)}) %collective-permute-start.26) | collective-permute-done | bytes 409632 | tf_op jit(solution)/shard_map/ppermute | solution.py:25
  141.3 1.3 collective-permute-start.29
  143.2 2.0 %collective-permute-start.32 = (bf16[2,2,64,1280]{3,2,1,0:T(8,128)(2,1)S(1)}, bf16[2,2,64,1280]{3,2,1,0:T(8,128)(2,1)S(1)}, u32[]{:S(2)}, u32[]{:S(2)}) collective-permute-start(bf16[2,2,64,1280]{3,2,1,0:T(8,128)(2,1)S(1)} %get-tuple-element.69), channel_id=1, source_target_pairs={{0,12},{1,13},{2,14},{3,15},{4,0},{5,1},{6,2},{7,3},{8,4},{9,5},{1... | collective-permute-start | bytes 1966088 | tf_op jit(solution)/shard_map/ppermute | solution.py:36
  145.2 1.5 collective-permute-start.33
  148.9 6.8 %attended.1 = bf16[256,1280]{1,0:T(8,128)(2,1)} custom-call(s32[8]{0:T(128)} %pad_add_fusion.1.where, bf16[1280,256]{1,0:T(8,128)(2,1)} %copy-done, bf16[160,1280]{1,0:T(8,128)(2,1)} %copy-done.1, bf16[160,1280]{1,0:T(8,128)(2,1)} %copy-done.4, bf16[160,1280]{1,0:T(8,128)(2,1)} %copy-done.5, bf16[160,1280]{1,0:T(8,128)(2,1)} %copy-done.6, ...), custom_call_target="tpu_custom_call" | custom-call | flops 115000000 | tf_op jit(solution)/shard_map/attended/pallas_call | solution.py:319
  155.7 1.1 collective-permute-start.37
  157.5 2.9 %collective-permute-done.32.refs_1_ = bf16[2,2,64,1280]{3,2,1,0:T(8,128)(2,1)S(1)} collective-permute-done((bf16[2,2,64,1280]{3,2,1,0:T(8,128)(2,1)S(1)}, bf16[2,2,64,1280]{3,2,1,0:T(8,128)(2,1)S(1)}, u32[]{:S(2)}, u32[]{:S(2)}) %collective-permute-start.32) | collective-permute-done | bytes 655392 | tf_op jit(solution)/shard_map/ppermute | solution.py:36
  160.7 3.6 %collective-permute-done.34.refs_3_ = bf16[2,2,64,1280]{3,2,1,0:T(8,128)(2,1)S(1)} collective-permute-done((bf16[2,2,64,1280]{3,2,1,0:T(8,128)(2,1)S(1)}, bf16[2,2,64,1280]{3,2,1,0:T(8,128)(2,1)S(1)}, u32[]{:S(2)}, u32[]{:S(2)}) %collective-permute-start.34) | collective-permute-done | bytes 655392 | tf_op jit(solution)/shard_map/ppermute | solution.py:36
  164.3 2.4 %total_rows.1 = f32[2,2,64,1280]{3,2,1,0:T(8,128)} custom-call(bf16[2,2,64,1280]{3,2,1,0:T(8,128)(2,1)S(1)} %get-tuple-element.68.refs_0_, bf16[2,2,64,1280]{3,2,1,0:T(8,128)(2,1)S(1)} %collective-permute-done.32.refs_1_, bf16[2,2,64,1280]{3,2,1,0:T(8,128)(2,1)S(1)} %collective-permute-done.33.refs_2_, ...), custom_call_target="tpu_custom_call" | custom-call | flops 4600000000 | tf_op jit(solution)/shard_map/total_rows/pallas_call | solution.py:137
  (140 shorter events, 17.7 us)
Async XLA Ops:
  2.4 10.1 %collective-permute-start.2 = (bf16[16,1280]{1,0:T(8,128)(2,1)S(1)}, bf16[16,1280]{1,0:T(8,128)(2,1)S(1)}, u32[]{:S(2)}, u32[]{:S(2)}) collective-permute-start(bf16[16,1280]{1,0:T(8,128)(2,1)S(1)} %maximum_maximum_fusion), channel_id=1, source_target_pairs={{0,3},{1,0},{2,1},{3,2},{4,7},{5,4},{6,5},{7,6},{8,11},{9,8},{10,9... | collective-permute-start | bytes 122888 | tf_op jit(solution)/shard_map/ppermute | solution.py:36
  5.4 8.6 %collective-permute-start.1 = (bf16[16,1280]{1,0:T(8,128)(2,1)S(1)}, bf16[16,1280]{1,0:T(8,128)(2,1)S(1)}, u32[]{:S(2)}, u32[]{:S(2)}) collective-permute-start(bf16[16,1280]{1,0:T(8,128)(2,1)S(1)} %maximum_maximum_fusion), channel_id=1, source_target_pairs={{0,2},{1,3},{2,0},{3,1},{4,6},{5,7},{6,4},{7,5},{8,10},{9,11},{10,... | collective-permute-start | bytes 122888 | tf_op jit(solution)/shard_map/ppermute | solution.py:36
  6.0 7.9 %collective-permute-start = (bf16[16,1280]{1,0:T(8,128)(2,1)S(1)}, bf16[16,1280]{1,0:T(8,128)(2,1)S(1)}, u32[]{:S(2)}, u32[]{:S(2)}) collective-permute-start(bf16[16,1280]{1,0:T(8,128)(2,1)S(1)} %maximum_maximum_fusion), channel_id=1, source_target_pairs={{0,1},{1,2},{2,3},{3,0},{4,5},{5,6},{6,7},{7,4},{8,9},{9,10},{10,1... | collective-permute-start | bytes 122888 | tf_op jit(solution)/shard_map/ppermute | solution.py:36
  7.0 12.0 %collective-permute-start.3 = (bf16[2,2,64,1280]{3,2,1,0:T(8,128)(2,1)}, bf16[2,2,64,1280]{3,2,1,0:T(8,128)(2,1)S(1)}, u32[]{:S(2)}, u32[]{:S(2)}) collective-permute-start(bf16[2,2,64,1280]{3,2,1,0:T(8,128)(2,1)} %refs_0_.1), channel_id=1, source_target_pairs={{0,4},{1,5},{2,6},{3,7},{4,8},{5,9},{6,10},{7,11},{8,12},{9,13},{1... | collective-permute-start | bytes 1966088 | tf_op jit(solution)/shard_map/ppermute | solution.py:36
  8.5 18.6 %collective-permute-start.4 = (bf16[2,2,64,1280]{3,2,1,0:T(8,128)(2,1)}, bf16[2,2,64,1280]{3,2,1,0:T(8,128)(2,1)S(1)}, u32[]{:S(2)}, u32[]{:S(2)}) collective-permute-start(bf16[2,2,64,1280]{3,2,1,0:T(8,128)(2,1)} %refs_0_.1), channel_id=1, source_target_pairs={{0,8},{1,9},{2,10},{3,11},{4,12},{5,13},{6,14},{7,15},{8,0},{9,1},... | collective-permute-start | bytes 1966088 | tf_op jit(solution)/shard_map/ppermute | solution.py:36
  12.5 14.6 %collective-permute-start.5 = (bf16[2,2,64,1280]{3,2,1,0:T(8,128)(2,1)}, bf16[2,2,64,1280]{3,2,1,0:T(8,128)(2,1)S(1)}, u32[]{:S(2)}, u32[]{:S(2)}) collective-permute-start(bf16[2,2,64,1280]{3,2,1,0:T(8,128)(2,1)} %refs_0_.1), channel_id=1, source_target_pairs={{0,12},{1,13},{2,14},{3,15},{4,0},{5,1},{6,2},{7,3},{8,4},{9,5},{1... | collective-permute-start | bytes 1966088 | tf_op jit(solution)/shard_map/ppermute | solution.py:36
  19.0 16.1 %collective-permute-start.11 = (bf16[4,16,1280]{2,1,0:T(8,128)(2,1)S(1)}, bf16[4,16,1280]{2,1,0:T(8,128)(2,1)S(1)}, u32[]{:S(2)}, u32[]{:S(2)}) collective-permute-start(bf16[4,16,1280]{2,1,0:T(8,128)(2,1)S(1)} %pad_maximum_fusion.1), channel_id=1, source_target_pairs={{0,12},{1,13},{2,14},{3,15},{4,0},{5,1},{6,2},{7,3},{8,4},{9,5},{1... | collective-permute-start | bytes 491528 | tf_op jit(solution)/shard_map/ppermute | solution.py:36
  20.6 14.6 %collective-permute-start.10 = (bf16[4,16,1280]{2,1,0:T(8,128)(2,1)S(1)}, bf16[4,16,1280]{2,1,0:T(8,128)(2,1)S(1)}, u32[]{:S(2)}, u32[]{:S(2)}) collective-permute-start(bf16[4,16,1280]{2,1,0:T(8,128)(2,1)S(1)} %pad_maximum_fusion.1), channel_id=1, source_target_pairs={{0,8},{1,9},{2,10},{3,11},{4,12},{5,13},{6,14},{7,15},{8,0},{9,1},... | collective-permute-start | bytes 491528 | tf_op jit(solution)/shard_map/ppermute | solution.py:36
  21.4 13.8 %collective-permute-start.9 = (bf16[4,16,1280]{2,1,0:T(8,128)(2,1)S(1)}, bf16[4,16,1280]{2,1,0:T(8,128)(2,1)S(1)}, u32[]{:S(2)}, u32[]{:S(2)}) collective-permute-start(bf16[4,16,1280]{2,1,0:T(8,128)(2,1)S(1)} %pad_maximum_fusion.1), channel_id=1, source_target_pairs={{0,4},{1,5},{2,6},{3,7},{4,8},{5,9},{6,10},{7,11},{8,12},{9,13},{1... | collective-permute-start | bytes 491528 | tf_op jit(solution)/shard_map/ppermute | solution.py:36
  31.4 36.3 %copy-start.2 = (bf16[1,256,1280]{2,1,0:T(8,128)(2,1)S(1)}, bf16[1,256,1280]{2,1,0:T(8,128)(2,1)}, u32[]{:S(2)}) copy-start(bf16[1,256,1280]{2,1,0:T(8,128)(2,1)} %param.15) | copy-start | bytes 1966084
  31.4 30.7 %collective-permute-start.6 = (bf16[4,2,64,1280]{3,2,1,0:T(8,128)(2,1)S(1)}, bf16[4,2,64,1280]{3,2,1,0:T(8,128)(2,1)S(1)}, u32[]{:S(2)}, u32[]{:S(2)}) collective-permute-start(bf16[4,2,64,1280]{3,2,1,0:T(8,128)(2,1)S(1)} %get-tuple-element.39), channel_id=1, source_target_pairs={{0,1},{1,2},{2,3},{3,0},{4,5},{5,6},{6,7},{7,4},{8,9},{9,10},{10,1... | collective-permute-start | bytes 3932168 | tf_op jit(solution)/shard_map/ppermute | solution.py:36
  33.3 31.5 %collective-permute-start.7 = (bf16[4,2,64,1280]{3,2,1,0:T(8,128)(2,1)S(1)}, bf16[4,2,64,1280]{3,2,1,0:T(8,128)(2,1)S(1)}, u32[]{:S(2)}, u32[]{:S(2)}) collective-permute-start(bf16[4,2,64,1280]{3,2,1,0:T(8,128)(2,1)S(1)} %get-tuple-element.40), channel_id=1, source_target_pairs={{0,2},{1,3},{2,0},{3,1},{4,6},{5,7},{6,4},{7,5},{8,10},{9,11},{10,... | collective-permute-start | bytes 3932168 | tf_op jit(solution)/shard_map/ppermute | solution.py:36
  35.5 35.9 %copy-start.1 = (bf16[160,1280]{1,0:T(8,128)(2,1)}, bf16[160,1280]{1,0:T(8,128)(2,1)S(1)}, u32[]{:S(2)}) copy-start(bf16[160,1280]{1,0:T(8,128)(2,1)S(1)} %convolution_convert_fusion.refs_0_) | copy-start | bytes 1228804
  35.5 18.2 %collective-permute-start.12 = (bf16[160,1280]{1,0:T(8,128)(2,1)S(1)}, bf16[160,1280]{1,0:T(8,128)(2,1)S(1)}, u32[]{:S(2)}, u32[]{:S(2)}) collective-permute-start(bf16[160,1280]{1,0:T(8,128)(2,1)S(1)} %convolution_convert_fusion.refs_0_), channel_id=1, source_target_pairs={{0,32},{32,64},{64,96},{96,0},{1,33},{33,65},{65,97},{97,1},{2,34}... | collective-permute-start | bytes 1228808 | tf_op jit(solution)/shard_map/ppermute | solution.py:25
  37.5 29.2 %collective-permute-start.8 = (bf16[4,2,64,1280]{3,2,1,0:T(8,128)(2,1)}, bf16[4,2,64,1280]{3,2,1,0:T(8,128)(2,1)}, u32[]{:S(2)}, u32[]{:S(2)}) collective-permute-start(bf16[4,2,64,1280]{3,2,1,0:T(8,128)(2,1)} %get-tuple-element.41), channel_id=1, source_target_pairs={{0,3},{1,0},{2,1},{3,2},{4,7},{5,4},{6,5},{7,6},{8,11},{9,8},{10,9... | collective-permute-start | bytes 3932168 | tf_op jit(solution)/shard_map/ppermute | solution.py:36
  38.4 15.5 %collective-permute-start.13 = (bf16[160,1280]{1,0:T(8,128)(2,1)S(1)}, bf16[160,1280]{1,0:T(8,128)(2,1)S(1)}, u32[]{:S(2)}, u32[]{:S(2)}) collective-permute-start(bf16[160,1280]{1,0:T(8,128)(2,1)S(1)} %convolution_convert_fusion.refs_0_), channel_id=1, source_target_pairs={{0,64},{32,96},{64,0},{96,32},{1,65},{33,97},{65,1},{97,33},{2,66}... | collective-permute-start | bytes 1228808 | tf_op jit(solution)/shard_map/ppermute | solution.py:25
  53.7 17.7 %copy-start.4 = (bf16[160,1280]{1,0:T(8,128)(2,1)}, bf16[160,1280]{1,0:T(8,128)(2,1)S(1)}, u32[]{:S(2)}) copy-start(bf16[160,1280]{1,0:T(8,128)(2,1)S(1)} %collective-permute-done.12.refs_1_) | copy-start | bytes 1228804
  53.7 8.4 %collective-permute-start.14 = (bf16[160,1280]{1,0:T(8,128)(2,1)S(1)}, bf16[160,1280]{1,0:T(8,128)(2,1)S(1)}, u32[]{:S(2)}, u32[]{:S(2)}) collective-permute-start(bf16[160,1280]{1,0:T(8,128)(2,1)S(1)} %convolution_convert_fusion.refs_0_), channel_id=1, source_target_pairs={{0,96},{32,0},{64,32},{96,64},{1,97},{33,1},{65,33},{97,65},{2,98}... | collective-permute-start | bytes 1228808 | tf_op jit(solution)/shard_map/ppermute | solution.py:25
  53.9 17.5 %copy-start.5 = (bf16[160,1280]{1,0:T(8,128)(2,1)}, bf16[160,1280]{1,0:T(8,128)(2,1)S(1)}, u32[]{:S(2)}) copy-start(bf16[160,1280]{1,0:T(8,128)(2,1)S(1)} %collective-permute-done.13.refs_2_) | copy-start | bytes 1228804
  53.9 12.8 %collective-permute-start.15 = (bf16[160,1280]{1,0:T(8,128)(2,1)S(1)}, bf16[160,1280]{1,0:T(8,128)(2,1)S(1)}, u32[]{:S(2)}, u32[]{:S(2)}) collective-permute-start(bf16[160,1280]{1,0:T(8,128)(2,1)S(1)} %convolution_convert_fusion.refs_0_), channel_id=1, source_target_pairs={{0,16},{16,0},{1,17},{17,1},{2,18},{18,2},{3,19},{19,3},{4,20},{20... | collective-permute-start | bytes 1228808 | tf_op jit(solution)/shard_map/ppermute | solution.py:25
  62.1 4.6 %collective-permute-start.16 = (bf16[160,1280]{1,0:T(8,128)(2,1)S(1)}, bf16[160,1280]{1,0:T(8,128)(2,1)S(1)}, u32[]{:S(2)}, u32[]{:S(2)}) collective-permute-start(bf16[160,1280]{1,0:T(8,128)(2,1)S(1)} %collective-permute-done.12.refs_1_), channel_id=1, source_target_pairs={{0,16},{16,0},{1,17},{17,1},{2,18},{18,2},{3,19},{19,3},{4,20},{20... | collective-permute-start | bytes 1228808 | tf_op jit(solution)/shard_map/ppermute | solution.py:25
  63.2 3.5 %collective-permute-start.17 = (bf16[160,1280]{1,0:T(8,128)(2,1)S(1)}, bf16[160,1280]{1,0:T(8,128)(2,1)S(1)}, u32[]{:S(2)}, u32[]{:S(2)}) collective-permute-start(bf16[160,1280]{1,0:T(8,128)(2,1)S(1)} %collective-permute-done.13.refs_2_), channel_id=1, source_target_pairs={{0,16},{16,0},{1,17},{17,1},{2,18},{18,2},{3,19},{19,3},{4,20},{20... | collective-permute-start | bytes 1228808 | tf_op jit(solution)/shard_map/ppermute | solution.py:25
  65.8 1.9 %collective-permute-start.18 = (bf16[160,1280]{1,0:T(8,128)(2,1)S(1)}, bf16[160,1280]{1,0:T(8,128)(2,1)}, u32[]{:S(2)}, u32[]{:S(2)}) collective-permute-start(bf16[160,1280]{1,0:T(8,128)(2,1)S(1)} %collective-permute-done.14.refs_3_), channel_id=1, source_target_pairs={{0,16},{16,0},{1,17},{17,1},{2,18},{18,2},{3,19},{19,3},{4,20},{20... | collective-permute-start | bytes 1228808 | tf_op jit(solution)/shard_map/ppermute | solution.py:25
  82.4 18.1 %collective-permute-start.19 = (bf16[4,2,64,512]{3,2,1,0:T(8,128)(2,1)S(1)}, bf16[4,2,64,512]{3,2,1,0:T(8,128)(2,1)S(1)}, u32[]{:S(2)}, u32[]{:S(2)}) collective-permute-start(bf16[4,2,64,512]{3,2,1,0:T(8,128)(2,1)S(1)} %get-tuple-element.51), channel_id=1, source_target_pairs={{0,3},{1,0},{2,1},{3,2},{4,7},{5,4},{6,5},{7,6},{8,11},{9,8},{10,9... | collective-permute-start | bytes 1572872 | tf_op jit(solution)/shard_map/ppermute | solution.py:36
  83.4 17.0 %collective-permute-start.20 = (bf16[4,2,64,512]{3,2,1,0:T(8,128)(2,1)S(1)}, bf16[4,2,64,512]{3,2,1,0:T(8,128)(2,1)S(1)}, u32[]{:S(2)}, u32[]{:S(2)}) collective-permute-start(bf16[4,2,64,512]{3,2,1,0:T(8,128)(2,1)S(1)} %get-tuple-element.52), channel_id=1, source_target_pairs={{0,2},{1,3},{2,0},{3,1},{4,6},{5,7},{6,4},{7,5},{8,10},{9,11},{10,... | collective-permute-start | bytes 1572872 | tf_op jit(solution)/shard_map/ppermute | solution.py:36
  84.5 16.9 %collective-permute-start.21 = (bf16[4,2,64,512]{3,2,1,0:T(8,128)(2,1)S(1)}, bf16[4,2,64,512]{3,2,1,0:T(8,128)(2,1)S(1)}, u32[]{:S(2)}, u32[]{:S(2)}) collective-permute-start(bf16[4,2,64,512]{3,2,1,0:T(8,128)(2,1)S(1)} %get-tuple-element.53), channel_id=1, source_target_pairs={{0,1},{1,2},{2,3},{3,0},{4,5},{5,6},{6,7},{7,4},{8,9},{9,10},{10,1... | collective-permute-start | bytes 1572872 | tf_op jit(solution)/shard_map/ppermute | solution.py:36
  85.5 16.9 %copy-start.3 = (bf16[1,256,1280]{2,1,0:T(8,128)(2,1)S(1)}, bf16[1,256,1280]{2,1,0:T(8,128)(2,1)}, u32[]{:S(2)}) copy-start(bf16[1,256,1280]{2,1,0:T(8,128)(2,1)} %param.15) | copy-start | bytes 1966084
  107.5 4.8 %collective-permute-start.22 = (bf16[4,160,1280]{2,1,0:T(8,128)(2,1)}, bf16[4,160,1280]{2,1,0:T(8,128)(2,1)}, u32[]{:S(2)}, u32[]{:S(2)}) collective-permute-start(bf16[4,160,1280]{2,1,0:T(8,128)(2,1)} %get-tuple-element.56), channel_id=1, source_target_pairs={{0,16},{16,0},{1,17},{17,1},{2,18},{18,2},{3,19},{19,3},{4,20},{20... | collective-permute-start | bytes 4915208 | tf_op jit(solution)/shard_map/ppermute | solution.py:25
  108.3 20.1 %collective-permute-start.23 = (bf16[4,2,64,768]{3,2,1,0:T(8,128)(2,1)}, bf16[4,2,64,768]{3,2,1,0:T(8,128)(2,1)S(1)}, u32[]{:S(2)}, u32[]{:S(2)}) collective-permute-start(bf16[4,2,64,768]{3,2,1,0:T(8,128)(2,1)} %copy-done.16), channel_id=1, source_target_pairs={{0,3},{1,0},{2,1},{3,2},{4,7},{5,4},{6,5},{7,6},{8,11},{9,8},{10,9... | collective-permute-start | bytes 2359304 | tf_op jit(solution)/shard_map/ppermute | solution.py:36
  110.0 20.3 %collective-permute-start.24 = (bf16[4,2,64,768]{3,2,1,0:T(8,128)(2,1)}, bf16[4,2,64,768]{3,2,1,0:T(8,128)(2,1)S(1)}, u32[]{:S(2)}, u32[]{:S(2)}) collective-permute-start(bf16[4,2,64,768]{3,2,1,0:T(8,128)(2,1)} %copy-done.15), channel_id=1, source_target_pairs={{0,2},{1,3},{2,0},{3,1},{4,6},{5,7},{6,4},{7,5},{8,10},{9,11},{10,... | collective-permute-start | bytes 2359304 | tf_op jit(solution)/shard_map/ppermute | solution.py:36
  111.3 20.8 %collective-permute-start.25 = (bf16[4,2,64,768]{3,2,1,0:T(8,128)(2,1)}, bf16[4,2,64,768]{3,2,1,0:T(8,128)(2,1)S(1)}, u32[]{:S(2)}, u32[]{:S(2)}) collective-permute-start(bf16[4,2,64,768]{3,2,1,0:T(8,128)(2,1)} %copy-done.14), channel_id=1, source_target_pairs={{0,1},{1,2},{2,3},{3,0},{4,5},{5,6},{6,7},{7,4},{8,9},{9,10},{10,1... | collective-permute-start | bytes 2359304 | tf_op jit(solution)/shard_map/ppermute | solution.py:36
  112.3 19.9 %copy-start.32 = (bf16[4,2,64,512]{3,2,1,0:T(8,128)(2,1)S(1)}, bf16[4,2,64,512]{3,2,1,0:T(8,128)(2,1)}, u32[]{:S(2)}) copy-start(bf16[4,2,64,512]{3,2,1,0:T(8,128)(2,1)} %copy-done.31) | copy-start | bytes 1572868
  114.1 18.1 %copy-start.22 = (bf16[4,2,64,512]{3,2,1,0:T(8,128)(2,1)S(1)}, bf16[4,2,64,512]{3,2,1,0:T(8,128)(2,1)}, u32[]{:S(2)}) copy-start(bf16[4,2,64,512]{3,2,1,0:T(8,128)(2,1)} %copy-done.21) | copy-start | bytes 1572868
  114.1 18.1 %copy-start.24 = (bf16[4,2,64,512]{3,2,1,0:T(8,128)(2,1)S(1)}, bf16[4,2,64,512]{3,2,1,0:T(8,128)(2,1)}, u32[]{:S(2)}) copy-start(bf16[4,2,64,512]{3,2,1,0:T(8,128)(2,1)} %copy-done.23) | copy-start | bytes 1572868
  114.1 18.1 %copy-start.26 = (bf16[4,2,64,512]{3,2,1,0:T(8,128)(2,1)S(1)}, bf16[4,2,64,512]{3,2,1,0:T(8,128)(2,1)}, u32[]{:S(2)}) copy-start(bf16[4,2,64,512]{3,2,1,0:T(8,128)(2,1)} %copy-done.25) | copy-start | bytes 1572868
  114.1 18.1 %copy-start.30 = (bf16[4,2,64,768]{3,2,1,0:T(8,128)(2,1)S(1)}, bf16[4,2,64,768]{3,2,1,0:T(8,128)(2,1)}, u32[]{:S(2)}) copy-start(bf16[4,2,64,768]{3,2,1,0:T(8,128)(2,1)} %copy-done.29) | copy-start | bytes 2359300
  114.3 21.5 %collective-permute-start.28 = (bf16[160,1280]{1,0:T(8,128)(2,1)S(1)}, bf16[160,1280]{1,0:T(8,128)(2,1)S(1)}, u32[]{:S(2)}, u32[]{:S(2)}) collective-permute-start(bf16[160,1280]{1,0:T(8,128)(2,1)S(1)} %get-tuple-element.73), channel_id=1, source_target_pairs={{0,64},{32,96},{64,0},{96,32},{1,65},{33,97},{65,1},{97,33},{2,66}... | collective-permute-start | bytes 1228808 | tf_op jit(solution)/shard_map/ppermute | solution.py:25
  117.3 18.5 %collective-permute-start.27 = (bf16[160,1280]{1,0:T(8,128)(2,1)S(1)}, bf16[160,1280]{1,0:T(8,128)(2,1)S(1)}, u32[]{:S(2)}, u32[]{:S(2)}) collective-permute-start(bf16[160,1280]{1,0:T(8,128)(2,1)S(1)} %get-tuple-element.74), channel_id=1, source_target_pairs={{0,96},{32,0},{64,32},{96,64},{1,97},{33,1},{65,33},{97,65},{2,98}... | collective-permute-start | bytes 1228808 | tf_op jit(solution)/shard_map/ppermute | solution.py:25
  128.3 11.9 %collective-permute-start.26 = (bf16[160,1280]{1,0:T(8,128)(2,1)S(1)}, bf16[160,1280]{1,0:T(8,128)(2,1)S(1)}, u32[]{:S(2)}, u32[]{:S(2)}) collective-permute-start(bf16[160,1280]{1,0:T(8,128)(2,1)S(1)} %get-tuple-element.72), channel_id=1, source_target_pairs={{0,32},{32,64},{64,96},{96,0},{1,33},{33,65},{65,97},{97,1},{2,34}... | collective-permute-start | bytes 1228808 | tf_op jit(solution)/shard_map/ppermute | solution.py:25
  140.5 7.1 %collective-permute-start.31 = (bf16[40,1280]{1,0:T(8,128)(2,1)S(1)}, bf16[40,1280]{1,0:T(8,128)(2,1)S(1)}, u32[]{:S(2)}, u32[]{:S(2)}) collective-permute-start(bf16[40,1280]{1,0:T(8,128)(2,1)S(1)} %get-tuple-element.76), channel_id=1, source_target_pairs={{0,8},{4,12},{8,0},{12,4},{1,9},{5,13},{9,1},{13,5},{2,10},{6,14},... | collective-permute-start | bytes 307208 | tf_op jit(solution)/shard_map/ppermute | solution.py:25
  140.6 7.6 %collective-permute-start.30 = (bf16[40,1280]{1,0:T(8,128)(2,1)S(1)}, bf16[40,1280]{1,0:T(8,128)(2,1)S(1)}, u32[]{:S(2)}, u32[]{:S(2)}) collective-permute-start(bf16[40,1280]{1,0:T(8,128)(2,1)S(1)} %get-tuple-element.77), channel_id=1, source_target_pairs={{0,12},{4,0},{8,4},{12,8},{1,13},{5,1},{9,5},{13,9},{2,14},{6,2},{... | collective-permute-start | bytes 307208 | tf_op jit(solution)/shard_map/ppermute | solution.py:25
  141.3 7.5 %collective-permute-start.29 = (bf16[40,1280]{1,0:T(8,128)(2,1)S(1)}, bf16[40,1280]{1,0:T(8,128)(2,1)S(1)}, u32[]{:S(2)}, u32[]{:S(2)}) collective-permute-start(bf16[40,1280]{1,0:T(8,128)(2,1)S(1)} %get-tuple-element.75), channel_id=1, source_target_pairs={{0,4},{4,8},{8,12},{12,0},{1,5},{5,9},{9,13},{13,1},{2,6},{6,10},{... | collective-permute-start | bytes 307208 | tf_op jit(solution)/shard_map/ppermute | solution.py:25
  143.2 17.1 %collective-permute-start.32 = (bf16[2,2,64,1280]{3,2,1,0:T(8,128)(2,1)S(1)}, bf16[2,2,64,1280]{3,2,1,0:T(8,128)(2,1)S(1)}, u32[]{:S(2)}, u32[]{:S(2)}) collective-permute-start(bf16[2,2,64,1280]{3,2,1,0:T(8,128)(2,1)S(1)} %get-tuple-element.69), channel_id=1, source_target_pairs={{0,12},{1,13},{2,14},{3,15},{4,0},{5,1},{6,2},{7,3},{8,4},{9,5},{1... | collective-permute-start | bytes 1966088 | tf_op jit(solution)/shard_map/ppermute | solution.py:36
  145.2 15.5 %collective-permute-start.33 = (bf16[2,2,64,1280]{3,2,1,0:T(8,128)(2,1)S(1)}, bf16[2,2,64,1280]{3,2,1,0:T(8,128)(2,1)S(1)}, u32[]{:S(2)}, u32[]{:S(2)}) collective-permute-start(bf16[2,2,64,1280]{3,2,1,0:T(8,128)(2,1)S(1)} %get-tuple-element.70), channel_id=1, source_target_pairs={{0,8},{1,9},{2,10},{3,11},{4,12},{5,13},{6,14},{7,15},{8,0},{9,1},... | collective-permute-start | bytes 1966088 | tf_op jit(solution)/shard_map/ppermute | solution.py:36
  147.5 16.8 %collective-permute-start.34 = (bf16[2,2,64,1280]{3,2,1,0:T(8,128)(2,1)S(1)}, bf16[2,2,64,1280]{3,2,1,0:T(8,128)(2,1)S(1)}, u32[]{:S(2)}, u32[]{:S(2)}) collective-permute-start(bf16[2,2,64,1280]{3,2,1,0:T(8,128)(2,1)S(1)} %get-tuple-element.71), channel_id=1, source_target_pairs={{0,4},{1,5},{2,6},{3,7},{4,8},{5,9},{6,10},{7,11},{8,12},{9,13},{1... | collective-permute-start | bytes 1966088 | tf_op jit(solution)/shard_map/ppermute | solution.py:36
  155.7 11.1 %collective-permute-start.37 = (bf16[10,1280]{1,0:T(8,128)(2,1)S(1)}, bf16[10,1280]{1,0:T(8,128)(2,1)S(1)}, u32[]{:S(2)}, u32[]{:S(2)}) collective-permute-start(bf16[10,1280]{1,0:T(8,128)(2,1)S(1)} %get-tuple-element.79), channel_id=1, source_target_pairs={{0,2},{1,3},{2,0},{3,1},{4,6},{5,7},{6,4},{7,5},{8,10},{9,11},{10,... | collective-permute-start | bytes 76808 | tf_op jit(solution)/shard_map/ppermute | solution.py:25
  156.8 9.9 %collective-permute-start.36 = (bf16[10,1280]{1,0:T(8,128)(2,1)S(1)}, bf16[10,1280]{1,0:T(8,128)(2,1)S(1)}, u32[]{:S(2)}, u32[]{:S(2)}) collective-permute-start(bf16[10,1280]{1,0:T(8,128)(2,1)S(1)} %get-tuple-element.80), channel_id=1, source_target_pairs={{0,3},{1,0},{2,1},{3,2},{4,7},{5,4},{6,5},{7,6},{8,11},{9,8},{10,9... | collective-permute-start | bytes 76808 | tf_op jit(solution)/shard_map/ppermute | solution.py:25
  160.4 6.4 %collective-permute-start.35 = (bf16[10,1280]{1,0:T(8,128)(2,1)S(1)}, bf16[10,1280]{1,0:T(8,128)(2,1)S(1)}, u32[]{:S(2)}, u32[]{:S(2)}) collective-permute-start(bf16[10,1280]{1,0:T(8,128)(2,1)S(1)} %get-tuple-element.78), channel_id=1, source_target_pairs={{0,1},{1,2},{2,3},{3,0},{4,5},{5,6},{6,7},{7,4},{8,9},{9,10},{10,1... | collective-permute-start | bytes 76808 | tf_op jit(solution)/shard_map/ppermute | solution.py:25
  (23 other events, 95.4 us)

commit v4 on v3

--- a/solution.py
+++ b/solution.py
@@ -118,7 +118,7 @@
             out_specs=[pl.BlockSpec((2, kinds, rows, STEP), lambda i, t: (0, 0, 0, i))] * 4,
         ),
         out_shape=[jax.ShapeDtypeStruct((2, kinds, rows, columns), BF)] * 4,
-        compiler_params=pltpu.CompilerParams(vmem_limit_bytes=16 * MIB),
+        compiler_params=pltpu.CompilerParams(vmem_limit_bytes=58 * MIB),
         cost_estimate=cost(4),
         name="fold_rows",
     )(table.reshape(-1), *backs[0], *backs[1])
@@ -251,7 +251,7 @@
         + [rows] * 3
         + [jax.ShapeDtypeStruct((4, 2, BLK, part[1]), BF)] * 4,
         input_output_aliases={9 + i: i for i in range(len(kept))},
-        compiler_params=pltpu.CompilerParams(vmem_limit_bytes=24 * MIB),
+        compiler_params=pltpu.CompilerParams(vmem_limit_bytes=58 * MIB),
         cost_estimate=cost(part[1] // STEP * 4.6),
         name="attend",
     )(meta, query, own_keys, own_values, grad_attn, *slots, *kept)
@@ -332,50 +332,37 @@
     )(where, attn_t, *pieces, *far)
 
 
-def grad_weight_kernel(core, attn_t_ref, grad_ref, far_ref, near_ref):
-    step = pl.program_id(0)
-    part = mm(attn_t_ref[...], grad_ref[...])
-
-    @pl.when(step < 4)
-    def _():
-        far_ref[0] = part.astype(BF)
-
-    @pl.when(step >= 4)
-    def _():
-        near_ref[0] = part
-
-
-def grad_weight_rows(attn_t, grad_rows):
+def grad_weight_kernel(core, attn_t_ref, grad_ref, out_ref):
+    out_ref[0] = mm(attn_t_ref[...], grad_ref[...]).astype(out_ref.dtype)
+
+
+def grad_weight_half(core, attn_t, grad_rows, dtype):
     features, frames = attn_t.shape
     size = features // 8
-    core, z = lax.axis_index("core"), lax.axis_index("z")
-    far, near = pl.pallas_call(
+    return pl.pallas_call(
         grad_weight_kernel,
         grid_spec=pltpu.PrefetchScalarGridSpec(
             num_scalar_prefetch=1,
-            grid=(8,),
+            grid=(4,),
             in_specs=[
-                pl.BlockSpec(
-                    (size, frames),
-                    lambda i, c: (jnp.where(i < 4, 2 * i + 1 - c[0], 2 * (i - 4) + c[0]), 0),
-                ),
+                pl.BlockSpec((size, frames), lambda i, c: (2 * i + c[0], 0)),
                 pl.BlockSpec((frames, features), lambda i, c: (0, 0)),
             ],
-            out_specs=[
-                pl.BlockSpec((1, size, features), lambda i, c: (jnp.minimum(i, 3), 0, 0)),
-                pl.BlockSpec((1, size, features), lambda i, c: (jnp.maximum(i - 4, 0), 0, 0)),
-            ],
+            out_specs=pl.BlockSpec((1, size, features), lambda i, c: (i, 0, 0)),
         ),
-        out_shape=[
-            jax.ShapeDtypeStruct((4, size, features), BF),
-            jax.ShapeDtypeStruct((4, size, features), F32),
-        ],
+        out_shape=jax.ShapeDtypeStruct((4, size, features), dtype),
         compiler_params=pltpu.CompilerParams(vmem_limit_bytes=12 * MIB),
         cost_estimate=cost(0.1),
         name="grad_weight",
     )(core.reshape(1).astype(jnp.int32), attn_t, grad_rows)
+
+
+def grad_weight_rows(attn_t, grad_rows):
+    core = lax.axis_index("core")
+    far = grad_weight_half(1 - core, attn_t, grad_rows, BF)
+    near = grad_weight_half(core, attn_t, grad_rows, F32)
     total = near + shift(far, "core", 1).astype(F32)
-    return total.reshape(4 * size, features)
+    return total.reshape(-1, grad_rows.shape[1])
 
 
 def begin_sum(total, axis):

time: 170 us -> 167 us (0.982); the launches traced: 167 us -> 166 us
  waiting for transfers between devices: 57.5 us -> 51.3 us
  starting transfers between devices: 44.3 us -> 47.4 us
  Pallas kernels: 47.9 us -> 50.3 us
    ppermute x17, waiting for transfers between devices: 29.3 us -> 23.8 us  [shift(): return lax.ppermute(array, axis, [(i, (i + amount) % n) for i in range(n)])]
    pallas_call x1, Pallas kernels: 3.46 us -> 6.47 us  [fold_rows(): pl.pallas_call(fold_kernel, grid_spec=pltpu.PrefetchScalarGridSpec(num_sc...]
    ppermute x17, starting transfers between devices: 14.9 us -> 17.2 us  [shift(): return lax.ppermute(array, axis, [(i, (i + amount) % n) for i in range(n)])]
    pallas_call x1 -> x2, Pallas kernels: 4.28 us -> 2.29 us  [grad_weight_half(): pl.pallas_call(grad_weight_kernel, grid_spec=pltpu.PrefetchScalarGridSpec...]
    unnamed x66 -> x48, local copies, waits for them, and re-layouts: 7.78 us -> 6.4 us
  transfers between devices with their start and end apart: 38 -> 38, of which waited for: 14 -> 11; matrix products, arithmetic and copies ran while one was open for 3% -> 4% of each run, Pallas kernels for 18% -> 21%
where the time goes in v4:
time: 167 us; the launch traced here: 166 us
  waiting for transfers between devices  51.3 us (31%)
  Pallas kernels  50.3 us (30%)
  starting transfers between devices  47.4 us (28%)
  other arithmetic  7.95 us (5%)
  local copies, waits for them, and re-layouts  7.02 us (4%)
  between operations  1.95 us (1%)
    ppermute x21, starting transfers between devices, move(): return lax.ppermute(array, PLANE, pairs)  30.2 us
    ppermute x21, waiting for transfers between devices, move(): return lax.ppermute(array, PLANE, pairs)  27.5 us
    pallas_call x2, Pallas kernels, attend(): pl.pallas_call(attend_kernel, grid_spec=pltpu.PrefetchScalarGridSpec(num_...  25.7 us
    ppermute x17, waiting for transfers between devices, shift(): return lax.ppermute(array, axis, [(i, (i + amount) % n) for i in range(n)])  23.8 us
    ppermute x17, starting transfers between devices, shift(): return lax.ppermute(array, axis, [(i, (i + amount) % n) for i in range(n)])  17.2 us
    pallas_call x1, Pallas kernels, attended_rows(): pl.pallas_call(attended_kernel, grid_spec=pltpu.PrefetchScalarGridSpec(nu...  6.95 us
    pallas_call x1, Pallas kernels, fold_rows(): pl.pallas_call(fold_kernel, grid_spec=pltpu.PrefetchScalarGridSpec(num_sc...  6.47 us
    unnamed x48, local copies, waits for them, and re-layouts  6.4 us
  transfers between devices with their start and end apart: 38, of which 11 were waited for; matrix products, arithmetic and copies ran while one was open for 4% of the time, Pallas kernels for 21%

profile of v4, /device:TPU:32, one launch (start us, length us, event | category | flops | bytes accessed | tf_op | source)
XLA Modules:
  0.0 166.2 jit_solution(14315147307345628922)
XLA Ops:
  2.4 3.0 %collective-permute-start.2 = (bf16[16,1280]{1,0:T(8,128)(2,1)S(1)}, bf16[16,1280]{1,0:T(8,128)(2,1)S(1)}, u32[]{:S(2)}, u32[]{:S(2)}) collective-permute-start(bf16[16,1280]{1,0:T(8,128)(2,1)S(1)} %maximum_maximum_fusion), channel_id=1, source_target_pairs={{0,3},{1,0},{2,1},{3,2},{4,7},{5,4},{6,5},{7,6},{8,11},{9,8},{10,9... | collective-permute-start | bytes 122888 | tf_op jit(solution)/shard_map/ppermute | solution.py:36
  6.0 1.0 collective-permute-start
  7.0 1.5 collective-permute-start.3
  8.5 2.7 %collective-permute-start.4 = (bf16[2,2,64,1280]{3,2,1,0:T(8,128)(2,1)}, bf16[2,2,64,1280]{3,2,1,0:T(8,128)(2,1)S(1)}, u32[]{:S(2)}, u32[]{:S(2)}) collective-permute-start(bf16[2,2,64,1280]{3,2,1,0:T(8,128)(2,1)} %refs_0_.1), channel_id=1, source_target_pairs={{0,8},{1,9},{2,10},{3,11},{4,12},{5,13},{6,14},{7,15},{8,0},{9,1},... | collective-permute-start | bytes 1966088 | tf_op jit(solution)/shard_map/ppermute | solution.py:36
  12.5 1.5 collective-permute-start.5
  15.0 4.0 %collective-permute-done.3.refs_1_ = bf16[2,2,64,1280]{3,2,1,0:T(8,128)(2,1)S(1)} collective-permute-done((bf16[2,2,64,1280]{3,2,1,0:T(8,128)(2,1)}, bf16[2,2,64,1280]{3,2,1,0:T(8,128)(2,1)S(1)}, u32[]{:S(2)}, u32[]{:S(2)}) %collective-permute-start.3) | collective-permute-done | bytes 655392 | tf_op jit(solution)/shard_map/ppermute | solution.py:36
  19.0 1.5 collective-permute-start.11
  22.3 4.9 %collective-permute-done.4.refs_2_ = bf16[2,2,64,1280]{3,2,1,0:T(8,128)(2,1)S(1)} collective-permute-done((bf16[2,2,64,1280]{3,2,1,0:T(8,128)(2,1)}, bf16[2,2,64,1280]{3,2,1,0:T(8,128)(2,1)S(1)}, u32[]{:S(2)}, u32[]{:S(2)}) %collective-permute-start.4) | collective-permute-done | bytes 655392 | tf_op jit(solution)/shard_map/ppermute | solution.py:36
  27.1 1.1 copy-done.10
  28.2 3.2 %select_rows.1 = (bf16[4,2,64,1280]{3,2,1,0:T(8,128)(2,1)S(1)}, bf16[4,2,64,1280]{3,2,1,0:T(8,128)(2,1)S(1)}, bf16[4,2,64,1280]{3,2,1,0:T(8,128)(2,1)S(1)}, bf16[4,2,64,1280]{3,2,1,0:T(8,128)(2,1)}) custom-call(s32[16]{0:T(128)S(1)} %reshape.349.table, bf16[2,2,64,1280]{3,2,1,0:T(8,128)(2,1)S(1)} %copy-done.10, ...), custom_call_target="tpu_custom_call" | custom-call | flops 3449999872 | tf_op jit(solution)/shard_map/select_rows/pallas_call | solution.py:67
  31.4 1.9 %collective-permute-start.6 = (bf16[4,2,64,1280]{3,2,1,0:T(8,128)(2,1)S(1)}, bf16[4,2,64,1280]{3,2,1,0:T(8,128)(2,1)S(1)}, u32[]{:S(2)}, u32[]{:S(2)}) collective-permute-start(bf16[4,2,64,1280]{3,2,1,0:T(8,128)(2,1)S(1)} %get-tuple-element.37), channel_id=1, source_target_pairs={{0,1},{1,2},{2,3},{3,0},{4,5},{5,6},{6,7},{7,4},{8,9},{9,10},{10,1... | collective-permute-start | bytes 3932168 | tf_op jit(solution)/shard_map/ppermute | solution.py:36
  33.3 1.8 %collective-permute-start.7 = (bf16[4,2,64,1280]{3,2,1,0:T(8,128)(2,1)S(1)}, bf16[4,2,64,1280]{3,2,1,0:T(8,128)(2,1)S(1)}, u32[]{:S(2)}, u32[]{:S(2)}) collective-permute-start(bf16[4,2,64,1280]{3,2,1,0:T(8,128)(2,1)S(1)} %get-tuple-element.38), channel_id=1, source_target_pairs={{0,2},{1,3},{2,0},{3,1},{4,6},{5,7},{6,4},{7,5},{8,10},{9,11},{10,... | collective-permute-start | bytes 3932168 | tf_op jit(solution)/shard_map/ppermute | solution.py:36
  35.5 2.0 %collective-permute-start.12 = (bf16[160,1280]{1,0:T(8,128)(2,1)S(1)}, bf16[160,1280]{1,0:T(8,128)(2,1)S(1)}, u32[]{:S(2)}, u32[]{:S(2)}) collective-permute-start(bf16[160,1280]{1,0:T(8,128)(2,1)S(1)} %convolution_convert_fusion.refs_0_), channel_id=1, source_target_pairs={{0,32},{32,64},{64,96},{96,0},{1,33},{33,65},{65,97},{97,1},{2,34}... | collective-permute-start | bytes 1228808 | tf_op jit(solution)/shard_map/ppermute | solution.py:25
  37.5 0.9 collective-permute-start.8
  38.4 1.1 collective-permute-start.13
  39.6 14.2 %collective-permute-done.12.refs_1_ = bf16[160,1280]{1,0:T(8,128)(2,1)S(1)} collective-permute-done((bf16[160,1280]{1,0:T(8,128)(2,1)S(1)}, bf16[160,1280]{1,0:T(8,128)(2,1)S(1)}, u32[]{:S(2)}, u32[]{:S(2)}) %collective-permute-start.12) | collective-permute-done | bytes 409632 | tf_op jit(solution)/shard_map/ppermute | solution.py:25
  54.0 8.1 %collective-permute-done.14.refs_3_ = bf16[160,1280]{1,0:T(8,128)(2,1)S(1)} collective-permute-done((bf16[160,1280]{1,0:T(8,128)(2,1)S(1)}, bf16[160,1280]{1,0:T(8,128)(2,1)S(1)}, u32[]{:S(2)}, u32[]{:S(2)}) %collective-permute-start.14) | collective-permute-done | bytes 409632 | tf_op jit(solution)/shard_map/ppermute | solution.py:25
  62.7 2.1 %collective-permute-done.7.refs_2_ = bf16[4,2,64,1280]{3,2,1,0:T(8,128)(2,1)S(1)} collective-permute-done((bf16[4,2,64,1280]{3,2,1,0:T(8,128)(2,1)S(1)}, bf16[4,2,64,1280]{3,2,1,0:T(8,128)(2,1)S(1)}, u32[]{:S(2)}, u32[]{:S(2)}) %collective-permute-start.7) | collective-permute-done | bytes 1310752 | tf_op jit(solution)/shard_map/ppermute | solution.py:36
  64.8 1.1 copy-done.15
  67.3 3.2 %grad_attn.1.g_ref = bf16[1280,256]{1,0:T(8,128)(2,1)S(1)} custom-call(s32[9]{0:T(128)S(1)} %pad_add_fusion.3.meta, bf16[256,1280]{1,0:T(8,128)(2,1)S(1)} %bitcast.28, bf16[160,1280]{1,0:T(8,128)(2,1)S(1)} %convolution_convert_fusion.refs_0_, bf16[160,1280]{1,0:T(8,128)(2,1)S(1)} %collective-permute-done.12.refs_1_, ...), custom_call_target="tpu_custom_call" | custom-call | flops 4600000000 | tf_op jit(solution)/shard_map/grad_attn/pallas_call | solution.py:292
  71.5 10.9 %attend.2 = (bf16[1280,256]{1,0:T(8,128)(2,1)}, bf16[256,1280]{1,0:T(8,128)(2,1)}, bf16[256,1280]{1,0:T(8,128)(2,1)}, bf16[256,1280]{1,0:T(8,128)(2,1)}, bf16[4,...) custom-call(s32[17]{0:T(128)} %pad_add_fusion.2.meta, ...), custom_call_target="tpu_custom_call" | custom-call | flops 10579999744 | tf_op jit(solution)/shard_map/attend/pallas_call | solution.py:239
  82.3 0.9 collective-permute-start.19
  83.2 1.1 collective-permute-start.20
  84.4 1.3 collective-permute-start.21
  85.7 14.8 %attend.3 = (bf16[1280,256]{1,0:T(8,128)(2,1)}, bf16[256,1280]{1,0:T(8,128)(2,1)}, bf16[256,1280]{1,0:T(8,128)(2,1)}, bf16[256,1280]{1,0:T(8,128)(2,1)}, bf16[4,...) custom-call(s32[17]{0:T(128)} %pad_add_fusion.2.meta, ...), custom_call_target="tpu_custom_call", output_to_operand_aliasing={{0}: (9, {}), {1}: (10, {}), {2}: (11, {}), {3}: (12, {})} | custom-call | flops 15870000128 | tf_op jit(solution)/shard_map/attend/pallas_call | solution.py:239
  100.6 1.6 copy-done
  102.1 1.2 grad_weight.3
  103.6 2.0 %collective-permute-start.23 = (bf16[4,2,64,768]{3,2,1,0:T(8,128)(2,1)}, bf16[4,2,64,768]{3,2,1,0:T(8,128)(2,1)S(1)}, u32[]{:S(2)}, u32[]{:S(2)}) collective-permute-start(bf16[4,2,64,768]{3,2,1,0:T(8,128)(2,1)} %get-tuple-element.55), channel_id=1, source_target_pairs={{0,3},{1,0},{2,1},{3,2},{4,7},{5,4},{6,5},{7,6},{8,11},{9,8},{10,9... | collective-permute-start | bytes 2359304 | tf_op jit(solution)/shard_map/ppermute | solution.py:36
  105.6 1.3 collective-permute-start.24
  106.8 1.3 collective-permute-start.25
  108.2 1.1 grad_weight.2
  109.3 1.9 %convert_add_fusion = f32[4,160,1280]{2,1,0:T(8,128)S(1)} fusion(f32[4,160,1280]{2,1,0:T(8,128)S(1)} %grad_weight.2, bf16[4,160,1280]{2,1,0:T(8,128)(2,1)} %collective-permute-done.22), kind=kLoop, calls=%fused_computation | loop fusion | flops 1638400 | bytes 8192000 | tf_op jit(solution)/shard_map/add | solution.py:364
  111.4 3.0 %collective-permute-start.28 = (bf16[160,1280]{1,0:T(8,128)(2,1)S(1)}, bf16[160,1280]{1,0:T(8,128)(2,1)S(1)}, u32[]{:S(2)}, u32[]{:S(2)}) collective-permute-start(bf16[160,1280]{1,0:T(8,128)(2,1)S(1)} %get-tuple-element.69), channel_id=1, source_target_pairs={{0,64},{32,96},{64,0},{96,32},{1,65},{33,97},{65,1},{97,33},{2,66}... | collective-permute-start | bytes 1228808 | tf_op jit(solution)/shard_map/ppermute | solution.py:25
  114.4 1.0 collective-permute-start.27
  115.4 8.4 %collective-permute-done.23.refs_5_ = bf16[4,2,64,768]{3,2,1,0:T(8,128)(2,1)S(1)} collective-permute-done((bf16[4,2,64,768]{3,2,1,0:T(8,128)(2,1)}, bf16[4,2,64,768]{3,2,1,0:T(8,128)(2,1)S(1)}, u32[]{:S(2)}, u32[]{:S(2)}) %collective-permute-start.23) | collective-permute-done | bytes 786464 | tf_op jit(solution)/shard_map/ppermute | solution.py:36
  123.9 1.9 %collective-permute-start.26 = (bf16[160,1280]{1,0:T(8,128)(2,1)S(1)}, bf16[160,1280]{1,0:T(8,128)(2,1)S(1)}, u32[]{:S(2)}, u32[]{:S(2)}) collective-permute-start(bf16[160,1280]{1,0:T(8,128)(2,1)S(1)} %get-tuple-element.68), channel_id=1, source_target_pairs={{0,32},{32,64},{64,96},{96,0},{1,33},{33,65},{65,97},{97,1},{2,34}... | collective-permute-start | bytes 1228808 | tf_op jit(solution)/shard_map/ppermute | solution.py:25
  126.7 1.0 collective-permute-done.25.refs_7_
  128.6 6.5 %fold_rows.1 = (bf16[2,2,64,1280]{3,2,1,0:T(8,128)(2,1)}, bf16[2,2,64,1280]{3,2,1,0:T(8,128)(2,1)}, bf16[2,2,64,1280]{3,2,1,0:T(8,128)(2,1)}, bf16[2,2,64,1280]{3,2,1,0:T(8,128)(2,1)}) custom-call(s32[16]{0:T(128)} %copy-done.9, bf16[4,2,64,512]{3,2,1,0:T(8,128)(2,1)} %get-tuple-element.53.refs_0_, bf16[4,2,64,512]{3,2,1,0:T(8,128)(2,1)} %copy-done.21, ...), custom_call_target="tpu_custom_call" | custom-call | flops 4600000000 | tf_op jit(solution)/shard_map/fold_rows/pallas_call | solution.py:112
  135.7 2.6 %collective-permute-start.31 = (bf16[40,1280]{1,0:T(8,128)(2,1)S(1)}, bf16[40,1280]{1,0:T(8,128)(2,1)S(1)}, u32[]{:S(2)}, u32[]{:S(2)}) collective-permute-start(bf16[40,1280]{1,0:T(8,128)(2,1)S(1)} %get-tuple-element.72), channel_id=1, source_target_pairs={{0,8},{4,12},{8,0},{12,4},{1,9},{5,13},{9,1},{13,5},{2,10},{6,14},... | collective-permute-start | bytes 307208 | tf_op jit(solution)/shard_map/ppermute | solution.py:25
  138.3 2.0 %collective-permute-start.30 = (bf16[40,1280]{1,0:T(8,128)(2,1)S(1)}, bf16[40,1280]{1,0:T(8,128)(2,1)S(1)}, u32[]{:S(2)}, u32[]{:S(2)}) collective-permute-start(bf16[40,1280]{1,0:T(8,128)(2,1)S(1)} %get-tuple-element.73), channel_id=1, source_target_pairs={{0,12},{4,0},{8,4},{12,8},{1,13},{5,1},{9,5},{13,9},{2,14},{6,2},{... | collective-permute-start | bytes 307208 | tf_op jit(solution)/shard_map/ppermute | solution.py:25
  140.9 3.2 %collective-permute-start.32 = (bf16[2,2,64,1280]{3,2,1,0:T(8,128)(2,1)}, bf16[2,2,64,1280]{3,2,1,0:T(8,128)(2,1)S(1)}, u32[]{:S(2)}, u32[]{:S(2)}) collective-permute-start(bf16[2,2,64,1280]{3,2,1,0:T(8,128)(2,1)} %get-tuple-element.65), channel_id=1, source_target_pairs={{0,12},{1,13},{2,14},{3,15},{4,0},{5,1},{6,2},{7,3},{8,4},{9,5},{1... | collective-permute-start | bytes 1966088 | tf_op jit(solution)/shard_map/ppermute | solution.py:36
  145.0 1.2 collective-permute-done.29
  146.3 6.9 %attended.1 = bf16[256,1280]{1,0:T(8,128)(2,1)} custom-call(s32[8]{0:T(128)} %pad_add_fusion.1.where, bf16[1280,256]{1,0:T(8,128)(2,1)} %get-tuple-element.60.attn_t_ref, bf16[160,1280]{1,0:T(8,128)(2,1)} %copy-done.3, bf16[160,1280]{1,0:T(8,128)(2,1)} %copy-done.4, bf16[160,1280]{1,0:T(8,128)(2,1)} %copy-done.5, bf16[160,1280]{1,0:T(8,128)(2,1)} %copy-done.6, ...), custom_call_target="tpu_custom_call" | custom-call | flops 115000000 | tf_op jit(solution)/shard_map/attended/pallas_call | solution.py:319
  153.3 1.3 collective-permute-start.37
  154.6 1.4 collective-permute-start.36
  156.0 3.6 %collective-permute-done.32.refs_1_ = bf16[2,2,64,1280]{3,2,1,0:T(8,128)(2,1)S(1)} collective-permute-done((bf16[2,2,64,1280]{3,2,1,0:T(8,128)(2,1)}, bf16[2,2,64,1280]{3,2,1,0:T(8,128)(2,1)S(1)}, u32[]{:S(2)}, u32[]{:S(2)}) %collective-permute-start.32) | collective-permute-done | bytes 655392 | tf_op jit(solution)/shard_map/ppermute | solution.py:36
  159.6 3.5 %collective-permute-done.34.refs_3_ = bf16[2,2,64,1280]{3,2,1,0:T(8,128)(2,1)S(1)} collective-permute-done((bf16[2,2,64,1280]{3,2,1,0:T(8,128)(2,1)S(1)}, bf16[2,2,64,1280]{3,2,1,0:T(8,128)(2,1)S(1)}, u32[]{:S(2)}, u32[]{:S(2)}) %collective-permute-start.34) | collective-permute-done | bytes 655392 | tf_op jit(solution)/shard_map/ppermute | solution.py:36
  163.1 2.4 %total_rows.1 = f32[2,2,64,1280]{3,2,1,0:T(8,128)} custom-call(bf16[2,2,64,1280]{3,2,1,0:T(8,128)(2,1)S(1)} %copy-done.12, bf16[2,2,64,1280]{3,2,1,0:T(8,128)(2,1)S(1)} %collective-permute-done.32.refs_1_, bf16[2,2,64,1280]{3,2,1,0:T(8,128)(2,1)S(1)} %collective-permute-done.33.refs_2_, bf16[2,2,64,1280]{3,2,1,0:T(8,128)(2,1)S(1)} %collective-permute-done.34.refs_3_), custom_call_target="tpu_custom_call" | custom-call | flops 4600000000 | tf_op jit(solution)/shard_map/total_rows/pallas_call | solution.py:137
  (123 shorter events, 13.9 us)
Async XLA Ops:
  2.4 10.1 %collective-permute-start.2 = (bf16[16,1280]{1,0:T(8,128)(2,1)S(1)}, bf16[16,1280]{1,0:T(8,128)(2,1)S(1)}, u32[]{:S(2)}, u32[]{:S(2)}) collective-permute-start(bf16[16,1280]{1,0:T(8,128)(2,1)S(1)} %maximum_maximum_fusion), channel_id=1, source_target_pairs={{0,3},{1,0},{2,1},{3,2},{4,7},{5,4},{6,5},{7,6},{8,11},{9,8},{10,9... | collective-permute-start | bytes 122888 | tf_op jit(solution)/shard_map/ppermute | solution.py:36
  5.4 8.6 %collective-permute-start.1 = (bf16[16,1280]{1,0:T(8,128)(2,1)S(1)}, bf16[16,1280]{1,0:T(8,128)(2,1)S(1)}, u32[]{:S(2)}, u32[]{:S(2)}) collective-permute-start(bf16[16,1280]{1,0:T(8,128)(2,1)S(1)} %maximum_maximum_fusion), channel_id=1, source_target_pairs={{0,2},{1,3},{2,0},{3,1},{4,6},{5,7},{6,4},{7,5},{8,10},{9,11},{10,... | collective-permute-start | bytes 122888 | tf_op jit(solution)/shard_map/ppermute | solution.py:36
  6.0 7.9 %collective-permute-start = (bf16[16,1280]{1,0:T(8,128)(2,1)S(1)}, bf16[16,1280]{1,0:T(8,128)(2,1)S(1)}, u32[]{:S(2)}, u32[]{:S(2)}) collective-permute-start(bf16[16,1280]{1,0:T(8,128)(2,1)S(1)} %maximum_maximum_fusion), channel_id=1, source_target_pairs={{0,1},{1,2},{2,3},{3,0},{4,5},{5,6},{6,7},{7,4},{8,9},{9,10},{10,1... | collective-permute-start | bytes 122888 | tf_op jit(solution)/shard_map/ppermute | solution.py:36
  7.0 12.0 %collective-permute-start.3 = (bf16[2,2,64,1280]{3,2,1,0:T(8,128)(2,1)}, bf16[2,2,64,1280]{3,2,1,0:T(8,128)(2,1)S(1)}, u32[]{:S(2)}, u32[]{:S(2)}) collective-permute-start(bf16[2,2,64,1280]{3,2,1,0:T(8,128)(2,1)} %refs_0_.1), channel_id=1, source_target_pairs={{0,4},{1,5},{2,6},{3,7},{4,8},{5,9},{6,10},{7,11},{8,12},{9,13},{1... | collective-permute-start | bytes 1966088 | tf_op jit(solution)/shard_map/ppermute | solution.py:36
  8.5 18.6 %collective-permute-start.4 = (bf16[2,2,64,1280]{3,2,1,0:T(8,128)(2,1)}, bf16[2,2,64,1280]{3,2,1,0:T(8,128)(2,1)S(1)}, u32[]{:S(2)}, u32[]{:S(2)}) collective-permute-start(bf16[2,2,64,1280]{3,2,1,0:T(8,128)(2,1)} %refs_0_.1), channel_id=1, source_target_pairs={{0,8},{1,9},{2,10},{3,11},{4,12},{5,13},{6,14},{7,15},{8,0},{9,1},... | collective-permute-start | bytes 1966088 | tf_op jit(solution)/shard_map/ppermute | solution.py:36
  12.5 14.6 %collective-permute-start.5 = (bf16[2,2,64,1280]{3,2,1,0:T(8,128)(2,1)}, bf16[2,2,64,1280]{3,2,1,0:T(8,128)(2,1)S(1)}, u32[]{:S(2)}, u32[]{:S(2)}) collective-permute-start(bf16[2,2,64,1280]{3,2,1,0:T(8,128)(2,1)} %refs_0_.1), channel_id=1, source_target_pairs={{0,12},{1,13},{2,14},{3,15},{4,0},{5,1},{6,2},{7,3},{8,4},{9,5},{1... | collective-permute-start | bytes 1966088 | tf_op jit(solution)/shard_map/ppermute | solution.py:36
  15.0 16.4 %copy-start.9 = (s32[16]{0:T(128)}, s32[16]{0:T(128)S(1)}, u32[]{:S(2)}) copy-start(s32[16]{0:T(128)S(1)} %reshape.349.table) | copy-start | bytes 196
  19.0 16.1 %collective-permute-start.11 = (bf16[4,16,1280]{2,1,0:T(8,128)(2,1)S(1)}, bf16[4,16,1280]{2,1,0:T(8,128)(2,1)S(1)}, u32[]{:S(2)}, u32[]{:S(2)}) collective-permute-start(bf16[4,16,1280]{2,1,0:T(8,128)(2,1)S(1)} %pad_maximum_fusion.1), channel_id=1, source_target_pairs={{0,12},{1,13},{2,14},{3,15},{4,0},{5,1},{6,2},{7,3},{8,4},{9,5},{1... | collective-permute-start | bytes 491528 | tf_op jit(solution)/shard_map/ppermute | solution.py:36
  20.6 14.6 %collective-permute-start.10 = (bf16[4,16,1280]{2,1,0:T(8,128)(2,1)S(1)}, bf16[4,16,1280]{2,1,0:T(8,128)(2,1)S(1)}, u32[]{:S(2)}, u32[]{:S(2)}) collective-permute-start(bf16[4,16,1280]{2,1,0:T(8,128)(2,1)S(1)} %pad_maximum_fusion.1), channel_id=1, source_target_pairs={{0,8},{1,9},{2,10},{3,11},{4,12},{5,13},{6,14},{7,15},{8,0},{9,1},... | collective-permute-start | bytes 491528 | tf_op jit(solution)/shard_map/ppermute | solution.py:36
  21.4 13.8 %collective-permute-start.9 = (bf16[4,16,1280]{2,1,0:T(8,128)(2,1)S(1)}, bf16[4,16,1280]{2,1,0:T(8,128)(2,1)S(1)}, u32[]{:S(2)}, u32[]{:S(2)}) collective-permute-start(bf16[4,16,1280]{2,1,0:T(8,128)(2,1)S(1)} %pad_maximum_fusion.1), channel_id=1, source_target_pairs={{0,4},{1,5},{2,6},{3,7},{4,8},{5,9},{6,10},{7,11},{8,12},{9,13},{1... | collective-permute-start | bytes 491528 | tf_op jit(solution)/shard_map/ppermute | solution.py:36
  31.4 35.9 %copy-start.2 = (bf16[1,256,1280]{2,1,0:T(8,128)(2,1)S(1)}, bf16[1,256,1280]{2,1,0:T(8,128)(2,1)}, u32[]{:S(2)}) copy-start(bf16[1,256,1280]{2,1,0:T(8,128)(2,1)} %param.15) | copy-start | bytes 1966084
  31.4 30.8 %collective-permute-start.6 = (bf16[4,2,64,1280]{3,2,1,0:T(8,128)(2,1)S(1)}, bf16[4,2,64,1280]{3,2,1,0:T(8,128)(2,1)S(1)}, u32[]{:S(2)}, u32[]{:S(2)}) collective-permute-start(bf16[4,2,64,1280]{3,2,1,0:T(8,128)(2,1)S(1)} %get-tuple-element.37), channel_id=1, source_target_pairs={{0,1},{1,2},{2,3},{3,0},{4,5},{5,6},{6,7},{7,4},{8,9},{9,10},{10,1... | collective-permute-start | bytes 3932168 | tf_op jit(solution)/shard_map/ppermute | solution.py:36
  33.3 31.5 %collective-permute-start.7 = (bf16[4,2,64,1280]{3,2,1,0:T(8,128)(2,1)S(1)}, bf16[4,2,64,1280]{3,2,1,0:T(8,128)(2,1)S(1)}, u32[]{:S(2)}, u32[]{:S(2)}) collective-permute-start(bf16[4,2,64,1280]{3,2,1,0:T(8,128)(2,1)S(1)} %get-tuple-element.38), channel_id=1, source_target_pairs={{0,2},{1,3},{2,0},{3,1},{4,6},{5,7},{6,4},{7,5},{8,10},{9,11},{10,... | collective-permute-start | bytes 3932168 | tf_op jit(solution)/shard_map/ppermute | solution.py:36
  35.5 35.0 %copy-start.3 = (bf16[160,1280]{1,0:T(8,128)(2,1)}, bf16[160,1280]{1,0:T(8,128)(2,1)S(1)}, u32[]{:S(2)}) copy-start(bf16[160,1280]{1,0:T(8,128)(2,1)S(1)} %convolution_convert_fusion.refs_0_) | copy-start | bytes 1228804
  35.5 18.2 %collective-permute-start.12 = (bf16[160,1280]{1,0:T(8,128)(2,1)S(1)}, bf16[160,1280]{1,0:T(8,128)(2,1)S(1)}, u32[]{:S(2)}, u32[]{:S(2)}) collective-permute-start(bf16[160,1280]{1,0:T(8,128)(2,1)S(1)} %convolution_convert_fusion.refs_0_), channel_id=1, source_target_pairs={{0,32},{32,64},{64,96},{96,0},{1,33},{33,65},{65,97},{97,1},{2,34}... | collective-permute-start | bytes 1228808 | tf_op jit(solution)/shard_map/ppermute | solution.py:25
  37.5 29.7 %collective-permute-start.8 = (bf16[4,2,64,1280]{3,2,1,0:T(8,128)(2,1)}, bf16[4,2,64,1280]{3,2,1,0:T(8,128)(2,1)}, u32[]{:S(2)}, u32[]{:S(2)}) collective-permute-start(bf16[4,2,64,1280]{3,2,1,0:T(8,128)(2,1)} %get-tuple-element.39), channel_id=1, source_target_pairs={{0,3},{1,0},{2,1},{3,2},{4,7},{5,4},{6,5},{7,6},{8,11},{9,8},{10,9... | collective-permute-start | bytes 3932168 | tf_op jit(solution)/shard_map/ppermute | solution.py:36
  38.4 15.5 %collective-permute-start.13 = (bf16[160,1280]{1,0:T(8,128)(2,1)S(1)}, bf16[160,1280]{1,0:T(8,128)(2,1)S(1)}, u32[]{:S(2)}, u32[]{:S(2)}) collective-permute-start(bf16[160,1280]{1,0:T(8,128)(2,1)S(1)} %convolution_convert_fusion.refs_0_), channel_id=1, source_target_pairs={{0,64},{32,96},{64,0},{96,32},{1,65},{33,97},{65,1},{97,33},{2,66}... | collective-permute-start | bytes 1228808 | tf_op jit(solution)/shard_map/ppermute | solution.py:25
  53.8 16.8 %copy-start.4 = (bf16[160,1280]{1,0:T(8,128)(2,1)}, bf16[160,1280]{1,0:T(8,128)(2,1)S(1)}, u32[]{:S(2)}) copy-start(bf16[160,1280]{1,0:T(8,128)(2,1)S(1)} %collective-permute-done.12.refs_1_) | copy-start | bytes 1228804
  53.8 8.4 %collective-permute-start.14 = (bf16[160,1280]{1,0:T(8,128)(2,1)S(1)}, bf16[160,1280]{1,0:T(8,128)(2,1)S(1)}, u32[]{:S(2)}, u32[]{:S(2)}) collective-permute-start(bf16[160,1280]{1,0:T(8,128)(2,1)S(1)} %convolution_convert_fusion.refs_0_), channel_id=1, source_target_pairs={{0,96},{32,0},{64,32},{96,64},{1,97},{33,1},{65,33},{97,65},{2,98}... | collective-permute-start | bytes 1228808 | tf_op jit(solution)/shard_map/ppermute | solution.py:25
  53.9 16.6 %copy-start.5 = (bf16[160,1280]{1,0:T(8,128)(2,1)}, bf16[160,1280]{1,0:T(8,128)(2,1)S(1)}, u32[]{:S(2)}) copy-start(bf16[160,1280]{1,0:T(8,128)(2,1)S(1)} %collective-permute-done.13.refs_2_) | copy-start | bytes 1228804
  54.0 13.3 %collective-permute-start.15 = (bf16[160,1280]{1,0:T(8,128)(2,1)S(1)}, bf16[160,1280]{1,0:T(8,128)(2,1)S(1)}, u32[]{:S(2)}, u32[]{:S(2)}) collective-permute-start(bf16[160,1280]{1,0:T(8,128)(2,1)S(1)} %convolution_convert_fusion.refs_0_), channel_id=1, source_target_pairs={{0,16},{16,0},{1,17},{17,1},{2,18},{18,2},{3,19},{19,3},{4,20},{20... | collective-permute-start | bytes 1228808 | tf_op jit(solution)/shard_map/ppermute | solution.py:25
  62.1 8.4 %copy-start.6 = (bf16[160,1280]{1,0:T(8,128)(2,1)}, bf16[160,1280]{1,0:T(8,128)(2,1)S(1)}, u32[]{:S(2)}) copy-start(bf16[160,1280]{1,0:T(8,128)(2,1)S(1)} %collective-permute-done.14.refs_3_) | copy-start | bytes 1228804
  62.1 5.1 %collective-permute-start.16 = (bf16[160,1280]{1,0:T(8,128)(2,1)S(1)}, bf16[160,1280]{1,0:T(8,128)(2,1)S(1)}, u32[]{:S(2)}, u32[]{:S(2)}) collective-permute-start(bf16[160,1280]{1,0:T(8,128)(2,1)S(1)} %collective-permute-done.12.refs_1_), channel_id=1, source_target_pairs={{0,16},{16,0},{1,17},{17,1},{2,18},{18,2},{3,19},{19,3},{4,20},{20... | collective-permute-start | bytes 1228808 | tf_op jit(solution)/shard_map/ppermute | solution.py:25
  62.2 5.1 %collective-permute-start.17 = (bf16[160,1280]{1,0:T(8,128)(2,1)S(1)}, bf16[160,1280]{1,0:T(8,128)(2,1)}, u32[]{:S(2)}, u32[]{:S(2)}) collective-permute-start(bf16[160,1280]{1,0:T(8,128)(2,1)S(1)} %collective-permute-done.13.refs_2_), channel_id=1, source_target_pairs={{0,16},{16,0},{1,17},{17,1},{2,18},{18,2},{3,19},{19,3},{4,20},{20... | collective-permute-start | bytes 1228808 | tf_op jit(solution)/shard_map/ppermute | solution.py:25
  64.8 2.5 %collective-permute-start.18 = (bf16[160,1280]{1,0:T(8,128)(2,1)S(1)}, bf16[160,1280]{1,0:T(8,128)(2,1)}, u32[]{:S(2)}, u32[]{:S(2)}) collective-permute-start(bf16[160,1280]{1,0:T(8,128)(2,1)S(1)} %collective-permute-done.14.refs_3_), channel_id=1, source_target_pairs={{0,16},{16,0},{1,17},{17,1},{2,18},{18,2},{3,19},{19,3},{4,20},{20... | collective-permute-start | bytes 1228808 | tf_op jit(solution)/shard_map/ppermute | solution.py:25
  82.3 18.2 %collective-permute-start.19 = (bf16[4,2,64,512]{3,2,1,0:T(8,128)(2,1)}, bf16[4,2,64,512]{3,2,1,0:T(8,128)(2,1)S(1)}, u32[]{:S(2)}, u32[]{:S(2)}) collective-permute-start(bf16[4,2,64,512]{3,2,1,0:T(8,128)(2,1)} %get-tuple-element.49), channel_id=1, source_target_pairs={{0,3},{1,0},{2,1},{3,2},{4,7},{5,4},{6,5},{7,6},{8,11},{9,8},{10,9... | collective-permute-start | bytes 1572872 | tf_op jit(solution)/shard_map/ppermute | solution.py:36
  83.2 17.3 %collective-permute-start.20 = (bf16[4,2,64,512]{3,2,1,0:T(8,128)(2,1)}, bf16[4,2,64,512]{3,2,1,0:T(8,128)(2,1)S(1)}, u32[]{:S(2)}, u32[]{:S(2)}) collective-permute-start(bf16[4,2,64,512]{3,2,1,0:T(8,128)(2,1)} %get-tuple-element.50), channel_id=1, source_target_pairs={{0,2},{1,3},{2,0},{3,1},{4,6},{5,7},{6,4},{7,5},{8,10},{9,11},{10,... | collective-permute-start | bytes 1572872 | tf_op jit(solution)/shard_map/ppermute | solution.py:36
  84.4 16.2 %collective-permute-start.21 = (bf16[4,2,64,512]{3,2,1,0:T(8,128)(2,1)}, bf16[4,2,64,512]{3,2,1,0:T(8,128)(2,1)S(1)}, u32[]{:S(2)}, u32[]{:S(2)}) collective-permute-start(bf16[4,2,64,512]{3,2,1,0:T(8,128)(2,1)} %get-tuple-element.51), channel_id=1, source_target_pairs={{0,1},{1,2},{2,3},{3,0},{4,5},{5,6},{6,7},{7,4},{8,9},{9,10},{10,1... | collective-permute-start | bytes 1572872 | tf_op jit(solution)/shard_map/ppermute | solution.py:36
  102.1 6.0 %copy-start.1 = (bf16[1280,256]{1,0:T(8,128)(2,1)S(1)}, bf16[1280,256]{1,0:T(8,128)(2,1)}, u32[]{:S(2)}) copy-start(bf16[1280,256]{1,0:T(8,128)(2,1)} %get-tuple-element.60.attn_t_ref) | copy-start | bytes 1966084
  103.3 6.0 %collective-permute-start.22 = (bf16[4,160,1280]{2,1,0:T(8,128)(2,1)S(1)}, bf16[4,160,1280]{2,1,0:T(8,128)(2,1)}, u32[]{:S(2)}, u32[]{:S(2)}) collective-permute-start(bf16[4,160,1280]{2,1,0:T(8,128)(2,1)S(1)} %grad_weight.3), channel_id=1, source_target_pairs={{0,16},{16,0},{1,17},{17,1},{2,18},{18,2},{3,19},{19,3},{4,20},{20... | collective-permute-start | bytes 4915208 | tf_op jit(solution)/shard_map/ppermute | solution.py:25
  103.6 20.2 %collective-permute-start.23 = (bf16[4,2,64,768]{3,2,1,0:T(8,128)(2,1)}, bf16[4,2,64,768]{3,2,1,0:T(8,128)(2,1)S(1)}, u32[]{:S(2)}, u32[]{:S(2)}) collective-permute-start(bf16[4,2,64,768]{3,2,1,0:T(8,128)(2,1)} %get-tuple-element.55), channel_id=1, source_target_pairs={{0,3},{1,0},{2,1},{3,2},{4,7},{5,4},{6,5},{7,6},{8,11},{9,8},{10,9... | collective-permute-start | bytes 2359304 | tf_op jit(solution)/shard_map/ppermute | solution.py:36
  105.6 20.2 %collective-permute-start.24 = (bf16[4,2,64,768]{3,2,1,0:T(8,128)(2,1)}, bf16[4,2,64,768]{3,2,1,0:T(8,128)(2,1)S(1)}, u32[]{:S(2)}, u32[]{:S(2)}) collective-permute-start(bf16[4,2,64,768]{3,2,1,0:T(8,128)(2,1)} %get-tuple-element.56), channel_id=1, source_target_pairs={{0,2},{1,3},{2,0},{3,1},{4,6},{5,7},{6,4},{7,5},{8,10},{9,11},{10,... | collective-permute-start | bytes 2359304 | tf_op jit(solution)/shard_map/ppermute | solution.py:36
  106.8 20.9 %collective-permute-start.25 = (bf16[4,2,64,768]{3,2,1,0:T(8,128)(2,1)}, bf16[4,2,64,768]{3,2,1,0:T(8,128)(2,1)S(1)}, u32[]{:S(2)}, u32[]{:S(2)}) collective-permute-start(bf16[4,2,64,768]{3,2,1,0:T(8,128)(2,1)} %get-tuple-element.57), channel_id=1, source_target_pairs={{0,1},{1,2},{2,3},{3,0},{4,5},{5,6},{6,7},{7,4},{8,9},{9,10},{10,1... | collective-permute-start | bytes 2359304 | tf_op jit(solution)/shard_map/ppermute | solution.py:36
  111.4 23.8 %collective-permute-start.28 = (bf16[160,1280]{1,0:T(8,128)(2,1)S(1)}, bf16[160,1280]{1,0:T(8,128)(2,1)S(1)}, u32[]{:S(2)}, u32[]{:S(2)}) collective-permute-start(bf16[160,1280]{1,0:T(8,128)(2,1)S(1)} %get-tuple-element.69), channel_id=1, source_target_pairs={{0,64},{32,96},{64,0},{96,32},{1,65},{33,97},{65,1},{97,33},{2,66}... | collective-permute-start | bytes 1228808 | tf_op jit(solution)/shard_map/ppermute | solution.py:25
  114.4 20.8 %collective-permute-start.27 = (bf16[160,1280]{1,0:T(8,128)(2,1)S(1)}, bf16[160,1280]{1,0:T(8,128)(2,1)S(1)}, u32[]{:S(2)}, u32[]{:S(2)}) collective-permute-start(bf16[160,1280]{1,0:T(8,128)(2,1)S(1)} %get-tuple-element.70), channel_id=1, source_target_pairs={{0,96},{32,0},{64,32},{96,64},{1,97},{33,1},{65,33},{97,65},{2,98}... | collective-permute-start | bytes 1228808 | tf_op jit(solution)/shard_map/ppermute | solution.py:25
  123.9 11.6 %collective-permute-start.26 = (bf16[160,1280]{1,0:T(8,128)(2,1)S(1)}, bf16[160,1280]{1,0:T(8,128)(2,1)S(1)}, u32[]{:S(2)}, u32[]{:S(2)}) collective-permute-start(bf16[160,1280]{1,0:T(8,128)(2,1)S(1)} %get-tuple-element.68), channel_id=1, source_target_pairs={{0,32},{32,64},{64,96},{96,0},{1,33},{33,65},{65,97},{97,1},{2,34}... | collective-permute-start | bytes 1228808 | tf_op jit(solution)/shard_map/ppermute | solution.py:25
  135.1 9.0 %copy-start.20 = (bf16[2,2,64,1280]{3,2,1,0:T(8,128)(2,1)S(1)}, bf16[2,2,64,1280]{3,2,1,0:T(8,128)(2,1)}, u32[]{:S(2)}) copy-start(bf16[2,2,64,1280]{3,2,1,0:T(8,128)(2,1)} %get-tuple-element.66) | copy-start | bytes 1966084
  135.1 9.0 %copy-start.19 = (bf16[2,2,64,1280]{3,2,1,0:T(8,128)(2,1)S(1)}, bf16[2,2,64,1280]{3,2,1,0:T(8,128)(2,1)}, u32[]{:S(2)}) copy-start(bf16[2,2,64,1280]{3,2,1,0:T(8,128)(2,1)} %get-tuple-element.67) | copy-start | bytes 1966084
  135.7 8.5 %collective-permute-start.31 = (bf16[40,1280]{1,0:T(8,128)(2,1)S(1)}, bf16[40,1280]{1,0:T(8,128)(2,1)S(1)}, u32[]{:S(2)}, u32[]{:S(2)}) collective-permute-start(bf16[40,1280]{1,0:T(8,128)(2,1)S(1)} %get-tuple-element.72), channel_id=1, source_target_pairs={{0,8},{4,12},{8,0},{12,4},{1,9},{5,13},{9,1},{13,5},{2,10},{6,14},... | collective-permute-start | bytes 307208 | tf_op jit(solution)/shard_map/ppermute | solution.py:25
  138.3 6.7 %collective-permute-start.30 = (bf16[40,1280]{1,0:T(8,128)(2,1)S(1)}, bf16[40,1280]{1,0:T(8,128)(2,1)S(1)}, u32[]{:S(2)}, u32[]{:S(2)}) collective-permute-start(bf16[40,1280]{1,0:T(8,128)(2,1)S(1)} %get-tuple-element.73), channel_id=1, source_target_pairs={{0,12},{4,0},{8,4},{12,8},{1,13},{5,1},{9,5},{13,9},{2,14},{6,2},{... | collective-permute-start | bytes 307208 | tf_op jit(solution)/shard_map/ppermute | solution.py:25
  140.3 5.9 %collective-permute-start.29 = (bf16[40,1280]{1,0:T(8,128)(2,1)S(1)}, bf16[40,1280]{1,0:T(8,128)(2,1)S(1)}, u32[]{:S(2)}, u32[]{:S(2)}) collective-permute-start(bf16[40,1280]{1,0:T(8,128)(2,1)S(1)} %get-tuple-element.71), channel_id=1, source_target_pairs={{0,4},{4,8},{8,12},{12,0},{1,5},{5,9},{9,13},{13,1},{2,6},{6,10},{... | collective-permute-start | bytes 307208 | tf_op jit(solution)/shard_map/ppermute | solution.py:25
  140.9 18.7 %collective-permute-start.32 = (bf16[2,2,64,1280]{3,2,1,0:T(8,128)(2,1)}, bf16[2,2,64,1280]{3,2,1,0:T(8,128)(2,1)S(1)}, u32[]{:S(2)}, u32[]{:S(2)}) collective-permute-start(bf16[2,2,64,1280]{3,2,1,0:T(8,128)(2,1)} %get-tuple-element.65), channel_id=1, source_target_pairs={{0,12},{1,13},{2,14},{3,15},{4,0},{5,1},{6,2},{7,3},{8,4},{9,5},{1... | collective-permute-start | bytes 1966088 | tf_op jit(solution)/shard_map/ppermute | solution.py:36
  144.2 15.4 %collective-permute-start.33 = (bf16[2,2,64,1280]{3,2,1,0:T(8,128)(2,1)S(1)}, bf16[2,2,64,1280]{3,2,1,0:T(8,128)(2,1)S(1)}, u32[]{:S(2)}, u32[]{:S(2)}) collective-permute-start(bf16[2,2,64,1280]{3,2,1,0:T(8,128)(2,1)S(1)} %copy-done.20), channel_id=1, source_target_pairs={{0,8},{1,9},{2,10},{3,11},{4,12},{5,13},{6,14},{7,15},{8,0},{9,1},... | collective-permute-start | bytes 1966088 | tf_op jit(solution)/shard_map/ppermute | solution.py:36
  144.2 18.9 %collective-permute-start.34 = (bf16[2,2,64,1280]{3,2,1,0:T(8,128)(2,1)S(1)}, bf16[2,2,64,1280]{3,2,1,0:T(8,128)(2,1)S(1)}, u32[]{:S(2)}, u32[]{:S(2)}) collective-permute-start(bf16[2,2,64,1280]{3,2,1,0:T(8,128)(2,1)S(1)} %copy-done.19), channel_id=1, source_target_pairs={{0,4},{1,5},{2,6},{3,7},{4,8},{5,9},{6,10},{7,11},{8,12},{9,13},{1... | collective-permute-start | bytes 1966088 | tf_op jit(solution)/shard_map/ppermute | solution.py:36
  146.3 16.8 %copy-start.12 = (bf16[2,2,64,1280]{3,2,1,0:T(8,128)(2,1)S(1)}, bf16[2,2,64,1280]{3,2,1,0:T(8,128)(2,1)}, u32[]{:S(2)}) copy-start(bf16[2,2,64,1280]{3,2,1,0:T(8,128)(2,1)} %get-tuple-element.64.refs_0_) | copy-start | bytes 1966084
  153.3 12.3 %collective-permute-start.37 = (bf16[10,1280]{1,0:T(8,128)(2,1)S(1)}, bf16[10,1280]{1,0:T(8,128)(2,1)S(1)}, u32[]{:S(2)}, u32[]{:S(2)}) collective-permute-start(bf16[10,1280]{1,0:T(8,128)(2,1)S(1)} %get-tuple-element.75), channel_id=1, source_target_pairs={{0,2},{1,3},{2,0},{3,1},{4,6},{5,7},{6,4},{7,5},{8,10},{9,11},{10,... | collective-permute-start | bytes 76808 | tf_op jit(solution)/shard_map/ppermute | solution.py:25
  154.6 10.9 %collective-permute-start.36 = (bf16[10,1280]{1,0:T(8,128)(2,1)S(1)}, bf16[10,1280]{1,0:T(8,128)(2,1)S(1)}, u32[]{:S(2)}, u32[]{:S(2)}) collective-permute-start(bf16[10,1280]{1,0:T(8,128)(2,1)S(1)} %get-tuple-element.76), channel_id=1, source_target_pairs={{0,3},{1,0},{2,1},{3,2},{4,7},{5,4},{6,5},{7,6},{8,11},{9,8},{10,9... | collective-permute-start | bytes 76808 | tf_op jit(solution)/shard_map/ppermute | solution.py:25
  159.6 5.9 %collective-permute-start.35 = (bf16[10,1280]{1,0:T(8,128)(2,1)S(1)}, bf16[10,1280]{1,0:T(8,128)(2,1)S(1)}, u32[]{:S(2)}, u32[]{:S(2)}) collective-permute-start(bf16[10,1280]{1,0:T(8,128)(2,1)S(1)} %get-tuple-element.74), channel_id=1, source_target_pairs={{0,1},{1,2},{2,3},{3,0},{4,5},{5,6},{6,7},{7,4},{8,9},{9,10},{10,1... | collective-permute-start | bytes 76808 | tf_op jit(solution)/shard_map/ppermute | solution.py:25
  (14 other events, 30.1 us)

commit v5 on v4

--- a/solution.py
+++ b/solution.py
@@ -351,7 +351,7 @@
             out_specs=pl.BlockSpec((1, size, features), lambda i, c: (i, 0, 0)),
         ),
         out_shape=jax.ShapeDtypeStruct((4, size, features), dtype),
-        compiler_params=pltpu.CompilerParams(vmem_limit_bytes=12 * MIB),
+        compiler_params=pltpu.CompilerParams(vmem_limit_bytes=58 * MIB),
         cost_estimate=cost(0.1),
         name="grad_weight",
     )(core.reshape(1).astype(jnp.int32), attn_t, grad_rows)

time: 167 us -> 172 us (1.030)
  Pallas kernels: 50.3 us -> 56.6 us
  local copies, waits for them, and re-layouts: 7.02 us -> 4.42 us
    pallas_call x2, Pallas kernels: 2.29 us -> 8.63 us  [grad_weight_half(): pl.pallas_call(grad_weight_kernel, grid_spec=pltpu.PrefetchScalarGridSpec...]
    ppermute x21, waiting for transfers between devices: 27.5 us -> 23.9 us  [move(): return lax.ppermute(array, PLANE, pairs)]
    unnamed x48 -> x38, local copies, waits for them, and re-layouts: 6.4 us -> 3.81 us
    ppermute x17, waiting for transfers between devices: 23.8 us -> 25.7 us  [shift(): return lax.ppermute(array, axis, [(i, (i + amount) % n) for i in range(n)])]
  transfers between devices with their start and end apart: 38 -> 38, of which waited for: 11 -> 12; matrix products, arithmetic and copies ran while one was open for 4% -> 4% of each run, Pallas kernels for 21% -> 23%
where the time goes in v5:
time: 172 us; the launch traced here: 170 us
  Pallas kernels  56.6 us (33%)
  waiting for transfers between devices  49.6 us (29%)
  starting transfers between devices  48.7 us (28%)
  other arithmetic  8.26 us (5%)
  local copies, waits for them, and re-layouts  4.42 us (3%)
  between operations  1.8 us (1%)
    ppermute x21, starting transfers between devices, move(): return lax.ppermute(array, PLANE, pairs)  30.2 us
    pallas_call x2, Pallas kernels, attend(): pl.pallas_call(attend_kernel, grid_spec=pltpu.PrefetchScalarGridSpec(num_...  25.7 us
    ppermute x17, waiting for transfers between devices, shift(): return lax.ppermute(array, axis, [(i, (i + amount) % n) for i in range(n)])  25.7 us
    ppermute x21, waiting for transfers between devices, move(): return lax.ppermute(array, PLANE, pairs)  23.9 us
    ppermute x17, starting transfers between devices, shift(): return lax.ppermute(array, axis, [(i, (i + amount) % n) for i in range(n)])  18.5 us
    pallas_call x2, Pallas kernels, grad_weight_half(): pl.pallas_call(grad_weight_kernel, grid_spec=pltpu.PrefetchScalarGridSpec...  8.63 us
    pallas_call x1, Pallas kernels, attended_rows(): pl.pallas_call(attended_kernel, grid_spec=pltpu.PrefetchScalarGridSpec(nu...  6.94 us
    pallas_call x1, Pallas kernels, fold_rows(): pl.pallas_call(fold_kernel, grid_spec=pltpu.PrefetchScalarGridSpec(num_sc...  6.55 us
  transfers between devices with their start and end apart: 38, of which 12 were waited for; matrix products, arithmetic and copies ran while one was open for 4% of the time, Pallas kernels for 23%

profile of v5, /device:TPU:32, one launch (start us, length us, event | category | flops | bytes accessed | tf_op | source)
XLA Modules:
  0.0 169.6 jit_solution(7315132890427789278)
XLA Ops:
  2.4 3.0 %collective-permute-start.2 = (bf16[16,1280]{1,0:T(8,128)(2,1)S(1)}, bf16[16,1280]{1,0:T(8,128)(2,1)S(1)}, u32[]{:S(2)}, u32[]{:S(2)}) collective-permute-start(bf16[16,1280]{1,0:T(8,128)(2,1)S(1)} %maximum_maximum_fusion), channel_id=1, source_target_pairs={{0,3},{1,0},{2,1},{3,2},{4,7},{5,4},{6,5},{7,6},{8,11},{9,8},{10,9... | collective-permute-start | bytes 122888 | tf_op jit(solution)/shard_map/ppermute | solution.py:36
  6.0 1.0 collective-permute-start
  7.0 1.5 collective-permute-start.3
  8.5 2.7 %collective-permute-start.4 = (bf16[2,2,64,1280]{3,2,1,0:T(8,128)(2,1)}, bf16[2,2,64,1280]{3,2,1,0:T(8,128)(2,1)S(1)}, u32[]{:S(2)}, u32[]{:S(2)}) collective-permute-start(bf16[2,2,64,1280]{3,2,1,0:T(8,128)(2,1)} %refs_0_.1), channel_id=1, source_target_pairs={{0,8},{1,9},{2,10},{3,11},{4,12},{5,13},{6,14},{7,15},{8,0},{9,1},... | collective-permute-start | bytes 1966088 | tf_op jit(solution)/shard_map/ppermute | solution.py:36
  12.5 1.5 collective-permute-start.5
  15.0 4.0 %collective-permute-done.3.refs_1_ = bf16[2,2,64,1280]{3,2,1,0:T(8,128)(2,1)S(1)} collective-permute-done((bf16[2,2,64,1280]{3,2,1,0:T(8,128)(2,1)}, bf16[2,2,64,1280]{3,2,1,0:T(8,128)(2,1)S(1)}, u32[]{:S(2)}, u32[]{:S(2)}) %collective-permute-start.3) | collective-permute-done | bytes 655392 | tf_op jit(solution)/shard_map/ppermute | solution.py:36
  19.0 1.5 collective-permute-start.11
  21.4 0.9 collective-permute-start.9
  22.3 4.9 %collective-permute-done.4.refs_2_ = bf16[2,2,64,1280]{3,2,1,0:T(8,128)(2,1)S(1)} collective-permute-done((bf16[2,2,64,1280]{3,2,1,0:T(8,128)(2,1)}, bf16[2,2,64,1280]{3,2,1,0:T(8,128)(2,1)S(1)}, u32[]{:S(2)}, u32[]{:S(2)}) %collective-permute-start.4) | collective-permute-done | bytes 655392 | tf_op jit(solution)/shard_map/ppermute | solution.py:36
  27.1 1.1 copy-done.9
  28.2 3.2 %select_rows.1 = (bf16[4,2,64,1280]{3,2,1,0:T(8,128)(2,1)S(1)}, bf16[4,2,64,1280]{3,2,1,0:T(8,128)(2,1)S(1)}, bf16[4,2,64,1280]{3,2,1,0:T(8,128)(2,1)S(1)}, bf16[4,2,64,1280]{3,2,1,0:T(8,128)(2,1)}) custom-call(s32[16]{0:T(128)S(1)} %reshape.349.table, bf16[2,2,64,1280]{3,2,1,0:T(8,128)(2,1)S(1)} %copy-done.9, ...), custom_call_target="tpu_custom_call" | custom-call | flops 3449999872 | tf_op jit(solution)/shard_map/select_rows/pallas_call | solution.py:67
  31.4 1.9 %collective-permute-start.6 = (bf16[4,2,64,1280]{3,2,1,0:T(8,128)(2,1)S(1)}, bf16[4,2,64,1280]{3,2,1,0:T(8,128)(2,1)S(1)}, u32[]{:S(2)}, u32[]{:S(2)}) collective-permute-start(bf16[4,2,64,1280]{3,2,1,0:T(8,128)(2,1)S(1)} %get-tuple-element.37), channel_id=1, source_target_pairs={{0,1},{1,2},{2,3},{3,0},{4,5},{5,6},{6,7},{7,4},{8,9},{9,10},{10,1... | collective-permute-start | bytes 3932168 | tf_op jit(solution)/shard_map/ppermute | solution.py:36
  33.3 1.8 %collective-permute-start.7 = (bf16[4,2,64,1280]{3,2,1,0:T(8,128)(2,1)S(1)}, bf16[4,2,64,1280]{3,2,1,0:T(8,128)(2,1)S(1)}, u32[]{:S(2)}, u32[]{:S(2)}) collective-permute-start(bf16[4,2,64,1280]{3,2,1,0:T(8,128)(2,1)S(1)} %get-tuple-element.38), channel_id=1, source_target_pairs={{0,2},{1,3},{2,0},{3,1},{4,6},{5,7},{6,4},{7,5},{8,10},{9,11},{10,... | collective-permute-start | bytes 3932168 | tf_op jit(solution)/shard_map/ppermute | solution.py:36
  35.5 2.0 %collective-permute-start.12 = (bf16[160,1280]{1,0:T(8,128)(2,1)S(1)}, bf16[160,1280]{1,0:T(8,128)(2,1)S(1)}, u32[]{:S(2)}, u32[]{:S(2)}) collective-permute-start(bf16[160,1280]{1,0:T(8,128)(2,1)S(1)} %convolution_convert_fusion.refs_0_), channel_id=1, source_target_pairs={{0,32},{32,64},{64,96},{96,0},{1,33},{33,65},{65,97},{97,1},{2,34}... | collective-permute-start | bytes 1228808 | tf_op jit(solution)/shard_map/ppermute | solution.py:25
  37.5 0.9 collective-permute-start.8
  38.4 1.1 collective-permute-start.13
  39.6 14.2 %collective-permute-done.12.refs_1_ = bf16[160,1280]{1,0:T(8,128)(2,1)S(1)} collective-permute-done((bf16[160,1280]{1,0:T(8,128)(2,1)S(1)}, bf16[160,1280]{1,0:T(8,128)(2,1)S(1)}, u32[]{:S(2)}, u32[]{:S(2)}) %collective-permute-start.12) | collective-permute-done | bytes 409632 | tf_op jit(solution)/shard_map/ppermute | solution.py:25
  54.0 8.1 %collective-permute-done.14.refs_3_ = bf16[160,1280]{1,0:T(8,128)(2,1)S(1)} collective-permute-done((bf16[160,1280]{1,0:T(8,128)(2,1)S(1)}, bf16[160,1280]{1,0:T(8,128)(2,1)S(1)}, u32[]{:S(2)}, u32[]{:S(2)}) %collective-permute-start.14) | collective-permute-done | bytes 409632 | tf_op jit(solution)/shard_map/ppermute | solution.py:25
  62.7 2.1 %collective-permute-done.7.refs_2_ = bf16[4,2,64,1280]{3,2,1,0:T(8,128)(2,1)S(1)} collective-permute-done((bf16[4,2,64,1280]{3,2,1,0:T(8,128)(2,1)S(1)}, bf16[4,2,64,1280]{3,2,1,0:T(8,128)(2,1)S(1)}, u32[]{:S(2)}, u32[]{:S(2)}) %collective-permute-start.7) | collective-permute-done | bytes 1310752 | tf_op jit(solution)/shard_map/ppermute | solution.py:36
  64.8 1.1 copy-done.14
  67.3 3.2 %grad_attn.1.g_ref = bf16[1280,256]{1,0:T(8,128)(2,1)S(1)} custom-call(s32[9]{0:T(128)S(1)} %pad_add_fusion.3.meta, bf16[256,1280]{1,0:T(8,128)(2,1)S(1)} %bitcast.30, bf16[160,1280]{1,0:T(8,128)(2,1)S(1)} %convolution_convert_fusion.refs_0_, bf16[160,1280]{1,0:T(8,128)(2,1)S(1)} %collective-permute-done.12.refs_1_, ...), custom_call_target="tpu_custom_call" | custom-call | flops 4600000000 | tf_op jit(solution)/shard_map/grad_attn/pallas_call | solution.py:292
  71.4 10.9 %attend.2 = (bf16[1280,256]{1,0:T(8,128)(2,1)}, bf16[256,1280]{1,0:T(8,128)(2,1)}, bf16[256,1280]{1,0:T(8,128)(2,1)}, bf16[256,1280]{1,0:T(8,128)(2,1)}, bf16[4,...) custom-call(s32[17]{0:T(128)} %pad_add_fusion.2.meta, ...), custom_call_target="tpu_custom_call" | custom-call | flops 10579999744 | tf_op jit(solution)/shard_map/attend/pallas_call | solution.py:239
  82.3 0.9 collective-permute-start.19
  83.2 1.1 collective-permute-start.20
  84.3 1.3 collective-permute-start.21
  85.6 14.8 %attend.3 = (bf16[1280,256]{1,0:T(8,128)(2,1)}, bf16[256,1280]{1,0:T(8,128)(2,1)}, bf16[256,1280]{1,0:T(8,128)(2,1)}, bf16[256,1280]{1,0:T(8,128)(2,1)}, bf16[4,...) custom-call(s32[17]{0:T(128)} %pad_add_fusion.2.meta, ...), custom_call_target="tpu_custom_call", output_to_operand_aliasing={{0}: (9, {}), {1}: (10, {}), {2}: (11, {}), {3}: (12, {})} | custom-call | flops 15870000128 | tf_op jit(solution)/shard_map/attend/pallas_call | solution.py:239
  101.2 4.2 %grad_weight.3 = bf16[4,160,1280]{2,1,0:T(8,128)(2,1)} custom-call(s32[1]{0:T(128)} %bitcast.15.core, bf16[1280,256]{1,0:T(8,128)(2,1)} %get-tuple-element.60.attn_t_ref, bf16[256,1280]{1,0:T(8,128)(2,1)} %bitcast.28), custom_call_target="tpu_custom_call" | custom-call | flops 115000000 | tf_op jit(solution)/shard_map/grad_weight/pallas_call | solution.py:342
  105.6 2.0 %collective-permute-start.23 = (bf16[4,2,64,768]{3,2,1,0:T(8,128)(2,1)S(1)}, bf16[4,2,64,768]{3,2,1,0:T(8,128)(2,1)}, u32[]{:S(2)}, u32[]{:S(2)}) collective-permute-start(bf16[4,2,64,768]{3,2,1,0:T(8,128)(2,1)S(1)} %copy-done.15), channel_id=1, source_target_pairs={{0,3},{1,0},{2,1},{3,2},{4,7},{5,4},{6,5},{7,6},{8,11},{9,8},{10,9... | collective-permute-start | bytes 2359304 | tf_op jit(solution)/shard_map/ppermute | solution.py:36
  107.6 1.2 collective-permute-start.24
  108.8 1.3 collective-permute-start.25
  110.1 4.4 %grad_weight.2 = f32[4,160,1280]{2,1,0:T(8,128)} custom-call(s32[1]{0:T(128)} %bitcast.14.core, bf16[1280,256]{1,0:T(8,128)(2,1)} %get-tuple-element.60.attn_t_ref, bf16[256,1280]{1,0:T(8,128)(2,1)} %bitcast.29), custom_call_target="tpu_custom_call" | custom-call | flops 115000000 | tf_op jit(solution)/shard_map/grad_weight/pallas_call | solution.py:342
  114.6 2.2 %convert_add_fusion = f32[4,160,1280]{2,1,0:T(8,128)S(1)} fusion(f32[4,160,1280]{2,1,0:T(8,128)} %grad_weight.2, bf16[4,160,1280]{2,1,0:T(8,128)(2,1)S(1)} %collective-permute-done.22), kind=kLoop, calls=%fused_computation | loop fusion | flops 1638400 | bytes 8192000 | tf_op jit(solution)/shard_map/add | solution.py:364
  117.0 3.1 %collective-permute-start.28 = (bf16[160,1280]{1,0:T(8,128)(2,1)S(1)}, bf16[160,1280]{1,0:T(8,128)(2,1)S(1)}, u32[]{:S(2)}, u32[]{:S(2)}) collective-permute-start(bf16[160,1280]{1,0:T(8,128)(2,1)S(1)} %get-tuple-element.69), channel_id=1, source_target_pairs={{0,64},{32,96},{64,0},{96,32},{1,65},{33,97},{65,1},{97,33},{2,66}... | collective-permute-start | bytes 1228808 | tf_op jit(solution)/shard_map/ppermute | solution.py:25
  120.0 1.0 collective-permute-start.27
  121.0 4.5 %collective-permute-done.23.refs_5_ = bf16[4,2,64,768]{3,2,1,0:T(8,128)(2,1)} collective-permute-done((bf16[4,2,64,768]{3,2,1,0:T(8,128)(2,1)S(1)}, bf16[4,2,64,768]{3,2,1,0:T(8,128)(2,1)}, u32[]{:S(2)}, u32[]{:S(2)}) %collective-permute-start.23) | collective-permute-done | bytes 786464 | tf_op jit(solution)/shard_map/ppermute | solution.py:36
  125.6 1.9 %collective-permute-start.26 = (bf16[160,1280]{1,0:T(8,128)(2,1)S(1)}, bf16[160,1280]{1,0:T(8,128)(2,1)S(1)}, u32[]{:S(2)}, u32[]{:S(2)}) collective-permute-start(bf16[160,1280]{1,0:T(8,128)(2,1)S(1)} %get-tuple-element.68), channel_id=1, source_target_pairs={{0,32},{32,64},{64,96},{96,0},{1,33},{33,65},{65,97},{97,1},{2,34}... | collective-permute-start | bytes 1228808 | tf_op jit(solution)/shard_map/ppermute | solution.py:25
  127.5 2.4 %collective-permute-done.25.refs_7_ = bf16[4,2,64,768]{3,2,1,0:T(8,128)(2,1)} collective-permute-done((bf16[4,2,64,768]{3,2,1,0:T(8,128)(2,1)}, bf16[4,2,64,768]{3,2,1,0:T(8,128)(2,1)}, u32[]{:S(2)}, u32[]{:S(2)}) %collective-permute-start.25) | collective-permute-done | bytes 786464 | tf_op jit(solution)/shard_map/ppermute | solution.py:36
  129.8 6.6 %fold_rows.1 = (bf16[2,2,64,1280]{3,2,1,0:T(8,128)(2,1)}, bf16[2,2,64,1280]{3,2,1,0:T(8,128)(2,1)}, bf16[2,2,64,1280]{3,2,1,0:T(8,128)(2,1)}, bf16[2,2,64,1280]{3,2,1,0:T(8,128)(2,1)}) custom-call(s32[16]{0:T(128)} %copy-done.8, bf16[4,2,64,512]{3,2,1,0:T(8,128)(2,1)} %get-tuple-element.53.refs_0_, bf16[4,2,64,512]{3,2,1,0:T(8,128)(2,1)} %copy-done.16, ...), custom_call_target="tpu_custom_call" | custom-call | flops 4600000000 | tf_op jit(solution)/shard_map/fold_rows/pallas_call | solution.py:112
  136.5 1.7 %collective-permute-done.27 = bf16[160,1280]{1,0:T(8,128)(2,1)S(1)} collective-permute-done((bf16[160,1280]{1,0:T(8,128)(2,1)S(1)}, bf16[160,1280]{1,0:T(8,128)(2,1)S(1)}, u32[]{:S(2)}, u32[]{:S(2)}) %collective-permute-start.27) | collective-permute-done | bytes 409632 | tf_op jit(solution)/shard_map/ppermute | solution.py:25
  138.9 2.2 %collective-permute-start.31 = (bf16[40,1280]{1,0:T(8,128)(2,1)S(1)}, bf16[40,1280]{1,0:T(8,128)(2,1)S(1)}, u32[]{:S(2)}, u32[]{:S(2)}) collective-permute-start(bf16[40,1280]{1,0:T(8,128)(2,1)S(1)} %get-tuple-element.72), channel_id=1, source_target_pairs={{0,8},{4,12},{8,0},{12,4},{1,9},{5,13},{9,1},{13,5},{2,10},{6,14},... | collective-permute-start | bytes 307208 | tf_op jit(solution)/shard_map/ppermute | solution.py:25
  141.0 2.3 %collective-permute-start.30 = (bf16[40,1280]{1,0:T(8,128)(2,1)S(1)}, bf16[40,1280]{1,0:T(8,128)(2,1)S(1)}, u32[]{:S(2)}, u32[]{:S(2)}) collective-permute-start(bf16[40,1280]{1,0:T(8,128)(2,1)S(1)} %get-tuple-element.73), channel_id=1, source_target_pairs={{0,12},{4,0},{8,4},{12,8},{1,13},{5,1},{9,5},{13,9},{2,14},{6,2},{... | collective-permute-start | bytes 307208 | tf_op jit(solution)/shard_map/ppermute | solution.py:25
  144.0 3.2 %collective-permute-start.32 = (bf16[2,2,64,1280]{3,2,1,0:T(8,128)(2,1)}, bf16[2,2,64,1280]{3,2,1,0:T(8,128)(2,1)S(1)}, u32[]{:S(2)}, u32[]{:S(2)}) collective-permute-start(bf16[2,2,64,1280]{3,2,1,0:T(8,128)(2,1)} %get-tuple-element.65), channel_id=1, source_target_pairs={{0,12},{1,13},{2,14},{3,15},{4,0},{5,1},{6,2},{7,3},{8,4},{9,5},{1... | collective-permute-start | bytes 1966088 | tf_op jit(solution)/shard_map/ppermute | solution.py:36
  148.1 1.2 collective-permute-done.29
  149.3 6.9 %attended.1 = bf16[256,1280]{1,0:T(8,128)(2,1)} custom-call(s32[8]{0:T(128)} %pad_add_fusion.1.where, bf16[1280,256]{1,0:T(8,128)(2,1)} %get-tuple-element.60.attn_t_ref, bf16[160,1280]{1,0:T(8,128)(2,1)} %copy-done.1, bf16[160,1280]{1,0:T(8,128)(2,1)} %copy-done.2, bf16[160,1280]{1,0:T(8,128)(2,1)} %copy-done.3, bf16[160,1280]{1,0:T(8,128)(2,1)} %copy-done.4, ...), custom_call_target="tpu_custom_call" | custom-call | flops 115000000 | tf_op jit(solution)/shard_map/attended/pallas_call | solution.py:319
  156.3 2.8 %collective-permute-start.37 = (bf16[10,1280]{1,0:T(8,128)(2,1)S(1)}, bf16[10,1280]{1,0:T(8,128)(2,1)S(1)}, u32[]{:S(2)}, u32[]{:S(2)}) collective-permute-start(bf16[10,1280]{1,0:T(8,128)(2,1)S(1)} %get-tuple-element.75), channel_id=1, source_target_pairs={{0,2},{1,3},{2,0},{3,1},{4,6},{5,7},{6,4},{7,5},{8,10},{9,11},{10,... | collective-permute-start | bytes 76808 | tf_op jit(solution)/shard_map/ppermute | solution.py:25
  159.7 2.9 %collective-permute-done.32.refs_1_ = bf16[2,2,64,1280]{3,2,1,0:T(8,128)(2,1)S(1)} collective-permute-done((bf16[2,2,64,1280]{3,2,1,0:T(8,128)(2,1)}, bf16[2,2,64,1280]{3,2,1,0:T(8,128)(2,1)S(1)}, u32[]{:S(2)}, u32[]{:S(2)}) %collective-permute-start.32) | collective-permute-done | bytes 655392 | tf_op jit(solution)/shard_map/ppermute | solution.py:36
  163.3 3.2 %collective-permute-done.34.refs_3_ = bf16[2,2,64,1280]{3,2,1,0:T(8,128)(2,1)S(1)} collective-permute-done((bf16[2,2,64,1280]{3,2,1,0:T(8,128)(2,1)}, bf16[2,2,64,1280]{3,2,1,0:T(8,128)(2,1)S(1)}, u32[]{:S(2)}, u32[]{:S(2)}) %collective-permute-start.34) | collective-permute-done | bytes 655392 | tf_op jit(solution)/shard_map/ppermute | solution.py:36
  166.5 2.4 %total_rows.1 = f32[2,2,64,1280]{3,2,1,0:T(8,128)} custom-call(bf16[2,2,64,1280]{3,2,1,0:T(8,128)(2,1)S(1)} %copy-done.11, bf16[2,2,64,1280]{3,2,1,0:T(8,128)(2,1)S(1)} %collective-permute-done.32.refs_1_, bf16[2,2,64,1280]{3,2,1,0:T(8,128)(2,1)S(1)} %collective-permute-done.33.refs_2_, bf16[2,2,64,1280]{3,2,1,0:T(8,128)(2,1)S(1)} %collective-permute-done.34.refs_3_), custom_call_target="tpu_custom_call" | custom-call | flops 4600000000 | tf_op jit(solution)/shard_map/total_rows/pallas_call | solution.py:137
  (113 shorter events, 13.4 us)
Async XLA Ops:
  2.4 10.1 %collective-permute-start.2 = (bf16[16,1280]{1,0:T(8,128)(2,1)S(1)}, bf16[16,1280]{1,0:T(8,128)(2,1)S(1)}, u32[]{:S(2)}, u32[]{:S(2)}) collective-permute-start(bf16[16,1280]{1,0:T(8,128)(2,1)S(1)} %maximum_maximum_fusion), channel_id=1, source_target_pairs={{0,3},{1,0},{2,1},{3,2},{4,7},{5,4},{6,5},{7,6},{8,11},{9,8},{10,9... | collective-permute-start | bytes 122888 | tf_op jit(solution)/shard_map/ppermute | solution.py:36
  5.4 8.6 %collective-permute-start.1 = (bf16[16,1280]{1,0:T(8,128)(2,1)S(1)}, bf16[16,1280]{1,0:T(8,128)(2,1)S(1)}, u32[]{:S(2)}, u32[]{:S(2)}) collective-permute-start(bf16[16,1280]{1,0:T(8,128)(2,1)S(1)} %maximum_maximum_fusion), channel_id=1, source_target_pairs={{0,2},{1,3},{2,0},{3,1},{4,6},{5,7},{6,4},{7,5},{8,10},{9,11},{10,... | collective-permute-start | bytes 122888 | tf_op jit(solution)/shard_map/ppermute | solution.py:36
  6.0 7.9 %collective-permute-start = (bf16[16,1280]{1,0:T(8,128)(2,1)S(1)}, bf16[16,1280]{1,0:T(8,128)(2,1)S(1)}, u32[]{:S(2)}, u32[]{:S(2)}) collective-permute-start(bf16[16,1280]{1,0:T(8,128)(2,1)S(1)} %maximum_maximum_fusion), channel_id=1, source_target_pairs={{0,1},{1,2},{2,3},{3,0},{4,5},{5,6},{6,7},{7,4},{8,9},{9,10},{10,1... | collective-permute-start | bytes 122888 | tf_op jit(solution)/shard_map/ppermute | solution.py:36
  7.0 12.0 %collective-permute-start.3 = (bf16[2,2,64,1280]{3,2,1,0:T(8,128)(2,1)}, bf16[2,2,64,1280]{3,2,1,0:T(8,128)(2,1)S(1)}, u32[]{:S(2)}, u32[]{:S(2)}) collective-permute-start(bf16[2,2,64,1280]{3,2,1,0:T(8,128)(2,1)} %refs_0_.1), channel_id=1, source_target_pairs={{0,4},{1,5},{2,6},{3,7},{4,8},{5,9},{6,10},{7,11},{8,12},{9,13},{1... | collective-permute-start | bytes 1966088 | tf_op jit(solution)/shard_map/ppermute | solution.py:36
  8.5 18.6 %collective-permute-start.4 = (bf16[2,2,64,1280]{3,2,1,0:T(8,128)(2,1)}, bf16[2,2,64,1280]{3,2,1,0:T(8,128)(2,1)S(1)}, u32[]{:S(2)}, u32[]{:S(2)}) collective-permute-start(bf16[2,2,64,1280]{3,2,1,0:T(8,128)(2,1)} %refs_0_.1), channel_id=1, source_target_pairs={{0,8},{1,9},{2,10},{3,11},{4,12},{5,13},{6,14},{7,15},{8,0},{9,1},... | collective-permute-start | bytes 1966088 | tf_op jit(solution)/shard_map/ppermute | solution.py:36
  12.5 14.6 %collective-permute-start.5 = (bf16[2,2,64,1280]{3,2,1,0:T(8,128)(2,1)}, bf16[2,2,64,1280]{3,2,1,0:T(8,128)(2,1)S(1)}, u32[]{:S(2)}, u32[]{:S(2)}) collective-permute-start(bf16[2,2,64,1280]{3,2,1,0:T(8,128)(2,1)} %refs_0_.1), channel_id=1, source_target_pairs={{0,12},{1,13},{2,14},{3,15},{4,0},{5,1},{6,2},{7,3},{8,4},{9,5},{1... | collective-permute-start | bytes 1966088 | tf_op jit(solution)/shard_map/ppermute | solution.py:36
  15.0 16.4 %copy-start.8 = (s32[16]{0:T(128)}, s32[16]{0:T(128)S(1)}, u32[]{:S(2)}) copy-start(s32[16]{0:T(128)S(1)} %reshape.349.table) | copy-start | bytes 196
  19.0 16.1 %collective-permute-start.11 = (bf16[4,16,1280]{2,1,0:T(8,128)(2,1)S(1)}, bf16[4,16,1280]{2,1,0:T(8,128)(2,1)S(1)}, u32[]{:S(2)}, u32[]{:S(2)}) collective-permute-start(bf16[4,16,1280]{2,1,0:T(8,128)(2,1)S(1)} %pad_maximum_fusion.1), channel_id=1, source_target_pairs={{0,12},{1,13},{2,14},{3,15},{4,0},{5,1},{6,2},{7,3},{8,4},{9,5},{1... | collective-permute-start | bytes 491528 | tf_op jit(solution)/shard_map/ppermute | solution.py:36
  20.6 14.6 %collective-permute-start.10 = (bf16[4,16,1280]{2,1,0:T(8,128)(2,1)S(1)}, bf16[4,16,1280]{2,1,0:T(8,128)(2,1)S(1)}, u32[]{:S(2)}, u32[]{:S(2)}) collective-permute-start(bf16[4,16,1280]{2,1,0:T(8,128)(2,1)S(1)} %pad_maximum_fusion.1), channel_id=1, source_target_pairs={{0,8},{1,9},{2,10},{3,11},{4,12},{5,13},{6,14},{7,15},{8,0},{9,1},... | collective-permute-start | bytes 491528 | tf_op jit(solution)/shard_map/ppermute | solution.py:36
  21.4 13.8 %collective-permute-start.9 = (bf16[4,16,1280]{2,1,0:T(8,128)(2,1)S(1)}, bf16[4,16,1280]{2,1,0:T(8,128)(2,1)S(1)}, u32[]{:S(2)}, u32[]{:S(2)}) collective-permute-start(bf16[4,16,1280]{2,1,0:T(8,128)(2,1)S(1)} %pad_maximum_fusion.1), channel_id=1, source_target_pairs={{0,4},{1,5},{2,6},{3,7},{4,8},{5,9},{6,10},{7,11},{8,12},{9,13},{1... | collective-permute-start | bytes 491528 | tf_op jit(solution)/shard_map/ppermute | solution.py:36
  31.4 8.2 %copy-start.10 = (bf16[4,2,64,1280]{3,2,1,0:T(8,128)(2,1)}, bf16[4,2,64,1280]{3,2,1,0:T(8,128)(2,1)S(1)}, u32[]{:S(2)}) copy-start(bf16[4,2,64,1280]{3,2,1,0:T(8,128)(2,1)S(1)} %get-tuple-element.42.refs_0_) | copy-start | bytes 3932164
  31.4 35.9 %copy-start = (bf16[1,256,1280]{2,1,0:T(8,128)(2,1)S(1)}, bf16[1,256,1280]{2,1,0:T(8,128)(2,1)}, u32[]{:S(2)}) copy-start(bf16[1,256,1280]{2,1,0:T(8,128)(2,1)} %param.15) | copy-start | bytes 1966084
  31.4 30.8 %collective-permute-start.6 = (bf16[4,2,64,1280]{3,2,1,0:T(8,128)(2,1)S(1)}, bf16[4,2,64,1280]{3,2,1,0:T(8,128)(2,1)S(1)}, u32[]{:S(2)}, u32[]{:S(2)}) collective-permute-start(bf16[4,2,64,1280]{3,2,1,0:T(8,128)(2,1)S(1)} %get-tuple-element.37), channel_id=1, source_target_pairs={{0,1},{1,2},{2,3},{3,0},{4,5},{5,6},{6,7},{7,4},{8,9},{9,10},{10,1... | collective-permute-start | bytes 3932168 | tf_op jit(solution)/shard_map/ppermute | solution.py:36
  33.3 31.5 %collective-permute-start.7 = (bf16[4,2,64,1280]{3,2,1,0:T(8,128)(2,1)S(1)}, bf16[4,2,64,1280]{3,2,1,0:T(8,128)(2,1)S(1)}, u32[]{:S(2)}, u32[]{:S(2)}) collective-permute-start(bf16[4,2,64,1280]{3,2,1,0:T(8,128)(2,1)S(1)} %get-tuple-element.38), channel_id=1, source_target_pairs={{0,2},{1,3},{2,0},{3,1},{4,6},{5,7},{6,4},{7,5},{8,10},{9,11},{10,... | collective-permute-start | bytes 3932168 | tf_op jit(solution)/shard_map/ppermute | solution.py:36
  35.5 35.0 %copy-start.1 = (bf16[160,1280]{1,0:T(8,128)(2,1)}, bf16[160,1280]{1,0:T(8,128)(2,1)S(1)}, u32[]{:S(2)}) copy-start(bf16[160,1280]{1,0:T(8,128)(2,1)S(1)} %convolution_convert_fusion.refs_0_) | copy-start | bytes 1228804
  35.5 18.2 %collective-permute-start.12 = (bf16[160,1280]{1,0:T(8,128)(2,1)S(1)}, bf16[160,1280]{1,0:T(8,128)(2,1)S(1)}, u32[]{:S(2)}, u32[]{:S(2)}) collective-permute-start(bf16[160,1280]{1,0:T(8,128)(2,1)S(1)} %convolution_convert_fusion.refs_0_), channel_id=1, source_target_pairs={{0,32},{32,64},{64,96},{96,0},{1,33},{33,65},{65,97},{97,1},{2,34}... | collective-permute-start | bytes 1228808 | tf_op jit(solution)/shard_map/ppermute | solution.py:25
  37.5 29.7 %collective-permute-start.8 = (bf16[4,2,64,1280]{3,2,1,0:T(8,128)(2,1)}, bf16[4,2,64,1280]{3,2,1,0:T(8,128)(2,1)}, u32[]{:S(2)}, u32[]{:S(2)}) collective-permute-start(bf16[4,2,64,1280]{3,2,1,0:T(8,128)(2,1)} %get-tuple-element.39), channel_id=1, source_target_pairs={{0,3},{1,0},{2,1},{3,2},{4,7},{5,4},{6,5},{7,6},{8,11},{9,8},{10,9... | collective-permute-start | bytes 3932168 | tf_op jit(solution)/shard_map/ppermute | solution.py:36
  38.4 15.5 %collective-permute-start.13 = (bf16[160,1280]{1,0:T(8,128)(2,1)S(1)}, bf16[160,1280]{1,0:T(8,128)(2,1)S(1)}, u32[]{:S(2)}, u32[]{:S(2)}) collective-permute-start(bf16[160,1280]{1,0:T(8,128)(2,1)S(1)} %convolution_convert_fusion.refs_0_), channel_id=1, source_target_pairs={{0,64},{32,96},{64,0},{96,32},{1,65},{33,97},{65,1},{97,33},{2,66}... | collective-permute-start | bytes 1228808 | tf_op jit(solution)/shard_map/ppermute | solution.py:25
  53.8 16.7 %copy-start.2 = (bf16[160,1280]{1,0:T(8,128)(2,1)}, bf16[160,1280]{1,0:T(8,128)(2,1)S(1)}, u32[]{:S(2)}) copy-start(bf16[160,1280]{1,0:T(8,128)(2,1)S(1)} %collective-permute-done.12.refs_1_) | copy-start | bytes 1228804
  53.8 8.4 %collective-permute-start.14 = (bf16[160,1280]{1,0:T(8,128)(2,1)S(1)}, bf16[160,1280]{1,0:T(8,128)(2,1)S(1)}, u32[]{:S(2)}, u32[]{:S(2)}) collective-permute-start(bf16[160,1280]{1,0:T(8,128)(2,1)S(1)} %convolution_convert_fusion.refs_0_), channel_id=1, source_target_pairs={{0,96},{32,0},{64,32},{96,64},{1,97},{33,1},{65,33},{97,65},{2,98}... | collective-permute-start | bytes 1228808 | tf_op jit(solution)/shard_map/ppermute | solution.py:25
  53.9 16.5 %copy-start.3 = (bf16[160,1280]{1,0:T(8,128)(2,1)}, bf16[160,1280]{1,0:T(8,128)(2,1)S(1)}, u32[]{:S(2)}) copy-start(bf16[160,1280]{1,0:T(8,128)(2,1)S(1)} %collective-permute-done.13.refs_2_) | copy-start | bytes 1228804
  53.9 13.3 %collective-permute-start.15 = (bf16[160,1280]{1,0:T(8,128)(2,1)S(1)}, bf16[160,1280]{1,0:T(8,128)(2,1)S(1)}, u32[]{:S(2)}, u32[]{:S(2)}) collective-permute-start(bf16[160,1280]{1,0:T(8,128)(2,1)S(1)} %convolution_convert_fusion.refs_0_), channel_id=1, source_target_pairs={{0,16},{16,0},{1,17},{17,1},{2,18},{18,2},{3,19},{19,3},{4,20},{20... | collective-permute-start | bytes 1228808 | tf_op jit(solution)/shard_map/ppermute | solution.py:25
  62.1 8.4 %copy-start.4 = (bf16[160,1280]{1,0:T(8,128)(2,1)}, bf16[160,1280]{1,0:T(8,128)(2,1)S(1)}, u32[]{:S(2)}) copy-start(bf16[160,1280]{1,0:T(8,128)(2,1)S(1)} %collective-permute-done.14.refs_3_) | copy-start | bytes 1228804
  62.1 5.1 %collective-permute-start.16 = (bf16[160,1280]{1,0:T(8,128)(2,1)S(1)}, bf16[160,1280]{1,0:T(8,128)(2,1)S(1)}, u32[]{:S(2)}, u32[]{:S(2)}) collective-permute-start(bf16[160,1280]{1,0:T(8,128)(2,1)S(1)} %collective-permute-done.12.refs_1_), channel_id=1, source_target_pairs={{0,16},{16,0},{1,17},{17,1},{2,18},{18,2},{3,19},{19,3},{4,20},{20... | collective-permute-start | bytes 1228808 | tf_op jit(solution)/shard_map/ppermute | solution.py:25
  62.2 5.1 %collective-permute-start.17 = (bf16[160,1280]{1,0:T(8,128)(2,1)S(1)}, bf16[160,1280]{1,0:T(8,128)(2,1)S(1)}, u32[]{:S(2)}, u32[]{:S(2)}) collective-permute-start(bf16[160,1280]{1,0:T(8,128)(2,1)S(1)} %collective-permute-done.13.refs_2_), channel_id=1, source_target_pairs={{0,16},{16,0},{1,17},{17,1},{2,18},{18,2},{3,19},{19,3},{4,20},{20... | collective-permute-start | bytes 1228808 | tf_op jit(solution)/shard_map/ppermute | solution.py:25
  64.8 2.5 %collective-permute-start.18 = (bf16[160,1280]{1,0:T(8,128)(2,1)S(1)}, bf16[160,1280]{1,0:T(8,128)(2,1)}, u32[]{:S(2)}, u32[]{:S(2)}) collective-permute-start(bf16[160,1280]{1,0:T(8,128)(2,1)S(1)} %collective-permute-done.14.refs_3_), channel_id=1, source_target_pairs={{0,16},{16,0},{1,17},{17,1},{2,18},{18,2},{3,19},{19,3},{4,20},{20... | collective-permute-start | bytes 1228808 | tf_op jit(solution)/shard_map/ppermute | solution.py:25
  82.3 18.1 %collective-permute-start.19 = (bf16[4,2,64,512]{3,2,1,0:T(8,128)(2,1)}, bf16[4,2,64,512]{3,2,1,0:T(8,128)(2,1)S(1)}, u32[]{:S(2)}, u32[]{:S(2)}) collective-permute-start(bf16[4,2,64,512]{3,2,1,0:T(8,128)(2,1)} %get-tuple-element.49), channel_id=1, source_target_pairs={{0,3},{1,0},{2,1},{3,2},{4,7},{5,4},{6,5},{7,6},{8,11},{9,8},{10,9... | collective-permute-start | bytes 1572872 | tf_op jit(solution)/shard_map/ppermute | solution.py:36
  83.2 17.3 %collective-permute-start.20 = (bf16[4,2,64,512]{3,2,1,0:T(8,128)(2,1)}, bf16[4,2,64,512]{3,2,1,0:T(8,128)(2,1)S(1)}, u32[]{:S(2)}, u32[]{:S(2)}) collective-permute-start(bf16[4,2,64,512]{3,2,1,0:T(8,128)(2,1)} %get-tuple-element.50), channel_id=1, source_target_pairs={{0,2},{1,3},{2,0},{3,1},{4,6},{5,7},{6,4},{7,5},{8,10},{9,11},{10,... | collective-permute-start | bytes 1572872 | tf_op jit(solution)/shard_map/ppermute | solution.py:36
  84.3 16.2 %collective-permute-start.21 = (bf16[4,2,64,512]{3,2,1,0:T(8,128)(2,1)}, bf16[4,2,64,512]{3,2,1,0:T(8,128)(2,1)S(1)}, u32[]{:S(2)}, u32[]{:S(2)}) collective-permute-start(bf16[4,2,64,512]{3,2,1,0:T(8,128)(2,1)} %get-tuple-element.51), channel_id=1, source_target_pairs={{0,1},{1,2},{2,3},{3,0},{4,5},{5,6},{6,7},{7,4},{8,9},{9,10},{10,1... | collective-permute-start | bytes 1572872 | tf_op jit(solution)/shard_map/ppermute | solution.py:36
  100.4 5.0 %copy-start.17 = (bf16[4,2,64,512]{3,2,1,0:T(8,128)(2,1)}, bf16[4,2,64,512]{3,2,1,0:T(8,128)(2,1)S(1)}, u32[]{:S(2)}) copy-start(bf16[4,2,64,512]{3,2,1,0:T(8,128)(2,1)S(1)} %collective-permute-done.20.refs_2_) | copy-start | bytes 1572868
  100.5 5.0 %copy-start.18 = (bf16[4,2,64,512]{3,2,1,0:T(8,128)(2,1)}, bf16[4,2,64,512]{3,2,1,0:T(8,128)(2,1)S(1)}, u32[]{:S(2)}) copy-start(bf16[4,2,64,512]{3,2,1,0:T(8,128)(2,1)S(1)} %collective-permute-done.21.refs_3_) | copy-start | bytes 1572868
  105.4 9.2 %collective-permute-start.22 = (bf16[4,160,1280]{2,1,0:T(8,128)(2,1)}, bf16[4,160,1280]{2,1,0:T(8,128)(2,1)S(1)}, u32[]{:S(2)}, u32[]{:S(2)}) collective-permute-start(bf16[4,160,1280]{2,1,0:T(8,128)(2,1)} %grad_weight.3), channel_id=1, source_target_pairs={{0,16},{16,0},{1,17},{17,1},{2,18},{18,2},{3,19},{19,3},{4,20},{20... | collective-permute-start | bytes 4915208 | tf_op jit(solution)/shard_map/ppermute | solution.py:25
  105.6 20.0 %collective-permute-start.23 = (bf16[4,2,64,768]{3,2,1,0:T(8,128)(2,1)S(1)}, bf16[4,2,64,768]{3,2,1,0:T(8,128)(2,1)}, u32[]{:S(2)}, u32[]{:S(2)}) collective-permute-start(bf16[4,2,64,768]{3,2,1,0:T(8,128)(2,1)S(1)} %copy-done.15), channel_id=1, source_target_pairs={{0,3},{1,0},{2,1},{3,2},{4,7},{5,4},{6,5},{7,6},{8,11},{9,8},{10,9... | collective-permute-start | bytes 2359304 | tf_op jit(solution)/shard_map/ppermute | solution.py:36
  107.6 19.9 %collective-permute-start.24 = (bf16[4,2,64,768]{3,2,1,0:T(8,128)(2,1)}, bf16[4,2,64,768]{3,2,1,0:T(8,128)(2,1)}, u32[]{:S(2)}, u32[]{:S(2)}) collective-permute-start(bf16[4,2,64,768]{3,2,1,0:T(8,128)(2,1)} %get-tuple-element.56), channel_id=1, source_target_pairs={{0,2},{1,3},{2,0},{3,1},{4,6},{5,7},{6,4},{7,5},{8,10},{9,11},{10,... | collective-permute-start | bytes 2359304 | tf_op jit(solution)/shard_map/ppermute | solution.py:36
  108.8 21.0 %collective-permute-start.25 = (bf16[4,2,64,768]{3,2,1,0:T(8,128)(2,1)}, bf16[4,2,64,768]{3,2,1,0:T(8,128)(2,1)}, u32[]{:S(2)}, u32[]{:S(2)}) collective-permute-start(bf16[4,2,64,768]{3,2,1,0:T(8,128)(2,1)} %get-tuple-element.57), channel_id=1, source_target_pairs={{0,1},{1,2},{2,3},{3,0},{4,5},{5,6},{6,7},{7,4},{8,9},{9,10},{10,1... | collective-permute-start | bytes 2359304 | tf_op jit(solution)/shard_map/ppermute | solution.py:36
  117.0 19.5 %collective-permute-start.28 = (bf16[160,1280]{1,0:T(8,128)(2,1)S(1)}, bf16[160,1280]{1,0:T(8,128)(2,1)S(1)}, u32[]{:S(2)}, u32[]{:S(2)}) collective-permute-start(bf16[160,1280]{1,0:T(8,128)(2,1)S(1)} %get-tuple-element.69), channel_id=1, source_target_pairs={{0,64},{32,96},{64,0},{96,32},{1,65},{33,97},{65,1},{97,33},{2,66}... | collective-permute-start | bytes 1228808 | tf_op jit(solution)/shard_map/ppermute | solution.py:25
  120.0 18.2 %collective-permute-start.27 = (bf16[160,1280]{1,0:T(8,128)(2,1)S(1)}, bf16[160,1280]{1,0:T(8,128)(2,1)S(1)}, u32[]{:S(2)}, u32[]{:S(2)}) collective-permute-start(bf16[160,1280]{1,0:T(8,128)(2,1)S(1)} %get-tuple-element.70), channel_id=1, source_target_pairs={{0,96},{32,0},{64,32},{96,64},{1,97},{33,1},{65,33},{97,65},{2,98}... | collective-permute-start | bytes 1228808 | tf_op jit(solution)/shard_map/ppermute | solution.py:25
  125.6 13.1 %collective-permute-start.26 = (bf16[160,1280]{1,0:T(8,128)(2,1)S(1)}, bf16[160,1280]{1,0:T(8,128)(2,1)S(1)}, u32[]{:S(2)}, u32[]{:S(2)}) collective-permute-start(bf16[160,1280]{1,0:T(8,128)(2,1)S(1)} %get-tuple-element.68), channel_id=1, source_target_pairs={{0,32},{32,64},{64,96},{96,0},{1,33},{33,65},{65,97},{97,1},{2,34}... | collective-permute-start | bytes 1228808 | tf_op jit(solution)/shard_map/ppermute | solution.py:25
  138.9 8.6 %collective-permute-start.31 = (bf16[40,1280]{1,0:T(8,128)(2,1)S(1)}, bf16[40,1280]{1,0:T(8,128)(2,1)S(1)}, u32[]{:S(2)}, u32[]{:S(2)}) collective-permute-start(bf16[40,1280]{1,0:T(8,128)(2,1)S(1)} %get-tuple-element.72), channel_id=1, source_target_pairs={{0,8},{4,12},{8,0},{12,4},{1,9},{5,13},{9,1},{13,5},{2,10},{6,14},... | collective-permute-start | bytes 307208 | tf_op jit(solution)/shard_map/ppermute | solution.py:25
  141.0 7.0 %collective-permute-start.30 = (bf16[40,1280]{1,0:T(8,128)(2,1)S(1)}, bf16[40,1280]{1,0:T(8,128)(2,1)S(1)}, u32[]{:S(2)}, u32[]{:S(2)}) collective-permute-start(bf16[40,1280]{1,0:T(8,128)(2,1)S(1)} %get-tuple-element.73), channel_id=1, source_target_pairs={{0,12},{4,0},{8,4},{12,8},{1,13},{5,1},{9,5},{13,9},{2,14},{6,2},{... | collective-permute-start | bytes 307208 | tf_op jit(solution)/shard_map/ppermute | solution.py:25
  143.4 5.9 %collective-permute-start.29 = (bf16[40,1280]{1,0:T(8,128)(2,1)S(1)}, bf16[40,1280]{1,0:T(8,128)(2,1)S(1)}, u32[]{:S(2)}, u32[]{:S(2)}) collective-permute-start(bf16[40,1280]{1,0:T(8,128)(2,1)S(1)} %get-tuple-element.71), channel_id=1, source_target_pairs={{0,4},{4,8},{8,12},{12,0},{1,5},{5,9},{9,13},{13,1},{2,6},{6,10},{... | collective-permute-start | bytes 307208 | tf_op jit(solution)/shard_map/ppermute | solution.py:25
  144.0 18.7 %collective-permute-start.32 = (bf16[2,2,64,1280]{3,2,1,0:T(8,128)(2,1)}, bf16[2,2,64,1280]{3,2,1,0:T(8,128)(2,1)S(1)}, u32[]{:S(2)}, u32[]{:S(2)}) collective-permute-start(bf16[2,2,64,1280]{3,2,1,0:T(8,128)(2,1)} %get-tuple-element.65), channel_id=1, source_target_pairs={{0,12},{1,13},{2,14},{3,15},{4,0},{5,1},{6,2},{7,3},{8,4},{9,5},{1... | collective-permute-start | bytes 1966088 | tf_op jit(solution)/shard_map/ppermute | solution.py:36
  147.2 16.1 %collective-permute-start.33 = (bf16[2,2,64,1280]{3,2,1,0:T(8,128)(2,1)}, bf16[2,2,64,1280]{3,2,1,0:T(8,128)(2,1)S(1)}, u32[]{:S(2)}, u32[]{:S(2)}) collective-permute-start(bf16[2,2,64,1280]{3,2,1,0:T(8,128)(2,1)} %get-tuple-element.66), channel_id=1, source_target_pairs={{0,8},{1,9},{2,10},{3,11},{4,12},{5,13},{6,14},{7,15},{8,0},{9,1},... | collective-permute-start | bytes 1966088 | tf_op jit(solution)/shard_map/ppermute | solution.py:36
  147.5 19.0 %collective-permute-start.34 = (bf16[2,2,64,1280]{3,2,1,0:T(8,128)(2,1)}, bf16[2,2,64,1280]{3,2,1,0:T(8,128)(2,1)S(1)}, u32[]{:S(2)}, u32[]{:S(2)}) collective-permute-start(bf16[2,2,64,1280]{3,2,1,0:T(8,128)(2,1)} %get-tuple-element.67), channel_id=1, source_target_pairs={{0,4},{1,5},{2,6},{3,7},{4,8},{5,9},{6,10},{7,11},{8,12},{9,13},{1... | collective-permute-start | bytes 1966088 | tf_op jit(solution)/shard_map/ppermute | solution.py:36
  149.3 17.2 %copy-start.11 = (bf16[2,2,64,1280]{3,2,1,0:T(8,128)(2,1)S(1)}, bf16[2,2,64,1280]{3,2,1,0:T(8,128)(2,1)}, u32[]{:S(2)}) copy-start(bf16[2,2,64,1280]{3,2,1,0:T(8,128)(2,1)} %get-tuple-element.64.refs_0_) | copy-start | bytes 1966084
  156.3 12.6 %collective-permute-start.37 = (bf16[10,1280]{1,0:T(8,128)(2,1)S(1)}, bf16[10,1280]{1,0:T(8,128)(2,1)S(1)}, u32[]{:S(2)}, u32[]{:S(2)}) collective-permute-start(bf16[10,1280]{1,0:T(8,128)(2,1)S(1)} %get-tuple-element.75), channel_id=1, source_target_pairs={{0,2},{1,3},{2,0},{3,1},{4,6},{5,7},{6,4},{7,5},{8,10},{9,11},{10,... | collective-permute-start | bytes 76808 | tf_op jit(solution)/shard_map/ppermute | solution.py:25
  159.1 9.9 %collective-permute-start.36 = (bf16[10,1280]{1,0:T(8,128)(2,1)S(1)}, bf16[10,1280]{1,0:T(8,128)(2,1)S(1)}, u32[]{:S(2)}, u32[]{:S(2)}) collective-permute-start(bf16[10,1280]{1,0:T(8,128)(2,1)S(1)} %get-tuple-element.76), channel_id=1, source_target_pairs={{0,3},{1,0},{2,1},{3,2},{4,7},{5,4},{6,5},{7,6},{8,11},{9,8},{10,9... | collective-permute-start | bytes 76808 | tf_op jit(solution)/shard_map/ppermute | solution.py:25
  162.6 6.3 %collective-permute-start.35 = (bf16[10,1280]{1,0:T(8,128)(2,1)S(1)}, bf16[10,1280]{1,0:T(8,128)(2,1)S(1)}, u32[]{:S(2)}, u32[]{:S(2)}) collective-permute-start(bf16[10,1280]{1,0:T(8,128)(2,1)S(1)} %get-tuple-element.74), channel_id=1, source_target_pairs={{0,1},{1,2},{2,3},{3,0},{4,5},{5,6},{6,7},{7,4},{8,9},{9,10},{10,1... | collective-permute-start | bytes 76808 | tf_op jit(solution)/shard_map/ppermute | solution.py:25
  (9 other events, 20.7 us)
